TPU v7x, 128 devices: a whole 4x4x4 slice. The times are simulated.
128 devices in a mesh: section: 2 (over core), expert: 2 (over x_lo), dp: 32 (over z, y, x_hi).
Axes of the slice: x: 4 (x_hi: 2, x_lo: 2; x = x_hi * 2 + x_lo), y: 4, z: 4, core: 2. Of those that a mesh axis runs over, the one named last changes fastest.
Arguments:
- inputs: bfloat16 [2, 256, 2048], P(None, ('section', 'expert')), may hold values from -6 to 6
- cotangent: bfloat16 [2, 256, 2048], P(None, ('section', 'expert')), may hold values from -6 to 6
- w_gate: bfloat16 [8, 7168, 2048], P('expert', 'dp', 'section'), may hold values from -0.125 to 0.125
- w_up: bfloat16 [8, 7168, 2048], P('expert', 'dp', 'section'), may hold values from -0.125 to 0.125
- w_down: bfloat16 [8, 7168, 2048], P('expert', 'dp', 'section'), may hold values from -0.0625 to 0.0625
- router: float32 [2048, 8], replicated, may hold values from -0.25 to 0.25
- norm_gain: float32 [2048], replicated, may hold values from 0.5 to 1.5
- routes: int32 [2, 256, 2], P(None, ('section', 'expert')), may hold values from 0 to 7, all different within a row; in each aligned block of 64 rows (0 to 63, 64 to 127, ..., all dimensions but the last counted through in order) at most 32 rows name the same one
Outputs:
- layer_out: bfloat16 [2, 256, 2048], P(None, ('section', 'expert'))
- grad_inputs: bfloat16 [2, 256, 2048], P(None, ('section', 'expert'))
- grad_router: float32 [2048, 8], replicated
- grad_gain: float32 [2048], replicated
Inputs may be any that keep to these rules, and one draw needn't show every extreme that they name: `routes`: the two experts of a token differ. In every micro-batch and every aligned block of 64 tokens (the tokens of one index of section and expert), no expert is named by more than 32 tokens, a bound that some block reaches.
All inputs are finite; a program needn't handle non-finite values.
Results may differ from a plain program's by a relative error of at most 0.0073.
Values may be sent and summed in bfloat16 or wider, within the bound.
No kernel may reach another device: no remote copies, remote signals or barrier semaphores. Data moves between devices by JAX's collectives and lax.ppermute only.
A program may use at most 128 MiB of HBM per device.

v0:
```python
import jax
import jax.numpy as jnp
from jax import lax
from jax.sharding import PartitionSpec as P

EPSILON = 1e-05


def normalize(wide_in, gain_row, router_map):
    scaling = lax.rsqrt(jnp.mean(wide_in * wide_in, axis=-1, keepdims=True) + EPSILON)
    normed = wide_in * scaling * gain_row
    logits = jnp.dot(
        normed, router_map, precision=lax.Precision.HIGHEST, preferred_element_type=jnp.float32
    )
    return (normed, logits)


def gate_pair(logits, expert_ids):
    chosen = jnp.take_along_axis(logits, expert_ids, axis=1)
    leading = jax.nn.sigmoid(chosen[:, 0] - chosen[:, 1])
    return (leading, 1.0 - leading)


def expert_pass(grouped, gate_map, up_map, down_map):
    pre_gate = jnp.einsum("selc,efc->self", grouped, gate_map, preferred_element_type=jnp.float32)
    pre_up = jnp.einsum("selc,efc->self", grouped, up_map, preferred_element_type=jnp.float32)
    squash = jax.nn.sigmoid(pre_gate)
    hidden = (pre_gate * squash * pre_up).astype(jnp.bfloat16)
    block_out = jnp.einsum("self,efc->selc", hidden, down_map, preferred_element_type=jnp.float32)
    return (pre_gate, pre_up, squash, block_out.astype(jnp.bfloat16))


def slot_table(expert_ids, experts, capacity):
    flat_ids = expert_ids.reshape(-1)
    one_hot = (flat_ids[:, None] == jnp.arange(experts, dtype=jnp.int32)[None, :]).astype(jnp.int32)
    before = jnp.cumsum(one_hot, axis=0) - one_hot
    rank_in = jnp.sum(before * one_hot, axis=1)
    target = flat_ids * capacity + rank_in
    slot_map = (jnp.arange(experts * capacity, dtype=jnp.int32)[:, None] == target[None, :]).astype(
        jnp.bfloat16
    )
    return slot_map.reshape(experts * capacity, expert_ids.shape[0], 2)


def pick_rows(selector, flat_rows):
    return lax.dot_general(
        selector, flat_rows, (((0,), (0,)), ((), ())), preferred_element_type=jnp.float32
    )


def logit_grads(leading, trailing, gate_sums, expert_ids, experts):
    delta_gate = leading * trailing * (gate_sums[:, 0] - gate_sums[:, 1])
    columns = jnp.arange(experts, dtype=jnp.int32)[None, :]
    return delta_gate[:, None] * (
        (expert_ids[:, 0:1] == columns).astype(jnp.float32)
        - (expert_ids[:, 1:2] == columns).astype(jnp.float32)
    )


def shards(inputs, cotangent, w_gate, w_up, w_down, router, norm_gain, routes):
    local_count = w_gate.shape[0]
    sources = lax.axis_size("expert")
    experts = local_count * sources
    gate_map, up_map, down_map = (
        lax.all_gather(w_gate, "section", axis=2, tiled=True),
        lax.all_gather(w_up, "section", axis=2, tiled=True),
        lax.all_gather(w_down, "section", axis=2, tiled=True),
    )
    micro_count = inputs.shape[0]
    tok_rows = inputs.shape[1]
    model_width = inputs.shape[2]
    capacity = min(tok_rows, 4 * tok_rows // experts)
    slot_count = experts * capacity
    layer_list, grad_list = ([], [])
    gain_total = jnp.zeros(norm_gain.shape, jnp.float32)
    router_total = jnp.zeros(router.shape, jnp.float32)
    for micro_idx in range(micro_count):
        expert_ids = routes[micro_idx]
        wide_in = inputs[micro_idx].astype(jnp.float32)
        wide_up = cotangent[micro_idx].astype(jnp.float32)
        normed, logits = normalize(wide_in, norm_gain, router)
        rows_low = normed.astype(jnp.bfloat16)
        leading, trailing = gate_pair(logits, expert_ids)
        slot_map = slot_table(expert_ids, experts, capacity)
        first_map = slot_map[:, :, 0]
        second_map = slot_map[:, :, 1]
        outgoing = jnp.dot(first_map + second_map, rows_low, preferred_element_type=jnp.float32)
        outgoing = outgoing.astype(jnp.bfloat16).reshape(experts, capacity, model_width)
        received = lax.all_to_all(outgoing, "expert", split_axis=0, concat_axis=0, tiled=True)
        grouped = received.reshape(sources, local_count, capacity, model_width)
        pre_gate, pre_up, squash, block_out = expert_pass(grouped, gate_map, up_map, down_map)
        returned = lax.all_to_all(
            block_out.reshape(experts, capacity, model_width),
            "expert",
            split_axis=0,
            concat_axis=0,
            tiled=True,
        )
        flat_out = returned.reshape(slot_count, model_width)
        first_part = pick_rows(first_map, flat_out)
        second_part = pick_rows(second_map, flat_out)
        mixed_part = leading[:, None] * first_part + trailing[:, None] * second_part
        back_first = (leading[:, None] * wide_up).astype(jnp.bfloat16)
        back_second = (trailing[:, None] * wide_up).astype(jnp.bfloat16)
        grad_outgoing = jnp.dot(
            first_map, back_first, preferred_element_type=jnp.float32
        ) + jnp.dot(second_map, back_second, preferred_element_type=jnp.float32)
        grad_outgoing = grad_outgoing.astype(jnp.bfloat16).reshape(experts, capacity, model_width)
        grad_received = lax.all_to_all(
            grad_outgoing, "expert", split_axis=0, concat_axis=0, tiled=True
        )
        grouped_back = grad_received.reshape(sources, local_count, capacity, model_width)
        hidden_grad = jnp.einsum(
            "selc,efc->self", grouped_back, down_map, preferred_element_type=jnp.float32
        )
        gate_grad = (hidden_grad * pre_up * (squash + pre_gate * squash * (1.0 - squash))).astype(
            jnp.bfloat16
        )
        up_grad = (hidden_grad * pre_gate * squash).astype(jnp.bfloat16)
        row_grad = jnp.einsum(
            "self,efc->selc", gate_grad, gate_map, preferred_element_type=jnp.float32
        ) + jnp.einsum("self,efc->selc", up_grad, up_map, preferred_element_type=jnp.float32)
        row_grad = row_grad.astype(jnp.bfloat16).reshape(experts, capacity, model_width)
        returned_grad = lax.all_to_all(row_grad, "expert", split_axis=0, concat_axis=0, tiled=True)
        flat_grad = returned_grad.reshape(slot_count, model_width)
        dnormed_part = pick_rows(first_map, flat_grad) + pick_rows(second_map, flat_grad)
        gate_part = jnp.stack(
            [jnp.sum(wide_up * first_part, axis=1), jnp.sum(wide_up * second_part, axis=1)], axis=1
        )
        mixed = lax.psum(mixed_part, "dp")
        layer_list.append((wide_in + mixed).astype(jnp.bfloat16))
        dnormed, gate_sums = lax.psum((dnormed_part, gate_part), "dp")
        pulled, pullback = jax.vjp(normalize, wide_in, norm_gain, router)
        dlogits = logit_grads(leading, trailing, gate_sums, expert_ids, experts)
        input_grad, gain_grad, router_grad = pullback((dnormed, dlogits))
        grad_list.append((wide_up + input_grad).astype(jnp.bfloat16))
        gain_total = gain_total + gain_grad
        router_total = router_total + router_grad
    total_router, total_gain = lax.psum((router_total, gain_total), ("section", "expert"))
    return (jnp.stack(layer_list), jnp.stack(grad_list), total_router, total_gain)


def solution(mesh):
    placed = (
        P(None, ("section", "expert"), None),
        P(None, ("section", "expert"), None),
        P("expert", "dp", "section"),
        P("expert", "dp", "section"),
        P("expert", "dp", "section"),
        P(),
        P(),
        P(None, ("section", "expert"), None),
    )
    return jax.shard_map(
        shards,
        mesh=mesh,
        in_specs=placed,
        out_specs=(
            P(None, ("section", "expert"), None),
            P(None, ("section", "expert"), None),
            P(),
            P(),
        ),
        check_vma=False,
    )
```

profile of v0, /device:TPU:0, one launch (start us, length us, event | category | flops | bytes accessed | tf_op | source)
XLA Modules:
  0.0 666.6 jit_solution(10033515939759403292)
XLA Ops:
  14.3 3.6 all-to-all-start.2
  24.3 7.3 %all-to-all-done.2 = bf16[8,32,2048]{2,1,0:T(8,128)(2,1)S(1)} async-done(((bf16[8,32,2048]{2,1,0:T(8,128)(2,1)}), bf16[8,32,2048]{2,1,0:T(8,128)(2,1)S(1)}, u32[]{:S(2)}, u32[]{:S(2)}) %all-to-all-start.2) | async-done | bytes 1048608 | tf_op jit(solution)/shard_map/all_to_all | solution.py:89
  31.6 3.6 all-to-all-start
  35.2 3.3 fusion.65
  38.5 7.9 %all-gather.4.cloned.1.call-done = bf16[4,224,2048]{2,1,0:T(8,128)(2,1)} async-done(((bf16[4,224,1024]{2,1,0:T(8,128)(2,1)}), bf16[4,224,2048]{2,1,0:T(8,128)(2,1)}) %all-gather.4.cloned.1.call-update) | async-done | bytes 3670032 | tf_op jit(solution)/shard_map/all_gather | solution.py:65
  46.4 3.3 fusion.59
  49.7 15.4 %all-gather.8.cloned.1.call-done = bf16[4,224,2048]{2,1,0:T(8,128)(2,1)} async-done(((bf16[4,224,1024]{2,1,0:T(8,128)(2,1)}), bf16[4,224,2048]{2,1,0:T(8,128)(2,1)}) %all-gather.8.cloned.1.call-update) | async-done | bytes 3670032 | tf_op jit(solution)/shard_map/all_gather | solution.py:67
  65.1 2.8 fusion.44
  69.0 3.6 all-to-all-start.3
  72.6 3.5 fusion.62
  80.1 6.9 %all-to-all-done.3 = bf16[8,32,2048]{2,1,0:T(8,128)(2,1)S(1)} async-done(((bf16[8,32,2048]{2,1,0:T(8,128)(2,1)}), bf16[8,32,2048]{2,1,0:T(8,128)(2,1)S(1)}, u32[]{:S(2)}, u32[]{:S(2)}) %all-to-all-start.3) | async-done | bytes 1048608 | tf_op jit(solution)/shard_map/all_to_all | solution.py:92
  86.9 3.6 all-to-all-start.1
  92.7 11.3 %all-to-all-done.1 = bf16[8,32,2048]{2,1,0:T(8,128)(2,1)S(1)} async-done(((bf16[8,32,2048]{2,1,0:T(8,128)(2,1)}), bf16[8,32,2048]{2,1,0:T(8,128)(2,1)S(1)}, u32[]{:S(2)}, u32[]{:S(2)}) %all-to-all-start.1) | async-done | bytes 1048608 | tf_op jit(solution)/shard_map/all_to_all | solution.py:92
  104.4 2.5 fusion.119
  106.9 96.8 %all-reduce = (f32[64,2]{0,1:T(2,128)S(1)}, f32[64,2]{0,1:T(2,128)S(1)}) all-reduce(f32[64,2]{0,1:T(2,128)S(1)} %pad_maximum_fusion.3, f32[64,2]{0,1:T(2,128)S(1)} %pad_maximum_fusion.2), channel_id=1, replica_groups=mesh['section'=2,'expert'=2,'dp'=32] {'dp'}, use_global_device_ids=true, to_apply=%region_16.18 | all-reduce | flops 256 | bytes 2048 | tf_op jit(solution)/shard_map/psum | solution.py:132
  208.1 3.9 all-to-all-start.6
  212.5 1.6 fusion.30
  215.0 7.0 %all-to-all-done.6 = bf16[8,32,2048]{2,1,0:T(8,128)(2,1)S(1)} async-done(((bf16[8,32,2048]{2,1,0:T(8,128)(2,1)}), bf16[8,32,2048]{2,1,0:T(8,128)(2,1)S(1)}, u32[]{:S(2)}, u32[]{:S(2)}) %all-to-all-start.6) | async-done | bytes 1048608 | tf_op jit(solution)/shard_map/all_to_all | solution.py:109
  222.0 3.6 all-to-all-start.4
  225.6 3.4 fusion.71
  233.0 1.9 all-to-all-done.4
  234.9 3.6 all-to-all-start.7
  238.5 3.4 fusion.68
  246.0 1.9 all-to-all-done.7
  247.9 3.6 all-to-all-start.5
  253.0 7.9 %all-to-all-done.5 = bf16[8,32,2048]{2,1,0:T(8,128)(2,1)S(1)} async-done(((bf16[8,32,2048]{2,1,0:T(8,128)(2,1)}), bf16[8,32,2048]{2,1,0:T(8,128)(2,1)S(1)}, u32[]{:S(2)}, u32[]{:S(2)}) %all-to-all-start.5) | async-done | bytes 1048608 | tf_op jit(solution)/shard_map/all_to_all | solution.py:124
  264.2 352.9 %all-reduce.7.cloned.1.call-done = (f32[64,2048]{1,0:T(8,128)}, f32[64,2048]{1,0:T(8,128)}, f32[64,2048]{1,0:T(8,128)}, f32[64,2048]{1,0:T(8,128)}) async-done(((f32[64,2048]{1,0:T(8,128)}, f32[64,2048]{1,0:T(8,128)}, f32[64,2048]{1,0:T(8,128)}, f32[64,2048]{1,0:T(8,128)}), (f32[64,2048]{1,0:T(8,128)}, f32[64,2048]{1,0:T(8,128)}, f32[64,2048]{1,0:T(8,128)}, ...) | async-done | bytes 2097168 | tf_op jit(solution)/shard_map/psum | solution.py:130
  617.1 1.7 convolution_add_fusion.4
  618.8 2.1 fusion.108
  620.9 1.7 fusion.140
  624.3 7.8 %psum.63 = f32[2048]{0:T(1024)} all-reduce(f32[2048]{0:T(1024)S(1)} %add.165), channel_id=1, replica_groups=mesh['section'=2,'expert'=2,'dp'=32] {'section','expert'}, use_global_device_ids=true, to_apply=%region_21.23 | all-reduce | flops 2048 | bytes 16384 | tf_op jit(solution)/shard_map/psum | solution.py:139
  632.1 26.5 %all-reduce.5.cloned.1.call-done = f32[2048,8]{0,1:T(8,128)} async-done(((f32[2048,8]{0,1:T(8,128)}), f32[2048,8]{0,1:T(8,128)}) %all-reduce.5.cloned.1.call-update) | async-done | bytes 65552 | tf_op jit(solution)/shard_map/psum | solution.py:139
  (152 shorter events, 42.4 us)
Async XLA Ops:
  7.2 11.0 %copy-start = (f32[2048,8]{0,1:T(8,128)S(1)}, f32[2048,8]{0,1:T(8,128)}, u32[]{:S(2)}) copy-start(f32[2048,8]{0,1:T(8,128)} %param.15) | copy-start | bytes 196612
  7.2 5.5 copy-start.20
  7.2 28.0 %all-gather.6.cloned.1.call-start = ((), (), s32[]{:S(2)}) async-start(), calls=%async_computation.9 | async-start | bytes 5505024 | tf_op jit(solution)/shard_map/all_gather | solution.py:66
  7.9 38.4 %all-gather.4.cloned.1.call-start = ((), (), s32[]{:S(2)}) async-start(), calls=%async_computation.8 | async-start | bytes 5505024 | tf_op jit(solution)/shard_map/all_gather | solution.py:65
  8.7 56.4 %all-gather.8.cloned.1.call-start = ((), (), s32[]{:S(2)}) async-start(), calls=%async_computation.10 | async-start | bytes 5505024 | tf_op jit(solution)/shard_map/all_gather | solution.py:67
  12.1 7.8 %copy-start.25 = (f32[64]{0:T(128)}, f32[64]{0:T(128)S(1)}, u32[]{:S(2)}) copy-start(f32[64]{0:T(128)S(1)} %get-tuple-element.15) | copy-start | bytes 772
  12.6 7.6 %copy-start.29 = (f32[64]{0:T(128)}, f32[64]{0:T(128)S(1)}, u32[]{:S(2)}) copy-start(f32[64]{0:T(128)S(1)} %fusion.214) | copy-start | bytes 772
  14.3 17.3 %all-to-all-start.2 = ((bf16[8,32,2048]{2,1,0:T(8,128)(2,1)}), bf16[8,32,2048]{2,1,0:T(8,128)(2,1)S(1)}, u32[]{:S(2)}, u32[]{:S(2)}) async-start(bf16[8,32,2048]{2,1,0:T(8,128)(2,1)} %bitcast.30), calls=%async_computation.2 | async-start | bytes 2097152 | tf_op jit(solution)/shard_map/all_to_all | solution.py:89
  31.6 37.5 %all-to-all-start = ((bf16[8,32,2048]{2,1,0:T(8,128)(2,1)}), bf16[8,32,2048]{2,1,0:T(8,128)(2,1)S(1)}, u32[]{:S(2)}, u32[]{:S(2)}) async-start(bf16[8,32,2048]{2,1,0:T(8,128)(2,1)} %bitcast.7), calls=%async_computation | async-start | bytes 2097152 | tf_op jit(solution)/shard_map/all_to_all | solution.py:89
  38.5 26.6 %copy-start.17 = (f32[2,4,32,224]{3,2,0,1:T(8,128)}, f32[2,4,32,224]{3,2,0,1:T(8,128)S(1)}, u32[]{:S(2)}) copy-start(f32[2,4,32,224]{3,2,0,1:T(8,128)S(1)} %fusion.65) | copy-start | bytes 688132
  49.7 19.3 %copy-start.9 = (f32[2,4,32,224]{3,2,0,1:T(8,128)}, f32[2,4,32,224]{3,2,0,1:T(8,128)S(1)}, u32[]{:S(2)}) copy-start(f32[2,4,32,224]{3,2,0,1:T(8,128)S(1)} %fusion.59) | copy-start | bytes 688132
  69.0 17.9 %all-to-all-start.3 = ((bf16[8,32,2048]{2,1,0:T(8,128)(2,1)}), bf16[8,32,2048]{2,1,0:T(8,128)(2,1)S(1)}, u32[]{:S(2)}, u32[]{:S(2)}) async-start(bf16[8,32,2048]{2,1,0:T(8,128)(2,1)} %bitcast.38), calls=%async_computation.3 | async-start | bytes 2097152 | tf_op jit(solution)/shard_map/all_to_all | solution.py:92
  80.1 24.3 %copy-start.7 = (bf16[2,64,2048]{2,1,0:T(8,128)(2,1)S(1)}, bf16[2,64,2048]{2,1,0:T(8,128)(2,1)}, u32[]{:S(2)}) copy-start(bf16[2,64,2048]{2,1,0:T(8,128)(2,1)} %param.11) | copy-start | bytes 1572868
  86.9 17.1 %all-to-all-start.1 = ((bf16[8,32,2048]{2,1,0:T(8,128)(2,1)}), bf16[8,32,2048]{2,1,0:T(8,128)(2,1)S(1)}, u32[]{:S(2)}, u32[]{:S(2)}) async-start(bf16[8,32,2048]{2,1,0:T(8,128)(2,1)} %bitcast.325), calls=%async_computation.1 | async-start | bytes 2097152 | tf_op jit(solution)/shard_map/all_to_all | solution.py:92
  104.0 101.6 %copy-start.11 = (f32[64,2048]{1,0:T(8,128)S(1)}, f32[64,2048]{1,0:T(8,128)}, u32[]{:S(2)}) copy-start(f32[64,2048]{1,0:T(8,128)} %fusion.188) | copy-start | bytes 1572868
  104.0 101.6 %copy-start.12 = (f32[64,2048]{1,0:T(8,128)S(1)}, f32[64,2048]{1,0:T(8,128)}, u32[]{:S(2)}) copy-start(f32[64,2048]{1,0:T(8,128)} %fusion.187) | copy-start | bytes 1572868
  208.1 6.0 copy-start.19
  208.1 13.9 %all-to-all-start.6 = ((bf16[8,32,2048]{2,1,0:T(8,128)(2,1)}), bf16[8,32,2048]{2,1,0:T(8,128)(2,1)S(1)}, u32[]{:S(2)}, u32[]{:S(2)}) async-start(bf16[8,32,2048]{2,1,0:T(8,128)(2,1)} %bitcast.61), calls=%async_computation.6 | async-start | bytes 2097152 | tf_op jit(solution)/shard_map/all_to_all | solution.py:109
  222.0 13.0 %all-to-all-start.4 = ((bf16[8,32,2048]{2,1,0:T(8,128)(2,1)}), bf16[8,32,2048]{2,1,0:T(8,128)(2,1)S(1)}, u32[]{:S(2)}, u32[]{:S(2)}) async-start(bf16[8,32,2048]{2,1,0:T(8,128)(2,1)} %bitcast.46), calls=%async_computation.4 | async-start | bytes 2097152 | tf_op jit(solution)/shard_map/all_to_all | solution.py:109
  234.9 13.0 %all-to-all-start.7 = ((bf16[8,32,2048]{2,1,0:T(8,128)(2,1)}), bf16[8,32,2048]{2,1,0:T(8,128)(2,1)S(1)}, u32[]{:S(2)}, u32[]{:S(2)}) async-start(bf16[8,32,2048]{2,1,0:T(8,128)(2,1)} %bitcast.65), calls=%async_computation.7 | async-start | bytes 2097152 | tf_op jit(solution)/shard_map/all_to_all | solution.py:124
  247.9 13.0 %all-to-all-start.5 = ((bf16[8,32,2048]{2,1,0:T(8,128)(2,1)}), bf16[8,32,2048]{2,1,0:T(8,128)(2,1)S(1)}, u32[]{:S(2)}, u32[]{:S(2)}) async-start(bf16[8,32,2048]{2,1,0:T(8,128)(2,1)} %bitcast.50), calls=%async_computation.5 | async-start | bytes 2097152 | tf_op jit(solution)/shard_map/all_to_all | solution.py:124
  251.5 365.6 %all-reduce.7.cloned.1.call-start = ((), (), s32[]{:S(2)}) async-start(), calls=%async_computation.12 | async-start | bytes 4194304 | tf_op jit(solution)/shard_map/psum | solution.py:130
  251.8 10.5 %copy-start.23 = (s32[64,2]{0,1:T(2,128)S(1)}, s32[64,2]{0,1:T(2,128)}, u32[]{:S(2)}) copy-start(s32[64,2]{0,1:T(2,128)} %get-tuple-element.32) | copy-start | bytes 1540
  251.9 10.5 %copy-start.22 = (s32[64,2]{0,1:T(2,128)S(1)}, s32[64,2]{0,1:T(2,128)}, u32[]{:S(2)}) copy-start(s32[64,2]{0,1:T(2,128)} %get-tuple-element.31) | copy-start | bytes 1540
  251.9 10.5 %copy-start.14 = (bf16[2,64,2048]{2,1,0:T(8,128)(2,1)S(1)}, bf16[2,64,2048]{2,1,0:T(8,128)(2,1)}, u32[]{:S(2)}) copy-start(bf16[2,64,2048]{2,1,0:T(8,128)(2,1)} %param.10) | copy-start | bytes 1572868
  251.9 10.5 %copy-start.32 = (f32[64]{0:T(128)S(1)}, f32[64]{0:T(128)}, u32[]{:S(2)}) copy-start(f32[64]{0:T(128)} %copy-done.31) | copy-start | bytes 772
  253.0 10.0 %copy-start.24 = (f32[64]{0:T(128)S(1)}, f32[64]{0:T(128)}, u32[]{:S(2)}) copy-start(f32[64]{0:T(128)} %get-tuple-element.25) | copy-start | bytes 772
  253.0 10.0 %copy-start.30 = (f32[64]{0:T(128)S(1)}, f32[64]{0:T(128)}, u32[]{:S(2)}) copy-start(f32[64]{0:T(128)} %copy-done.29) | copy-start | bytes 772
  262.3 358.6 %copy-start.26 = (f32[64]{0:T(128)S(1)}, f32[64]{0:T(128)}, u32[]{:S(2)}) copy-start(f32[64]{0:T(128)} %copy-done.25) | copy-start | bytes 772
  262.3 358.6 %copy-start.28 = (f32[64]{0:T(128)S(1)}, f32[64]{0:T(128)}, u32[]{:S(2)}) copy-start(f32[64]{0:T(128)} %copy-done.27) | copy-start | bytes 772
  262.3 358.6 %copy-start.8 = (bf16[2,64,2048]{2,1,0:T(8,128)(2,1)S(1)}, bf16[2,64,2048]{2,1,0:T(8,128)(2,1)}, u32[]{:S(2)}) copy-start(bf16[2,64,2048]{2,1,0:T(8,128)(2,1)} %param.11) | copy-start | bytes 1572868
  262.3 396.3 %all-reduce.5.cloned.1.call-start = ((), (), s32[]{:S(2)}) async-start(), calls=%async_computation.11 | async-start | bytes 131072 | tf_op jit(solution)/shard_map/psum | solution.py:139
  (14 other events, 37.6 us)
Sparse Core Ops, SparseCore 0:
  9.7 18.0 all-gather.5
  29.4 16.9 all-gather.3
  48.0 16.9 all-gather.7
  262.4 354.6 all-reduce.6
  620.1 38.4 all-reduce.4
where the time goes:
time: 669 us; the launch traced here: 667 us
  waiting for transfers between devices  449 us (67%)
  blocking collectives  105 us (16%)
  matrix products  46.7 us (7%)
  starting transfers between devices  29.1 us (4%)
  between operations  14.5 us (2%)
  local copies, waits for them, and re-layouts  14.2 us (2%)
  other arithmetic  8.5 us (1%)
    psum x1, waiting for transfers between devices, shards(): mixed = lax.psum(mixed_part, 'dp')  353 us
    psum x1, blocking collectives, shards(): dnormed, gate_sums = lax.psum((dnormed_part, gate_part), 'dp')  96.8 us
    psum x1, waiting for transfers between devices, shards(): lax.psum((router_total, gain_total), ('section', 'expert'))  26.5 us
    all_to_all x2, waiting for transfers between devices, shards(): lax.all_to_all(block_out.reshape(experts, capacity, model_width), 'expert...  18.2 us
    all_gather x1, waiting for transfers between devices, shards(): lax.all_gather(w_down, 'section', axis=2, tiled=True)  15.4 us
  transfers between devices with their start and end apart: 13, of which 11 were waited for; matrix products, arithmetic and copies ran while one was open for 8% of the time, Pallas kernels for 0%

commit v1 on v0

v1 whole, which is shorter than its diff:
```python
import functools

import jax
import jax.numpy as jnp
from jax import lax
from jax.experimental import pallas as pl
from jax.experimental.pallas import tpu as pltpu
from jax.sharding import PartitionSpec as P

EPSILON = 1e-05
EXT = 128
F32 = jnp.float32
BF16 = jnp.bfloat16
HIGHEST = lax.Precision.HIGHEST
NT = (((1,), (1,)), ((), ()))
VMEM_BYTES = 40 * 1024 * 1024


def params():
    return pltpu.CompilerParams(vmem_limit_bytes=VMEM_BYTES)


def lanes(rows):
    return lax.broadcasted_iota(jnp.int32, (rows, EXT), 1)


def split_low(value):
    high = value.astype(BF16).astype(F32)
    return high, value - high


def inverse_rms(wide):
    return lax.rsqrt(jnp.mean(wide * wide, axis=-1, keepdims=True) + EPSILON)


def prologue_kernel(x_ref, gain_ref, router_ref, routes_ref, rows_ref, coef_ref):
    width = x_ref.shape[1]
    count = router_ref.shape[0]
    wide = x_ref[...].astype(F32)
    normed = wide * inverse_rms(wide) * gain_ref[...]
    rows_ref[:, :width] = normed.astype(BF16)
    logits = lax.dot_general(normed, router_ref[...], NT, precision=HIGHEST, preferred_element_type=F32)
    first, second = routes_ref[:, 0:1], routes_ref[:, 1:2]
    column = lax.broadcasted_iota(jnp.int32, logits.shape, 1)
    signs = (column == first).astype(F32) - (column == second).astype(F32)
    leading = jax.nn.sigmoid(jnp.sum(signs * logits, axis=1, keepdims=True))
    trailing = 1.0 - leading
    lead_high, lead_low = split_low(leading)
    trail_high, trail_low = split_low(trailing)
    lane = lanes(x_ref.shape[0])

    def place(start, at_first, at_second):
        return jnp.where(lane == first + start, at_first, 0.0) + jnp.where(
            lane == second + start, at_second, 0.0
        )

    extra = (
        place(0, lead_high, trail_high)
        + place(count, lead_low, trail_low)
        + place(2 * count, 1.0, -1.0)
    )
    rows_ref[:, width:] = extra.astype(BF16)
    slope = leading * trailing
    coef_ref[...] = place(0, slope, -slope)


def forward_kernel(
    count,
    meta,
    rows_own, rows_a, rows_b, cot_own, cot_a, cot_b,
    gate_0, gate_1, up_0, up_1, down_0, down_1,
    mix_own, mix_a, mix_b, dgate_ref, dup_ref, sums_ref,
    r_0, r_1, c_0, c_1, acc_0, acc_1, aux,
):
    step = pl.program_id(0)
    local = pl.num_programs(0)
    half = acc_0.shape[1]
    own, sub = rows_own.shape[0], rows_a.shape[0]
    at_0 = pl.multiple_of(meta[0] * half, half)
    at_1 = pl.multiple_of((1 - meta[0]) * half, half)
    parts = ((0, own, rows_own, cot_own), (own, sub, rows_a, cot_a), (own + sub, sub, rows_b, cot_b))

    @pl.when(step == 0)
    def _():
        for start, size, rows, cot in parts:
            r_0[start:start + size, :] = rows[:, pl.ds(at_0, half)]
            r_1[start:start + size, :] = rows[:, pl.ds(at_1, half)]
            c_0[start:start + size, :] = cot[:, pl.ds(at_0, half)]
            c_1[start:start + size, :] = cot[:, pl.ds(at_1, half)]
            aux[start:start + size, :] = rows[:, 2 * half:].astype(F32)
        acc_0[...] = jnp.zeros_like(acc_0)
        acc_1[...] = jnp.zeros_like(acc_1)
        sums_ref[...] = jnp.zeros_like(sums_ref)

    def both(left_0, left_1, map_0, map_1):
        return lax.dot_general(left_0[...], map_0[0], NT, preferred_element_type=F32) + lax.dot_general(
            left_1[...], map_1[0], NT, preferred_element_type=F32
        )

    expert = meta[1] * local + step
    lane = lanes(aux.shape[0])
    extra = aux[...]
    weight = jnp.sum(
        jnp.where((lane == expert) | (lane == expert + count), extra, 0.0), axis=1, keepdims=True
    )
    sign = jnp.sum(jnp.where(lane == expert + 2 * count, extra, 0.0), axis=1, keepdims=True)
    pre_gate = both(r_0, r_1, gate_0, gate_1)
    pre_up = both(r_0, r_1, up_0, up_1)
    dhid = both(c_0, c_1, down_0, down_1)
    squash = jax.nn.sigmoid(pre_gate)
    act = pre_gate * squash
    hidden = act * pre_up
    gate_sum = jnp.sum(hidden * dhid, axis=1, keepdims=True) * sign
    sums_ref[...] += jnp.where(lane == 0, gate_sum, 0.0)
    dhid = dhid * weight
    dgate_ref[0] = (dhid * pre_up * (squash + act * (1.0 - squash))).astype(BF16)
    dup_ref[0] = (dhid * act).astype(BF16)
    weighted = (hidden * weight).astype(BF16)
    acc_0[...] += jnp.dot(weighted, down_0[0], preferred_element_type=F32)
    acc_1[...] += jnp.dot(weighted, down_1[0], preferred_element_type=F32)

    @pl.when(step == local - 1)
    def _():
        for start, size, out in ((0, own, mix_own), (own, sub, mix_a), (own + sub, sub, mix_b)):
            out[:, pl.ds(at_0, half)] = acc_0[start:start + size, :].astype(BF16)
            out[:, pl.ds(at_1, half)] = acc_1[start:start + size, :].astype(BF16)


def backward_kernel(
    meta,
    dgate_ref, dup_ref, gate_0, gate_1, up_0, up_1, rows_own, rows_a, rows_b, sums_ref,
    dn_own, dn_a, dn_b, gain_ext,
    acc_0, acc_1, line, block,
):
    step = pl.program_id(0)
    half = acc_0.shape[1]
    own, sub = rows_own.shape[0], rows_a.shape[0]
    at_0 = pl.multiple_of(meta[0] * half, half)
    at_1 = pl.multiple_of((1 - meta[0]) * half, half)

    @pl.when(step == 0)
    def _():
        acc_0[...] = jnp.zeros_like(acc_0)
        acc_1[...] = jnp.zeros_like(acc_1)

    dgate, dup = dgate_ref[0], dup_ref[0]
    for acc, gate_map, up_map in ((acc_0, gate_0, up_0), (acc_1, gate_1, up_1)):
        acc[...] += jnp.dot(dgate, gate_map[0], preferred_element_type=F32) + jnp.dot(
            dup, up_map[0], preferred_element_type=F32
        )

    @pl.when(step == pl.num_programs(0) - 1)
    def _():
        high, low = split_low(sums_ref[:, 0:1])
        lane = lanes(sums_ref.shape[0])
        extra = jnp.where(lane == 0, high, jnp.where(lane == 1, low, 0.0)).astype(BF16)
        totals = [0.0, 0.0]
        for start, size, out, rows in (
            (0, own, dn_own, rows_own), (own, sub, dn_a, rows_a), (own + sub, sub, dn_b, rows_b),
        ):
            out[:, 2 * half:] = extra[start:start + size, :]
            for which, (acc, at) in enumerate(((acc_0, at_0), (acc_1, at_1))):
                value = acc[start:start + size, :]
                out[:, pl.ds(at, half)] = value.astype(BF16)
                totals[which] += jnp.sum(
                    value * rows[:, pl.ds(at, half)].astype(F32), axis=0, keepdims=True
                )
        line[:, pl.ds(at_0, half)] = totals[0]
        line[:, pl.ds(at_1, half)] = totals[1]
        block[...] = jnp.zeros_like(block)
        for place in range(2 * half // EXT):
            high, low = split_low(line[:, place * EXT:(place + 1) * EXT])
            block[8 * place:8 * place + 1, :] = high
            block[8 * place + 1:8 * place + 2, :] = low
        gain_ext[...] = block[...].astype(BF16)


def pack_kernel(mix_own, mix_a, mix_b, gain_ext, dn_own, dn_a, dn_b, out_ref):
    own, width = mix_own.shape
    sub = mix_a.shape[0]
    for start, mix, grad in ((0, mix_a, dn_a), (sub, mix_b, dn_b)):
        span = slice(start, start + sub)
        out_ref[span, :width] = (mix_own[span, :].astype(F32) + mix[...].astype(F32)).astype(BF16)
        under = slice(own + start, own + start + sub)
        out_ref[under, :width] = (
            dn_own[span, :width].astype(F32) + grad[:, :width].astype(F32)
        ).astype(BF16)
        both = dn_own[span, width:].astype(F32) + grad[:, width:].astype(F32)
        high, low = split_low(jnp.sum(both, axis=1, keepdims=True))
        lane = lanes(sub)
        out_ref[under, width:] = jnp.where(lane == 0, high, jnp.where(lane == 1, low, 0.0)).astype(BF16)
    out_ref[:own, width:] = gain_ext[...]


def finish_kernel(meta, parts_ref, x_ref, cot_ref, coef_ref, gain_ref, router_ref, out_ref):
    chunks, rows, _ = parts_ref.shape
    width = x_ref.shape[2]
    total = parts_ref[0].astype(F32)
    for source in range(1, chunks):
        total = total + parts_ref[source].astype(F32)
    wide = x_ref[0].astype(F32)
    summed, extra = total[:, :width], total[:, width:]
    lane = lanes(rows)
    row = lax.broadcasted_iota(jnp.int32, (rows, EXT), 0)
    is_first = meta[0] < chunks // 2
    layer = wide + summed
    gain_high, gain_low = split_low(extra[0:1, :] + extra[1:2, :])
    layer_extra = jnp.where(row == 0, gain_high, jnp.where(row == 1, gain_low, 0.0))
    sums = extra[:, 0:1] + extra[:, 1:2]
    sum_high, sum_low = split_low(sums)
    grad_extra = jnp.where(lane == 0, sum_high, jnp.where(lane == 1, sum_low, 0.0))
    dlogits = coef_ref[0] * sums
    dnormed = summed
    for expert in range(router_ref.shape[0]):
        dnormed = dnormed + dlogits[:, expert:expert + 1] * router_ref[expert:expert + 1, :]
    scaling = inverse_rms(wide)
    unit = wide * scaling
    dunit = dnormed * gain_ref[...]
    dx = scaling * (dunit - unit * jnp.mean(dunit * unit, axis=-1, keepdims=True))
    grad = cot_ref[0].astype(F32) + dx
    out = jnp.where(is_first, layer, grad).astype(BF16)
    out_extra = jnp.where(is_first, layer_extra, grad_extra).astype(BF16)
    for place in range(chunks):
        out_ref[place, :, :width] = out
        out_ref[place, :, width:] = out_extra


def tail_kernel(all_ref, x_ref, coef_ref, layer_ref, grad_ref, sums_ref, wide_sums):
    chunks = all_ref.shape[0]
    width = x_ref.shape[1]
    mid = chunks // 2
    layer_ref[...] = all_ref[:mid, :, :width]
    grad_ref[...] = all_ref[mid:, :, :width]
    for place in range(mid):
        wide_sums[8 * place:8 * place + 8, :] = all_ref[mid + place, :, width:].astype(F32)
    dlogits = coef_ref[...] * (wide_sums[:, 0:1] + wide_sums[:, 1:2])
    wide = x_ref[...].astype(F32)
    unit = wide * inverse_rms(wide)
    sums_ref[0:8, :] = jnp.dot(dlogits.T[0:8, :], unit, precision=HIGHEST, preferred_element_type=F32)
    sums_ref[8:16, :] = jnp.zeros((8, width), F32)
    for place in range(mid):
        extra = all_ref[place, :, width:].astype(F32)
        sums_ref[8:9, place * EXT:(place + 1) * EXT] = extra[0:1, :] + extra[1:2, :]


def whole(array):
    return pl.BlockSpec(array.shape, lambda *_: (0,) * len(array.shape))


def struct(*shape, dtype=BF16):
    return jax.ShapeDtypeStruct(shape, dtype)


def shards(n_dp, inputs, cotangent, w_gate, w_up, w_down, router, norm_gain, routes):
    micro, sub, width = inputs.shape
    own = micro * sub
    total = 2 * own
    local, units, half = w_gate.shape
    count = router.shape[1]
    section, expert = lax.axis_index("section"), lax.axis_index("expert")
    place = lax.axis_index("dp")
    meta = jnp.stack([section, expert]).astype(jnp.int32)

    def around(shift):
        pairs = []
        for e in range(2):
            for d in range(n_dp):
                x = (d % 2 * 2 + e + shift) % 4
                pairs.append((e * n_dp + d, (x % 2) * n_dp + d - d % 2 + x // 2))
        return pairs

    def up_x(array):
        return lax.ppermute(array, ("expert", "dp"), around(1))

    def down_x(array):
        return lax.ppermute(array, ("expert", "dp"), around(3))

    def other_core(array):
        return lax.ppermute(array, "section", [(0, 1), (1, 0)])

    def other_expert(array):
        return lax.ppermute(array, "expert", [(0, 1), (1, 0)])

    maps = [(w, other_core(w)) for w in (w_gate, w_up, w_down)]
    (gate_0, gate_1), (up_0, up_1), (down_0, down_1) = maps
    cot_a, cot_b = up_x(cotangent[0]), down_x(cotangent[1])
    flat_x = inputs.reshape(own, width)
    flat_cot = cotangent.reshape(own, width)
    gain_row = norm_gain.reshape(1, width)
    router_rows = router.T
    rows_own, coef = pl.pallas_call(
        prologue_kernel,
        out_shape=(struct(own, width + EXT), struct(own, EXT, dtype=F32)),
        compiler_params=params(),
    )(flat_x, gain_row, router_rows, routes.reshape(own, 2))
    rows_a, rows_b = up_x(rows_own[:sub]), down_x(rows_own[sub:])

    map_spec = pl.BlockSpec((1, units, half), lambda i, m: (i, 0, 0))
    unit_spec = pl.BlockSpec((1, total, units), lambda i, m: (i, 0, 0))
    token_args = (rows_own, rows_a, rows_b, flat_cot, cot_a, cot_b)
    forward_out = (
        struct(own, width), struct(sub, width), struct(sub, width),
        struct(local, total, units), struct(local, total, units), struct(total, EXT, dtype=F32),
    )
    mix_own, mix_a, mix_b, dgate, dup, sums = pl.pallas_call(
        functools.partial(forward_kernel, count),
        grid_spec=pltpu.PrefetchScalarGridSpec(
            num_scalar_prefetch=1,
            grid=(local,),
            in_specs=[whole(a) for a in token_args] + [map_spec] * 6,
            out_specs=[whole(a) for a in forward_out[:3]] + [unit_spec, unit_spec, whole(forward_out[5])],
            scratch_shapes=[pltpu.VMEM((total, half), BF16)] * 4
            + [pltpu.VMEM((total, half), F32)] * 2
            + [pltpu.VMEM((total, EXT), F32)],
        ),
        out_shape=forward_out,
        compiler_params=params(),
        cost_estimate=pl.CostEstimate(
            flops=16 * total * local * units * half, bytes_accessed=24 * local * units * half, transcendentals=0
        ),
    )(meta, *token_args, gate_0, gate_1, up_0, up_1, down_0, down_1)
    mix_a, mix_b = up_x(mix_a), down_x(mix_b)

    backward_out = (struct(own, width + EXT), struct(sub, width + EXT), struct(sub, width + EXT), struct(own, EXT))
    row_args = (rows_own, rows_a, rows_b, sums)
    dn_own, dn_a, dn_b, gain_ext = pl.pallas_call(
        backward_kernel,
        grid_spec=pltpu.PrefetchScalarGridSpec(
            num_scalar_prefetch=1,
            grid=(local,),
            in_specs=[unit_spec] * 2 + [map_spec] * 4 + [whole(a) for a in row_args],
            out_specs=[whole(a) for a in backward_out],
            scratch_shapes=[pltpu.VMEM((total, half), F32)] * 2
            + [pltpu.VMEM((1, width), F32), pltpu.VMEM((own, EXT), F32)],
        ),
        out_shape=backward_out,
        compiler_params=params(),
        cost_estimate=pl.CostEstimate(
            flops=8 * total * local * units * half, bytes_accessed=16 * local * units * half, transcendentals=0
        ),
    )(meta, dgate, dup, gate_0, gate_1, up_0, up_1, *row_args)
    dn_a, dn_b = up_x(dn_a), down_x(dn_b)

    packed = pl.pallas_call(
        pack_kernel, out_shape=struct(total, width + EXT), compiler_params=params()
    )(mix_own, mix_a, mix_b, gain_ext, dn_own, dn_a, dn_b)
    rows_each = total // n_dp
    chunks = lax.all_to_all(packed.reshape(n_dp, rows_each, width + EXT), "dp", 0, 0, tiled=True)

    blocks = own // rows_each
    spot = jnp.stack([place, place % blocks]).astype(jnp.int32)

    def at_spot(last):
        return pl.BlockSpec((1, rows_each, last), lambda i, m: (m[1], 0, 0))

    finished = pl.pallas_call(
        finish_kernel,
        grid_spec=pltpu.PrefetchScalarGridSpec(
            num_scalar_prefetch=1,
            grid=(1,),
            in_specs=[whole(chunks), at_spot(width), at_spot(width), at_spot(EXT), whole(gain_row), whole(router_rows)],
            out_specs=whole(chunks),
        ),
        out_shape=struct(*chunks.shape),
        compiler_params=params(),
    )(
        spot,
        chunks,
        inputs.reshape(blocks, rows_each, width),
        cotangent.reshape(blocks, rows_each, width),
        coef.reshape(blocks, rows_each, EXT),
        gain_row,
        router_rows,
    )
    gathered = lax.all_to_all(finished, "dp", 0, 0, tiled=True)

    layer, grad, summed = pl.pallas_call(
        tail_kernel,
        out_shape=(
            struct(blocks, rows_each, width), struct(blocks, rows_each, width), struct(16, width, dtype=F32),
        ),
        scratch_shapes=[pltpu.VMEM((own, EXT), F32)],
        compiler_params=params(),
    )(gathered, flat_x, coef)
    summed = summed + other_core(summed)
    summed = summed + other_expert(summed)
    moments = summed[:count]
    grad_router = (moments * gain_row).T
    grad_gain = summed[8] / norm_gain + jnp.sum(router_rows * moments, axis=0)
    return layer.reshape(micro, sub, width), grad.reshape(micro, sub, width), grad_router, grad_gain


def solution(mesh):
    tokens = P(None, ("section", "expert"), None)
    maps = P("expert", "dp", "section")
    return jax.shard_map(
        functools.partial(shards, mesh.shape["dp"]),
        mesh=mesh,
        in_specs=(tokens, tokens, maps, maps, maps, P(), P(), tokens),
        out_specs=(tokens, tokens, P(), P()),
        check_vma=False,
    )
```

time: 669 us -> 120 us (0.18)
  waiting for transfers between devices: 449 us -> 40.8 us
  blocking collectives: 105 us -> 22.2 us
  matrix products: 46.7 us -> 0 us
  Pallas kernels: 0 us -> 19.4 us
  between operations: 14.5 us -> 0.81 us
  other arithmetic: 8.5 us -> 1.43 us
    psum x2 -> x0, waiting for transfers between devices: 379 us -> none  [the longest x1 353 us: shards(): mixed = lax.psum(mixed_part, 'dp')]
    psum x2 -> x0, blocking collectives: 105 us -> none  [the longest x1 96.8 us: shards(): dnormed, gate_sums = lax.psum((dnormed_part, gate_part), 'dp')]
    dot_general x32 -> x0, matrix products: 46.7 us -> none  [the longest x8 7.82 us: pick_rows(): lax.dot_general(selector, flat_rows, (((0,), (0,)), ((), ())), preferred_...]
    all_to_all x8 -> x1, waiting for transfers between devices: 44.1 us -> 17.7 us  [shards(): lax.all_to_all(packed.reshape(n_dp, rows_each, width + EXT), 'dp', 0, 0,...]
    all_gather x3 -> x0, waiting for transfers between devices: 23.3 us -> none  [the longest x1 15.4 us: shards(): lax.all_gather(w_down, 'section', axis=2, tiled=True)]
    ppermute x0 -> x13, waiting for transfers between devices: none -> 23.1 us  [the longest x4 10.8 us: up_x(): return lax.ppermute(array, ('expert', 'dp'), around(1))]
    all_to_all x0 -> x1, blocking collectives: none -> 22.2 us  [shards(): gathered = lax.all_to_all(finished, 'dp', 0, 0, tiled=True)]
    all_to_all x8 -> x1, starting transfers between devices: 28.9 us -> 9.36 us  [shards(): lax.all_to_all(packed.reshape(n_dp, rows_each, width + EXT), 'dp', 0, 0,...]
  transfers between devices with their start and end apart: 13 -> 14, of which waited for: 11 -> 7; matrix products, arithmetic and copies ran while one was open for 8% -> 2% of each run, Pallas kernels for 0% -> 1%
where the time goes in v1:
time: 120 us; the launch traced here: 119 us
  waiting for transfers between devices  40.8 us (34%)
  starting transfers between devices  25.3 us (21%)
  blocking collectives  22.2 us (18%)
  Pallas kernels  19.4 us (16%)
  local copies, waits for them, and re-layouts  8.98 us (7%)
  other arithmetic  1.43 us (1%)
    all_to_all x1, blocking collectives, shards(): gathered = lax.all_to_all(finished, 'dp', 0, 0, tiled=True)  22.2 us
    all_to_all x1, waiting for transfers between devices, shards(): lax.all_to_all(packed.reshape(n_dp, rows_each, width + EXT), 'dp', 0, 0,...  17.7 us
    ppermute x4, starting transfers between devices, down_x(): return lax.ppermute(array, ('expert', 'dp'), around(3))  13.1 us
    ppermute x4, waiting for transfers between devices, up_x(): return lax.ppermute(array, ('expert', 'dp'), around(1))  10.8 us
    all_to_all x1, starting transfers between devices, shards(): lax.all_to_all(packed.reshape(n_dp, rows_each, width + EXT), 'dp', 0, 0,...  9.36 us
    pallas_call x1, Pallas kernels, shards(): pl.pallas_call(functools.partial(forward_kernel, count), grid_spec=pltpu....  8.22 us
    unnamed x25, local copies, waits for them, and re-layouts  7.87 us
    ppermute x4, waiting for transfers between devices, down_x(): return lax.ppermute(array, ('expert', 'dp'), around(3))  7.16 us
  transfers between devices with their start and end apart: 14, of which 7 were waited for; matrix products, arithmetic and copies ran while one was open for 2% of the time, Pallas kernels for 1%

profile of v1, /device:TPU:0, one launch (start us, length us, event | category | flops | bytes accessed | tf_op | source)
XLA Modules:
  0.0 118.9 jit_solution(9812052007460007859)
XLA Ops:
  0.7 0.5 collective-permute-start.4
  1.2 0.1 collective-permute-start.5
  1.3 1.1 slice_bitcast_fusion
  2.4 2.9 %collective-permute-start.3 = (bf16[64,2048]{1,0:T(8,128)(2,1)S(1)}, bf16[64,2048]{1,0:T(8,128)(2,1)S(1)}, u32[]{:S(2)}, u32[]{:S(2)}) collective-permute-start(bf16[64,2048]{1,0:T(8,128)(2,1)S(1)} %get-tuple-element.36), channel_id=1, source_target_pairs={{0,33},{1,32},{2,35},{3,34},{4,37},{5,36},{6,39},{7,38},{8,41},{9,... | collective-permute-start | bytes 786440 | tf_op jit(solution)/shard_map/ppermute | solution.py:276
  5.3 0.8 copy.12
  6.1 1.0 copy-done
  7.1 0.8 copy-done.7
  8.0 0.7 copy-done.9
  8.7 1.2 %shard_map.111 = (bf16[128,2176]{1,0:T(8,128)(2,1)S(1)}, f32[128,128]{1,0:T(8,128)S(1)}) custom-call(bf16[128,2048]{1,0:T(8,128)(2,1)S(1)} %bitcast.23, f32[1,2048]{1,0:T(1,128)S(1)} %bitcast.32, f32[8,2048]{1,0:T(8,128)S(1)} %bitcast.28, s32[128,2]{1,0:T(8,128)S(1)} %bitcast.30), custom_call_target="tpu_custom_call" | custom-call | tf_op jit(solution)/shard_map/pallas_call | solution.py:291
  9.9 1.5 %collective-permute-done.3.cot_b = bf16[64,2048]{1,0:T(8,128)(2,1)S(1)} collective-permute-done((bf16[64,2048]{1,0:T(8,128)(2,1)S(1)}, bf16[64,2048]{1,0:T(8,128)(2,1)S(1)}, u32[]{:S(2)}, u32[]{:S(2)}) %collective-permute-start.3) | collective-permute-done | bytes 262176 | tf_op jit(solution)/shard_map/ppermute | solution.py:276
  11.5 3.7 %collective-permute-start.1 = (bf16[64,2176]{1,0:T(8,128)(2,1)S(1)}, bf16[64,2176]{1,0:T(8,128)(2,1)S(1)}, u32[]{:S(2)}, u32[]{:S(2)}) collective-permute-start(bf16[64,2176]{1,0:T(8,128)(2,1)S(1)} %get-tuple-element.34), channel_id=1, source_target_pairs={{0,33},{1,32},{2,35},{3,34},{4,37},{5,36},{6,39},{7,38},{8,41},{9,... | collective-permute-start | bytes 835592 | tf_op jit(solution)/shard_map/ppermute | solution.py:276
  15.2 5.6 %collective-permute-done.1.rows_b = bf16[64,2176]{1,0:T(8,128)(2,1)S(1)} collective-permute-done((bf16[64,2176]{1,0:T(8,128)(2,1)S(1)}, bf16[64,2176]{1,0:T(8,128)(2,1)S(1)}, u32[]{:S(2)}, u32[]{:S(2)}) %collective-permute-start.1) | collective-permute-done | bytes 278560 | tf_op jit(solution)/shard_map/ppermute | solution.py:276
  20.9 3.4 %collective-permute-done.rows_a = bf16[64,2176]{1,0:T(8,128)(2,1)S(1)} collective-permute-done((bf16[64,2176]{1,0:T(8,128)(2,1)S(1)}, bf16[64,2176]{1,0:T(8,128)(2,1)S(1)}, u32[]{:S(2)}, u32[]{:S(2)}) %collective-permute-start) | collective-permute-done | bytes 278560 | tf_op jit(solution)/shard_map/ppermute | solution.py:273
  24.3 1.5 %copy-done.3 = bf16[4,224,1024]{2,1,0:T(8,128)(2,1)S(1)} copy-done((bf16[4,224,1024]{2,1,0:T(8,128)(2,1)S(1)}, bf16[4,224,1024]{2,1,0:T(8,128)(2,1)}, u32[]{:S(2)}) %copy-start.3) | copy-done | bytes 1835032
  25.8 1.5 %copy-done.5 = bf16[4,224,1024]{2,1,0:T(8,128)(2,1)S(1)} copy-done((bf16[4,224,1024]{2,1,0:T(8,128)(2,1)S(1)}, bf16[4,224,1024]{2,1,0:T(8,128)(2,1)}, u32[]{:S(2)}) %copy-start.5) | copy-done | bytes 1835032
  27.3 1.5 %copy-done.11 = bf16[4,224,1024]{2,1,0:T(8,128)(2,1)S(1)} copy-done((bf16[4,224,1024]{2,1,0:T(8,128)(2,1)S(1)}, bf16[4,224,1024]{2,1,0:T(8,128)(2,1)}, u32[]{:S(2)}) %copy-start.11) | copy-done | bytes 1835032
  28.8 8.2 %shard_map.112 = (bf16[128,2048]{1,0:T(8,128)(2,1)S(1)}, bf16[64,2048]{1,0:T(8,128)(2,1)S(1)}, bf16[64,2048]{1,0:T(8,128)(2,1)S(1)}, bf16[4,256,224]{2,1,0:T(8,1...) custom-call(s32[2]{0:T(128)S(1)} %pad_add_fusion.1.meta, ...), custom_call_target="tpu_custom_call" | custom-call | flops 3758096384 | bytes 22020096 | tf_op jit(solution)/shard_map/pallas_call | solution.py:305
  37.1 5.7 %shard_map.113 = (bf16[128,2176]{1,0:T(8,128)(2,1)S(1)}, bf16[64,2176]{1,0:T(8,128)(2,1)S(1)}, bf16[64,2176]{1,0:T(8,128)(2,1)S(1)}, bf16[128,128]{1,0:T(8,128)(2,1)S(1)}) custom-call(s32[2]{0:T(128)S(1)} %pad_add_fusion.1.meta, bf16[4,256,224]{2,1,0:T(8,128)(2,1)S(1)} %get-tuple-element.23.dgate_ref, bf16[4,256,224]{2,1,0:T(8,128)(2,1)S(1)} %get-tuple-element.24.dup_ref, ...), custom_call_target="tpu_custom_call" | custom-call | flops 1879048192 | bytes 14680064 | tf_op jit(solution)/shard_map/pallas_call | solution.py:326
  42.9 3.2 %collective-permute-start.10 = (bf16[64,2176]{1,0:T(8,128)(2,1)S(1)}, bf16[64,2176]{1,0:T(8,128)(2,1)S(1)}, u32[]{:S(2)}, u32[]{:S(2)}) collective-permute-start(bf16[64,2176]{1,0:T(8,128)(2,1)S(1)} %get-tuple-element.29), channel_id=1, source_target_pairs={{0,33},{1,32},{2,35},{3,34},{4,37},{5,36},{6,39},{7,38},{8,41},{9,... | collective-permute-start | bytes 835592 | tf_op jit(solution)/shard_map/ppermute | solution.py:276
  46.1 3.2 %collective-permute-start.8 = (bf16[64,2048]{1,0:T(8,128)(2,1)S(1)}, bf16[64,2048]{1,0:T(8,128)(2,1)S(1)}, u32[]{:S(2)}, u32[]{:S(2)}) collective-permute-start(bf16[64,2048]{1,0:T(8,128)(2,1)S(1)} %get-tuple-element.22), channel_id=1, source_target_pairs={{0,33},{1,32},{2,35},{3,34},{4,37},{5,36},{6,39},{7,38},{8,41},{9,... | collective-permute-start | bytes 786440 | tf_op jit(solution)/shard_map/ppermute | solution.py:276
  49.4 7.4 %collective-permute-done.7.mix_a = bf16[64,2048]{1,0:T(8,128)(2,1)S(1)} collective-permute-done((bf16[64,2048]{1,0:T(8,128)(2,1)S(1)}, bf16[64,2048]{1,0:T(8,128)(2,1)S(1)}, u32[]{:S(2)}, u32[]{:S(2)}) %collective-permute-start.7) | collective-permute-done | bytes 262176 | tf_op jit(solution)/shard_map/ppermute | solution.py:273
  56.7 1.5 %shard_map.114 = bf16[256,2176]{1,0:T(8,128)(2,1)} custom-call(bf16[128,2048]{1,0:T(8,128)(2,1)S(1)} %get-tuple-element.20.mix_own, bf16[64,2048]{1,0:T(8,128)(2,1)S(1)} %collective-permute-done.7.mix_a, bf16[64,2048]{1,0:T(8,128)(2,1)S(1)} %collective-permute-done.8.mix_b, bf16[128,128]{1,0:T(8,128)(2,1)S(1)} %get-tuple-element.26.gain_ext, ...), custom_call_target="tpu_custom_call" | custom-call | tf_op jit(solution)/shard_map/pallas_call | solution.py:344
  58.2 9.4 %all-to-all-start = ((bf16[32,8,2176]{2,1,0:T(8,128)(2,1)}), bf16[32,8,2176]{2,1,0:T(8,128)(2,1)S(1)}, u32[]{:S(2)}, u32[]{:S(2)}) async-start(bf16[32,8,2176]{2,1,0:T(8,128)(2,1)} %bitcast.11), calls=%async_computation | async-start | bytes 2228224 | tf_op jit(solution)/shard_map/all_to_all | solution.py:348
  67.7 17.7 %all-to-all-done.parts_ref = bf16[32,8,2176]{2,1,0:T(8,128)(2,1)S(1)} async-done(((bf16[32,8,2176]{2,1,0:T(8,128)(2,1)}), bf16[32,8,2176]{2,1,0:T(8,128)(2,1)S(1)}, u32[]{:S(2)}, u32[]{:S(2)}) %all-to-all-start) | async-done | bytes 1114144 | tf_op jit(solution)/shard_map/all_to_all | solution.py:348
  85.4 1.0 shard_map.115
  86.4 22.2 %all_to_all.10.all_ref = bf16[32,8,2176]{2,1,0:T(8,128)(2,1)S(1)} all-to-all(bf16[32,8,2176]{2,1,0:T(8,128)(2,1)S(1)} %shard_map.115), channel_id=1, replica_groups=mesh['section'=2,'expert'=2,'dp'=32] {'dp'}, dimensions={0} | all-to-all | bytes 2228224 | tf_op jit(solution)/shard_map/all_to_all | solution.py:375
  108.6 1.7 %shard_map.116 = (bf16[16,8,2048]{2,1,0:T(8,128)(2,1)}, bf16[16,8,2048]{2,1,0:T(8,128)(2,1)}, f32[16,2048]{1,0:T(8,128)S(1)}) custom-call(bf16[32,8,2176]{2,1,0:T(8,128)(2,1)S(1)} %all_to_all.10.all_ref, bf16[128,2048]{1,0:T(8,128)(2,1)S(1)} %bitcast.25, f32[128,128]{1,0:T(8,128)S(1)} %get-tuple-element.30.coef_ref), custom_call_target="tpu_custom_call" | custom-call | tf_op jit(solution)/shard_map/pallas_call | solution.py:377
  110.3 1.3 %collective-permute-done.11 = f32[16,2048]{1,0:T(8,128)S(1)} collective-permute-done((f32[16,2048]{1,0:T(8,128)S(1)}, f32[16,2048]{1,0:T(8,128)S(1)}, u32[]{:S(2)}, u32[]{:S(2)}) %collective-permute-start.11) | collective-permute-done | bytes 131104 | tf_op jit(solution)/shard_map/ppermute | solution.py:279
  111.7 2.2 %collective-permute-start.12 = (f32[16,2048]{1,0:T(8,128)S(1)}, f32[16,2048]{1,0:T(8,128)S(1)}, u32[]{:S(2)}, u32[]{:S(2)}) collective-permute-start(f32[16,2048]{1,0:T(8,128)S(1)} %add.14), channel_id=1, source_target_pairs={{0,32},{32,0},{1,33},{33,1},{2,34},{34,2},{3,35},{35,3},{4,36},{36... | collective-permute-start | bytes 393224 | tf_op jit(solution)/shard_map/ppermute | solution.py:282
  113.8 3.8 %collective-permute-done.12 = f32[16,2048]{1,0:T(8,128)S(1)} collective-permute-done((f32[16,2048]{1,0:T(8,128)S(1)}, f32[16,2048]{1,0:T(8,128)S(1)}, u32[]{:S(2)}, u32[]{:S(2)}) %collective-permute-start.12) | collective-permute-done | bytes 131104 | tf_op jit(solution)/shard_map/ppermute | solution.py:282
  117.7 0.6 multiply_reduce_fusion
  118.3 0.6 divide_add_fusion
  (37 shorter events, 0.5 us)
Async XLA Ops:
  0.6 23.7 %copy-start.2 = (bf16[2,64,2048]{2,1,0:T(8,128)(2,1)S(1)}, bf16[2,64,2048]{2,1,0:T(8,128)(2,1)}, u32[]{:S(2)}) copy-start(bf16[2,64,2048]{2,1,0:T(8,128)(2,1)} %param.9) | copy-start | bytes 1572868
  0.6 23.7 %collective-permute-start.6 = (bf16[4,224,1024]{2,1,0:T(8,128)(2,1)}, bf16[4,224,1024]{2,1,0:T(8,128)(2,1)}, u32[]{:S(2)}, u32[]{:S(2)}) collective-permute-start(bf16[4,224,1024]{2,1,0:T(8,128)(2,1)} %down_0.1), channel_id=1, source_target_pairs={{0,64},{64,0},{1,65},{65,1},{2,66},{66,2},{3,67},{67,3},{4,68},{68... | collective-permute-start | bytes 5505032 | tf_op jit(solution)/shard_map/ppermute | solution.py:279
  0.7 23.6 %collective-permute-start.4 = (bf16[4,224,1024]{2,1,0:T(8,128)(2,1)}, bf16[4,224,1024]{2,1,0:T(8,128)(2,1)}, u32[]{:S(2)}, u32[]{:S(2)}) collective-permute-start(bf16[4,224,1024]{2,1,0:T(8,128)(2,1)} %gate_0.3), channel_id=1, source_target_pairs={{0,64},{64,0},{1,65},{65,1},{2,66},{66,2},{3,67},{67,3},{4,68},{68... | collective-permute-start | bytes 5505032 | tf_op jit(solution)/shard_map/ppermute | solution.py:279
  1.2 23.1 %collective-permute-start.5 = (bf16[4,224,1024]{2,1,0:T(8,128)(2,1)}, bf16[4,224,1024]{2,1,0:T(8,128)(2,1)}, u32[]{:S(2)}, u32[]{:S(2)}) collective-permute-start(bf16[4,224,1024]{2,1,0:T(8,128)(2,1)} %up_0.3), channel_id=1, source_target_pairs={{0,64},{64,0},{1,65},{65,1},{2,66},{66,2},{3,67},{67,3},{4,68},{68... | collective-permute-start | bytes 5505032 | tf_op jit(solution)/shard_map/ppermute | solution.py:279
  2.4 9.1 %collective-permute-start.3 = (bf16[64,2048]{1,0:T(8,128)(2,1)S(1)}, bf16[64,2048]{1,0:T(8,128)(2,1)S(1)}, u32[]{:S(2)}, u32[]{:S(2)}) collective-permute-start(bf16[64,2048]{1,0:T(8,128)(2,1)S(1)} %get-tuple-element.36), channel_id=1, source_target_pairs={{0,33},{1,32},{2,35},{3,34},{4,37},{5,36},{6,39},{7,38},{8,41},{9,... | collective-permute-start | bytes 786440 | tf_op jit(solution)/shard_map/ppermute | solution.py:276
  5.3 9.9 %collective-permute-start.2 = (bf16[64,2048]{1,0:T(8,128)(2,1)S(1)}, bf16[64,2048]{1,0:T(8,128)(2,1)S(1)}, u32[]{:S(2)}, u32[]{:S(2)}) collective-permute-start(bf16[64,2048]{1,0:T(8,128)(2,1)S(1)} %get-tuple-element.37), channel_id=1, source_target_pairs={{0,32},{1,33},{2,34},{3,35},{4,36},{5,37},{6,38},{7,39},{8,40},{9,... | collective-permute-start | bytes 786440 | tf_op jit(solution)/shard_map/ppermute | solution.py:273
  6.1 1.0 copy-start
  7.1 0.8 copy-start.7
  8.0 0.7 copy-start.9
  11.5 9.4 %collective-permute-start.1 = (bf16[64,2176]{1,0:T(8,128)(2,1)S(1)}, bf16[64,2176]{1,0:T(8,128)(2,1)S(1)}, u32[]{:S(2)}, u32[]{:S(2)}) collective-permute-start(bf16[64,2176]{1,0:T(8,128)(2,1)S(1)} %get-tuple-element.34), channel_id=1, source_target_pairs={{0,33},{1,32},{2,35},{3,34},{4,37},{5,36},{6,39},{7,38},{8,41},{9,... | collective-permute-start | bytes 835592 | tf_op jit(solution)/shard_map/ppermute | solution.py:276
  15.2 9.1 %collective-permute-start = (bf16[64,2176]{1,0:T(8,128)(2,1)S(1)}, bf16[64,2176]{1,0:T(8,128)(2,1)S(1)}, u32[]{:S(2)}, u32[]{:S(2)}) collective-permute-start(bf16[64,2176]{1,0:T(8,128)(2,1)S(1)} %get-tuple-element.35), channel_id=1, source_target_pairs={{0,32},{1,33},{2,34},{3,35},{4,36},{5,37},{6,38},{7,39},{8,40},{9,... | collective-permute-start | bytes 835592 | tf_op jit(solution)/shard_map/ppermute | solution.py:273
  24.3 1.5 %copy-start.3 = (bf16[4,224,1024]{2,1,0:T(8,128)(2,1)S(1)}, bf16[4,224,1024]{2,1,0:T(8,128)(2,1)}, u32[]{:S(2)}) copy-start(bf16[4,224,1024]{2,1,0:T(8,128)(2,1)} %gate_0.3) | copy-start | bytes 5505028
  25.8 1.5 %copy-start.5 = (bf16[4,224,1024]{2,1,0:T(8,128)(2,1)S(1)}, bf16[4,224,1024]{2,1,0:T(8,128)(2,1)}, u32[]{:S(2)}) copy-start(bf16[4,224,1024]{2,1,0:T(8,128)(2,1)} %up_0.3) | copy-start | bytes 5505028
  27.3 1.5 %copy-start.11 = (bf16[4,224,1024]{2,1,0:T(8,128)(2,1)S(1)}, bf16[4,224,1024]{2,1,0:T(8,128)(2,1)}, u32[]{:S(2)}) copy-start(bf16[4,224,1024]{2,1,0:T(8,128)(2,1)} %down_0.1) | copy-start | bytes 5505028
  28.8 8.2 %copy-start.4 = (bf16[4,224,1024]{2,1,0:T(8,128)(2,1)S(1)}, bf16[4,224,1024]{2,1,0:T(8,128)(2,1)}, u32[]{:S(2)}) copy-start(bf16[4,224,1024]{2,1,0:T(8,128)(2,1)} %gate_0.3) | copy-start | bytes 5505028
  28.8 8.2 %copy-start.6 = (bf16[4,224,1024]{2,1,0:T(8,128)(2,1)S(1)}, bf16[4,224,1024]{2,1,0:T(8,128)(2,1)}, u32[]{:S(2)}) copy-start(bf16[4,224,1024]{2,1,0:T(8,128)(2,1)} %up_0.3) | copy-start | bytes 5505028
  42.8 13.9 %collective-permute-start.9 = (bf16[64,2176]{1,0:T(8,128)(2,1)S(1)}, bf16[64,2176]{1,0:T(8,128)(2,1)S(1)}, u32[]{:S(2)}, u32[]{:S(2)}) collective-permute-start(bf16[64,2176]{1,0:T(8,128)(2,1)S(1)} %get-tuple-element.28), channel_id=1, source_target_pairs={{0,32},{1,33},{2,34},{3,35},{4,36},{5,37},{6,38},{7,39},{8,40},{9,... | collective-permute-start | bytes 835592 | tf_op jit(solution)/shard_map/ppermute | solution.py:273
  42.9 13.8 %collective-permute-start.10 = (bf16[64,2176]{1,0:T(8,128)(2,1)S(1)}, bf16[64,2176]{1,0:T(8,128)(2,1)S(1)}, u32[]{:S(2)}, u32[]{:S(2)}) collective-permute-start(bf16[64,2176]{1,0:T(8,128)(2,1)S(1)} %get-tuple-element.29), channel_id=1, source_target_pairs={{0,33},{1,32},{2,35},{3,34},{4,37},{5,36},{6,39},{7,38},{8,41},{9,... | collective-permute-start | bytes 835592 | tf_op jit(solution)/shard_map/ppermute | solution.py:276
  46.1 10.6 %collective-permute-start.7 = (bf16[64,2048]{1,0:T(8,128)(2,1)S(1)}, bf16[64,2048]{1,0:T(8,128)(2,1)S(1)}, u32[]{:S(2)}, u32[]{:S(2)}) collective-permute-start(bf16[64,2048]{1,0:T(8,128)(2,1)S(1)} %get-tuple-element.21), channel_id=1, source_target_pairs={{0,32},{1,33},{2,34},{3,35},{4,36},{5,37},{6,38},{7,39},{8,40},{9,... | collective-permute-start | bytes 786440 | tf_op jit(solution)/shard_map/ppermute | solution.py:273
  46.1 10.6 %collective-permute-start.8 = (bf16[64,2048]{1,0:T(8,128)(2,1)S(1)}, bf16[64,2048]{1,0:T(8,128)(2,1)S(1)}, u32[]{:S(2)}, u32[]{:S(2)}) collective-permute-start(bf16[64,2048]{1,0:T(8,128)(2,1)S(1)} %get-tuple-element.22), channel_id=1, source_target_pairs={{0,33},{1,32},{2,35},{3,34},{4,37},{5,36},{6,39},{7,38},{8,41},{9,... | collective-permute-start | bytes 786440 | tf_op jit(solution)/shard_map/ppermute | solution.py:276
  58.2 27.1 %copy-start.1 = (bf16[2,64,2048]{2,1,0:T(8,128)(2,1)S(1)}, bf16[2,64,2048]{2,1,0:T(8,128)(2,1)}, u32[]{:S(2)}) copy-start(bf16[2,64,2048]{2,1,0:T(8,128)(2,1)} %param.8) | copy-start | bytes 1572868
  58.2 27.1 %copy-start.8 = (f32[2048,8]{0,1:T(8,128)S(1)}, f32[2048,8]{0,1:T(8,128)}, u32[]{:S(2)}) copy-start(f32[2048,8]{0,1:T(8,128)} %param.13) | copy-start | bytes 196612
  58.2 27.1 %copy-start.10 = (f32[2048]{0:T(1024)S(1)}, f32[2048]{0:T(1024)}, u32[]{:S(2)}) copy-start(f32[2048]{0:T(1024)} %param.14) | copy-start | bytes 24580
  58.2 27.1 %all-to-all-start = ((bf16[32,8,2176]{2,1,0:T(8,128)(2,1)}), bf16[32,8,2176]{2,1,0:T(8,128)(2,1)S(1)}, u32[]{:S(2)}, u32[]{:S(2)}) async-start(bf16[32,8,2176]{2,1,0:T(8,128)(2,1)} %bitcast.11), calls=%async_computation | async-start | bytes 2228224 | tf_op jit(solution)/shard_map/all_to_all | solution.py:348
  110.3 1.3 %collective-permute-start.11 = (f32[16,2048]{1,0:T(8,128)S(1)}, f32[16,2048]{1,0:T(8,128)S(1)}, u32[]{:S(2)}, u32[]{:S(2)}) collective-permute-start(f32[16,2048]{1,0:T(8,128)S(1)} %get-tuple-element.33), channel_id=1, source_target_pairs={{0,64},{64,0},{1,65},{65,1},{2,66},{66,2},{3,67},{67,3},{4,68},{68... | collective-permute-start | bytes 393224 | tf_op jit(solution)/shard_map/ppermute | solution.py:279
  111.7 6.0 %collective-permute-start.12 = (f32[16,2048]{1,0:T(8,128)S(1)}, f32[16,2048]{1,0:T(8,128)S(1)}, u32[]{:S(2)}, u32[]{:S(2)}) collective-permute-start(f32[16,2048]{1,0:T(8,128)S(1)} %add.14), channel_id=1, source_target_pairs={{0,32},{32,0},{1,33},{33,1},{2,34},{34,2},{3,35},{35,3},{4,36},{36... | collective-permute-start | bytes 393224 | tf_op jit(solution)/shard_map/ppermute | solution.py:282

commit v2 on v1

v2 whole, which is shorter than its diff:
```python
import functools

import jax
import jax.numpy as jnp
from jax import lax
from jax.experimental import pallas as pl
from jax.experimental.pallas import tpu as pltpu
from jax.sharding import PartitionSpec as P

EPSILON = 1e-05
EXT = 128
F32 = jnp.float32
BF16 = jnp.bfloat16
HIGHEST = lax.Precision.HIGHEST
NT = (((1,), (1,)), ((), ()))
VMEM_BYTES = 16 * 1024 * 1024
EXPERT_VMEM = 60 * 1024 * 1024
TILE = 256


def params(limit=VMEM_BYTES):
    return pltpu.CompilerParams(vmem_limit_bytes=limit)


def lanes(rows):
    return lax.broadcasted_iota(jnp.int32, (rows, EXT), 1)


def split_low(value):
    high = value.astype(BF16).astype(F32)
    return high, value - high


def inverse_rms(wide):
    return lax.rsqrt(jnp.mean(wide * wide, axis=-1, keepdims=True) + EPSILON)


def prologue_kernel(x_ref, gain_ref, router_ref, routes_ref, rows_ref, extra_ref, coef_ref):
    count = router_ref.shape[0]
    wide = x_ref[...].astype(F32)
    normed = wide * inverse_rms(wide) * gain_ref[...]
    rows_ref[...] = normed.astype(BF16)
    logits = lax.dot_general(normed, router_ref[...], NT, precision=HIGHEST, preferred_element_type=F32)
    first, second = routes_ref[:, 0:1], routes_ref[:, 1:2]
    column = lax.broadcasted_iota(jnp.int32, logits.shape, 1)
    signs = (column == first).astype(F32) - (column == second).astype(F32)
    leading = jax.nn.sigmoid(jnp.sum(signs * logits, axis=1, keepdims=True))
    trailing = 1.0 - leading
    lead_high, lead_low = split_low(leading)
    trail_high, trail_low = split_low(trailing)
    lane = lanes(x_ref.shape[0])

    def place(start, at_first, at_second):
        return jnp.where(lane == first + start, at_first, 0.0) + jnp.where(
            lane == second + start, at_second, 0.0
        )

    extra = (
        place(0, lead_high, trail_high)
        + place(count, lead_low, trail_low)
        + place(2 * count, 1.0, -1.0)
    )
    extra_ref[...] = extra.astype(BF16)
    slope = leading * trailing
    coef_ref[...] = place(0, slope, -slope)


def tiles_of(extent, size):
    return [(start, min(size, extent - start)) for start in range(0, extent, size)]

def expert_kernel(
    count, units, tile, fresh,
    meta, rows_ref, cot_ref, extra_ref, side_ref, gate_0, gate_1, up_0, up_1, down_0, down_1,
    mix_ref, grad_ref, params_ref,
    g_0, g_1, u_0, u_1, d_0, d_1, r_0, r_1, c_0, c_1, hid, dgate, dup, sems,
):
    hidden_units, half = gate_0.shape
    total = rows_ref.shape[0]
    width = 2 * half
    local = hidden_units // units
    at_0 = pl.multiple_of(meta[0] * half, half)
    at_1 = pl.multiple_of((1 - meta[0]) * half, half)
    tiles = tiles_of(hidden_units, tile)
    copies = []
    for number, (start, size) in enumerate(tiles):
        group = []
        for which, (source, target) in enumerate(
            ((gate_0, g_0), (gate_1, g_1), (up_0, u_0), (up_1, u_1), (down_0, d_0), (down_1, d_1))
        ):
            copy = pltpu.make_async_copy(
                source.at[pl.ds(start, size), :], target.at[pl.ds(start, size), :], sems.at[number, which]
            )
            copy.start()
            group.append(copy)
        copies.append(group)

    scaling = inverse_rms(rows_ref[...].astype(F32)) if fresh else None
    for at, r, c in ((at_0, r_0, c_0), (at_1, r_1, c_1)):
        rows = rows_ref[:, pl.ds(at, half)]
        if fresh:
            rows = (rows.astype(F32) * scaling * side_ref[:, pl.ds(at, half)]).astype(BF16)
        r[...] = rows
        c[...] = cot_ref[:, pl.ds(at, half)]

    lane = lanes(total)
    extra = extra_ref[...].astype(F32)
    weights, signs = [], []
    for which in range(local):
        expert = meta[1] * local + which
        weights.append(
            jnp.sum(jnp.where((lane == expert) | (lane == expert + count), extra, 0.0), axis=1, keepdims=True)
        )
        signs.append(jnp.sum(jnp.where(lane == expert + 2 * count, extra, 0.0), axis=1, keepdims=True))

    sums = jnp.zeros((total, 1), F32)
    for group, (start, size) in zip(copies, tiles):
        for copy in group:
            copy.wait()
        span = slice(start, start + size)

        def both(left_0, left_1, map_0, map_1):
            return lax.dot_general(left_0[...], map_0[span, :], NT, preferred_element_type=F32) + lax.dot_general(
                left_1[...], map_1[span, :], NT, preferred_element_type=F32
            )

        pre_gate = both(r_0, r_1, g_0, g_1)
        pre_up = both(r_0, r_1, u_0, u_1)
        dhid = both(c_0, c_1, d_0, d_1)
        column = lax.broadcasted_iota(jnp.int32, (total, size), 1) + start
        first = start // units
        weight, sign = weights[first], signs[first]
        for later in range(first + 1, (start + size - 1) // units + 1):
            weight = jnp.where(column < later * units, weight, weights[later])
            sign = jnp.where(column < later * units, sign, signs[later])
        squash = jax.nn.sigmoid(pre_gate)
        act = pre_gate * squash
        hidden = act * pre_up
        sums = sums + jnp.sum(hidden * dhid * sign, axis=1, keepdims=True)
        dhid = dhid * weight
        dgate[:, span] = (dhid * pre_up * (squash + act * (1.0 - squash))).astype(BF16)
        dup[:, span] = (dhid * act).astype(BF16)
        hid[:, span] = (hidden * weight).astype(BF16)

    high, low = split_low(sums)
    grad_ref[:, width:] = jnp.where(lane == 0, high, jnp.where(lane == 1, low, 0.0)).astype(BF16)
    share = jnp.where(lane < count, extra + pltpu.roll(extra, EXT - count, 1), 0.0)
    dlogits = share * (1.0 - share) * pltpu.roll(extra, EXT - 2 * count, 1) * sums
    high, low = split_low(dlogits)
    sides = jnp.concatenate([high.T[:count], low.T[:count]], axis=0).astype(BF16)
    for at, g, u, d, r in ((at_0, g_0, u_0, d_0, r_0), (at_1, g_1, u_1, d_1, r_1)):
        there = pl.ds(at, half)
        mix_ref[:, there] = jnp.dot(hid[...], d[...], preferred_element_type=F32).astype(BF16)
        grad = jnp.dot(dgate[...], g[...], preferred_element_type=F32) + jnp.dot(
            dup[...], u[...], preferred_element_type=F32
        )
        grad_ref[:, there] = grad.astype(BF16)
        routing = jnp.dot(sides, r[...], preferred_element_type=F32)
        routing = routing[:count] + routing[count:]
        moved = jnp.sum(grad * r[...].astype(F32), axis=0, keepdims=True)
        moved = jnp.broadcast_to(moved, routing.shape)
        if not fresh:
            routing = routing + side_ref[:count, there]
            moved = moved + side_ref[count:, there]
        params_ref[:count, there] = routing
        params_ref[count:, there] = moved


def pack_kernel(mix_own, mix_in, grad_own, grad_in, sums_own, sums_core, sums_across, sums_diagonal, out_ref):
    own, width = mix_own.shape
    out_ref[:own, :width] = (mix_own[...].astype(F32) + mix_in[...].astype(F32)).astype(BF16)
    out_ref[own:, :width] = (grad_own[:, :width].astype(F32) + grad_in[:, :width].astype(F32)).astype(BF16)
    both = grad_own[:, width:].astype(F32) + grad_in[:, width:].astype(F32)
    high, low = split_low(jnp.sum(both, axis=1, keepdims=True))
    lane = lanes(own)
    gate_sums = jnp.where(lane == 0, high, jnp.where(lane == 1, low, 0.0))
    totals = (sums_own[...] + sums_core[...]) + (sums_across[...] + sums_diagonal[...])
    upper, row = lanes(8) >= EXT // 2, lax.broadcasted_iota(jnp.int32, (8, EXT), 0)
    for pair in range(own // 16):
        routing, ends = [], []
        for place in (2 * pair, 2 * pair + 1):
            part = totals[:, place * EXT:(place + 1) * EXT]
            routing.append(part[:8])
            moved = jnp.where(row == 0, part[8:], jnp.where(row == 1, pltpu.roll(part[8:], EXT // 2, 1), 0.0))
            ends.append(jnp.where(upper, moved, gate_sums[8 * place:8 * place + 8]))
        span = slice(16 * pair, 16 * pair + 16)
        out_ref[span, width:] = jnp.concatenate(routing, axis=0).astype(BF16)
        out_ref[own + 16 * pair:own + 16 * pair + 16, width:] = jnp.concatenate(ends, axis=0).astype(BF16)


def finish_kernel(meta, parts_ref, x_ref, cot_ref, coef_ref, gain_ref, router_ref, out_ref):
    chunks = parts_ref.shape[0]
    width = x_ref.shape[2]
    total = parts_ref[0].astype(F32)
    for source in range(1, chunks):
        total = total + parts_ref[source].astype(F32)
    wide = x_ref[0].astype(F32)
    summed, extra = total[:, :width], total[:, width:]
    layer = wide + summed
    dlogits = coef_ref[0] * (extra[:, 0:1] + extra[:, 1:2])
    dnormed = summed
    for expert in range(router_ref.shape[0]):
        dnormed = dnormed + dlogits[:, expert:expert + 1] * router_ref[expert:expert + 1, :]
    scaling = inverse_rms(wide)
    unit = wide * scaling
    dunit = dnormed * gain_ref[...]
    dx = scaling * (dunit - unit * jnp.mean(dunit * unit, axis=-1, keepdims=True))
    grad = cot_ref[0].astype(F32) + dx
    out = jnp.where(meta[0] < chunks // 2, layer, grad).astype(BF16)
    ends = extra.astype(BF16)
    for place in range(chunks):
        out_ref[place, :, :width] = out
        out_ref[place, :, width:] = ends


def tail_kernel(all_ref, gain_ref, router_ref, layer_ref, grad_ref, grad_router_ref, grad_gain_ref):
    mid = all_ref.shape[0] // 2
    count, width = router_ref.shape
    layer_ref[...] = all_ref[:mid, :, :width]
    grad_ref[...] = all_ref[mid:, :, :width]
    upper = lanes(1) >= EXT // 2
    for place in range(mid):
        span = slice(place * EXT, (place + 1) * EXT)
        routing = all_ref[place, :, width:].astype(F32)
        ends = all_ref[mid + place, :, width:].astype(F32)
        moved = jnp.where(upper, ends[0:1], pltpu.roll(ends[1:2], EXT // 2, 1))
        grad_router_ref[:, span] = routing
        shares = jnp.sum(router_ref[:, span] * routing, axis=0, keepdims=True)
        grad_gain_ref[:, span] = (moved + shares) / gain_ref[:, span]


def whole(array):
    return pl.BlockSpec(array.shape, lambda *_: (0,) * len(array.shape))


def struct(*shape, dtype=BF16):
    return jax.ShapeDtypeStruct(shape, dtype)


def shards(n_dp, inputs, cotangent, w_gate, w_up, w_down, router, norm_gain, routes):
    micro, sub, width = inputs.shape
    own = micro * sub
    local, units, half = w_gate.shape
    count = router.shape[1]
    section, expert = lax.axis_index("section"), lax.axis_index("expert")
    place = lax.axis_index("dp")
    meta = jnp.stack([section, expert]).astype(jnp.int32)

    def around(shift):
        pairs = []
        for e in range(2):
            for d in range(n_dp):
                x = (d % 2 * 2 + e + shift) % 4
                pairs.append((e * n_dp + d, (x % 2) * n_dp + d - d % 2 + x // 2))
        return pairs

    def up_x(array):
        return lax.ppermute(array, ("expert", "dp"), around(1))

    def down_x(array):
        return lax.ppermute(array, ("expert", "dp"), around(3))

    def other_core(array):
        return lax.ppermute(array, "section", [(0, 1), (1, 0)])

    flat_x = inputs.reshape(own, width)
    flat_cot = cotangent.reshape(own, width)
    x_other, cot_other = up_x(flat_x), down_x(flat_cot)
    gate_0, up_0, down_0 = (w.reshape(local * units, half) for w in (w_gate, w_up, w_down))
    gate_1 = other_core(gate_0)
    up_1 = other_core(up_0)
    down_late, gate_1 = lax.optimization_barrier((down_0, gate_1))
    down_1 = other_core(down_late)
    maps = (gate_0, gate_1, up_0, up_1, down_0, down_1)
    gain_row = norm_gain.reshape(1, width)
    router_rows = router.T
    rows_own, extra_own, coef = pl.pallas_call(
        prologue_kernel,
        out_shape=(struct(own, width), struct(own, EXT), struct(own, EXT, dtype=F32)),
        compiler_params=params(),
        cost_estimate=pl.CostEstimate(flops=20_000_000_000, bytes_accessed=2**25, transcendentals=0),
    )(flat_x, gain_row, router_rows, routes.reshape(own, 2))
    extra_other = up_x(extra_own)

    hidden_units = local * units
    near = pl.BlockSpec(memory_space=pltpu.VMEM)
    far = pl.BlockSpec(memory_space=pltpu.HBM)
    sums_shape = struct(2 * count, width, dtype=F32)

    def experts(fresh, rows, cot, extra, side):
        return pl.pallas_call(
            functools.partial(expert_kernel, count, units, TILE, fresh),
            in_specs=[pl.BlockSpec(memory_space=pltpu.SMEM)] + [near] * 4 + [far] * 6,
            out_specs=(near, near, near),
            out_shape=(struct(own, width), struct(own, width + EXT), sums_shape),
            scratch_shapes=[pltpu.VMEM((hidden_units, half), BF16)] * 6
            + [pltpu.VMEM((own, half), BF16)] * 4
            + [pltpu.VMEM((own, hidden_units), BF16)] * 3
            + [pltpu.SemaphoreType.DMA((len(tiles_of(hidden_units, TILE)), 6))],
            compiler_params=params(EXPERT_VMEM),
            cost_estimate=pl.CostEstimate(
                flops=24 * own * hidden_units * half, bytes_accessed=12 * hidden_units * half, transcendentals=0
            ),
        )(meta, rows, cot, extra, side, *maps)

    mix_away, grad_away, sums = experts(True, x_other, cot_other, extra_other, gain_row)
    mix_in, grad_in = up_x(mix_away), down_x(grad_away)
    mix_own, grad_own, sums = experts(False, rows_own, flat_cot, extra_own, sums)
    core = other_core(sums)
    across = lax.ppermute(sums, "expert", [(0, 1), (1, 0)])
    diagonal = lax.ppermute(sums, ("section", "expert"), [(0, 3), (1, 2), (2, 1), (3, 0)])
    packed = pl.pallas_call(pack_kernel, out_shape=struct(2 * own, width + EXT), compiler_params=params())(
        mix_own, mix_in, grad_own, grad_in, sums, core, across, diagonal
    )
    rows_each = 2 * own // n_dp
    chunks = lax.all_to_all(packed.reshape(n_dp, rows_each, width + EXT), "dp", 0, 0, tiled=True)

    blocks = own // rows_each
    spot = jnp.stack([place, place % blocks]).astype(jnp.int32)

    def at_spot(last):
        return pl.BlockSpec((1, rows_each, last), lambda i, m: (m[1], 0, 0))

    finished = pl.pallas_call(
        finish_kernel,
        grid_spec=pltpu.PrefetchScalarGridSpec(
            num_scalar_prefetch=1,
            grid=(1,),
            in_specs=[whole(chunks), at_spot(width), at_spot(width), at_spot(EXT), whole(gain_row), whole(router_rows)],
            out_specs=whole(chunks),
        ),
        out_shape=struct(*chunks.shape),
        compiler_params=params(),
    )(
        spot,
        chunks,
        inputs.reshape(blocks, rows_each, width),
        cotangent.reshape(blocks, rows_each, width),
        coef.reshape(blocks, rows_each, EXT),
        gain_row,
        router_rows,
    )
    gathered = lax.all_to_all(finished, "dp", 0, 0, tiled=True)

    layer, grad, grad_router, grad_gain = pl.pallas_call(
        tail_kernel,
        out_shape=(
            struct(blocks, rows_each, width), struct(blocks, rows_each, width),
            struct(count, width, dtype=F32), struct(1, width, dtype=F32),
        ),
        compiler_params=params(),
    )(gathered, gain_row, router_rows)
    return (
        layer.reshape(micro, sub, width), grad.reshape(micro, sub, width), grad_router.T, grad_gain.reshape(width)
    )


def solution(mesh):
    tokens = P(None, ("section", "expert"), None)
    maps = P("expert", "dp", "section")
    return jax.shard_map(
        functools.partial(shards, mesh.shape["dp"]),
        mesh=mesh,
        in_specs=(tokens, tokens, maps, maps, maps, P(), P(), tokens),
        out_specs=(tokens, tokens, P(), P()),
        check_vma=False,
    )
```

time: 120 us -> 112 us (0.933)
  waiting for transfers between devices: 40.8 us -> 29.9 us
  Pallas kernels: 19.4 us -> 27.2 us
  starting transfers between devices: 25.3 us -> 20.9 us
    ppermute x4 -> x2, starting transfers between devices: 13.1 us -> 3.8 us  [down_x(): return lax.ppermute(array, ('expert', 'dp'), around(3))]
    pallas_call x4, Pallas kernels: 16.7 us -> 25.1 us  [the longest x2 22.3 us: experts(): pl.pallas_call(functools.partial(expert_kernel, count, units, TILE, fresh...]
    ppermute x4 -> x2, waiting for transfers between devices: 7.16 us -> 0.01 us  [down_x(): return lax.ppermute(array, ('expert', 'dp'), around(3))]
    ppermute x4 -> x3, waiting for transfers between devices: 10.8 us -> 4.45 us  [up_x(): return lax.ppermute(array, ('expert', 'dp'), around(1))]
    ppermute x4 -> x3, starting transfers between devices: 0.08 us -> 3.1 us  [up_x(): return lax.ppermute(array, ('expert', 'dp'), around(1))]
    all_to_all x1, waiting for transfers between devices: 17.7 us -> 20 us  [shards(): lax.all_to_all(packed.reshape(n_dp, rows_each, width + EXT), 'dp', 0, 0,...]
    all_to_all x1, starting transfers between devices: 9.36 us -> 11.3 us  [shards(): lax.all_to_all(packed.reshape(n_dp, rows_each, width + EXT), 'dp', 0, 0,...]
    ppermute x1 -> x2, waiting for transfers between devices: 3.81 us -> 5.45 us  [the longest x1 4.11 us: shards(): lax.ppermute(sums, ('section', 'expert'), [(0, 3), (1, 2), (2, 1), (3, 0)])]
  transfers between devices with their start and end apart: 14 -> 12, of which waited for: 7 -> 4; matrix products, arithmetic and copies ran while one was open for 2% -> 1% of each run, Pallas kernels for 1% -> 11%
where the time goes in v2:
time: 112 us; the launch traced here: 111 us
  waiting for transfers between devices  29.9 us (27%)
  Pallas kernels  27.2 us (24%)
  blocking collectives  22.4 us (20%)
  starting transfers between devices  20.9 us (19%)
  local copies, waits for them, and re-layouts  8.75 us (8%)
    all_to_all x1, blocking collectives, shards(): gathered = lax.all_to_all(finished, 'dp', 0, 0, tiled=True)  22.4 us
    pallas_call x2, Pallas kernels, experts(): pl.pallas_call(functools.partial(expert_kernel, count, units, TILE, fresh...  22.3 us
    all_to_all x1, waiting for transfers between devices, shards(): lax.all_to_all(packed.reshape(n_dp, rows_each, width + EXT), 'dp', 0, 0,...  20 us
    all_to_all x1, starting transfers between devices, shards(): lax.all_to_all(packed.reshape(n_dp, rows_each, width + EXT), 'dp', 0, 0,...  11.3 us
    unnamed x33, local copies, waits for them, and re-layouts  8.75 us
    ppermute x3, waiting for transfers between devices, up_x(): return lax.ppermute(array, ('expert', 'dp'), around(1))  4.45 us
    ppermute x1, waiting for transfers between devices, shards(): lax.ppermute(sums, ('section', 'expert'), [(0, 3), (1, 2), (2, 1), (3, 0)])  4.11 us
    ppermute x2, starting transfers between devices, down_x(): return lax.ppermute(array, ('expert', 'dp'), around(3))  3.8 us
  transfers between devices with their start and end apart: 12, of which 4 were waited for; matrix products, arithmetic and copies ran while one was open for 1% of the time, Pallas kernels for 11%

profile of v2, /device:TPU:0, one launch (start us, length us, event | category | flops | bytes accessed | tf_op | source)
XLA Modules:
  0.0 110.7 jit_solution(15692536785547654445)
XLA Ops:
  0.7 1.6 %collective-permute-start = (bf16[128,2048]{1,0:T(8,128)(2,1)}, bf16[128,2048]{1,0:T(8,128)(2,1)S(1)}, u32[]{:S(2)}, u32[]{:S(2)}) collective-permute-start(bf16[128,2048]{1,0:T(8,128)(2,1)} %bitcast.23), channel_id=1, source_target_pairs={{0,32},{1,33},{2,34},{3,35},{4,36},{5,37},{6,38},{7,39},{8,40},{9,... | collective-permute-start | bytes 1572872 | tf_op jit(solution)/shard_map/ppermute | solution.py:257
  2.4 1.7 %collective-permute-start.1 = (bf16[128,2048]{1,0:T(8,128)(2,1)}, bf16[128,2048]{1,0:T(8,128)(2,1)S(1)}, u32[]{:S(2)}, u32[]{:S(2)}) collective-permute-start(bf16[128,2048]{1,0:T(8,128)(2,1)} %bitcast.20), channel_id=1, source_target_pairs={{0,33},{1,32},{2,35},{3,34},{4,37},{5,36},{6,39},{7,38},{8,41},{9,... | collective-permute-start | bytes 1572872 | tf_op jit(solution)/shard_map/ppermute | solution.py:260
  4.0 0.8 copy.12
  4.8 0.6 collective-permute-start.5
  5.4 0.7 copy-done.12
  6.1 1.0 copy-done.3
  7.1 0.8 copy-done.6
  8.0 0.7 copy-done.9
  8.7 1.2 %shard_map.111 = (bf16[128,2048]{1,0:T(8,128)(2,1)S(1)}, bf16[128,128]{1,0:T(8,128)(2,1)S(1)}, f32[128,128]{1,0:T(8,128)S(1)}) custom-call(bf16[128,2048]{1,0:T(8,128)(2,1)S(1)} %bitcast.24, f32[1,2048]{1,0:T(1,128)S(1)} %bitcast.30, f32[8,2048]{1,0:T(8,128)S(1)} %bitcast.26, s32[128,2]{1,0:T(8,128)S(1)} %bitcast.34), custom_call_target="tpu_custom_call" | custom-call | flops 20000000000 | bytes 33554432 | tf_op jit(solution)/shard_map/pallas_call | solution.py:276
  9.9 0.8 copy-done.2
  10.7 1.5 %collective-permute-start.2 = (bf16[128,128]{1,0:T(8,128)(2,1)S(1)}, bf16[128,128]{1,0:T(8,128)(2,1)S(1)}, u32[]{:S(2)}, u32[]{:S(2)}) collective-permute-start(bf16[128,128]{1,0:T(8,128)(2,1)S(1)} %get-tuple-element.20.extra_ref), channel_id=1, source_target_pairs={{0,32},{1,33},{2,34},{3,35},{4,36},{5,37},{6,38},{7,39},{8,40},{9,... | collective-permute-start | bytes 98312 | tf_op jit(solution)/shard_map/ppermute | solution.py:257
  12.1 0.6 pad_add_fusion.1.meta
  12.7 4.4 %collective-permute-done.2.extra_ref = bf16[128,128]{1,0:T(8,128)(2,1)S(1)} collective-permute-done((bf16[128,128]{1,0:T(8,128)(2,1)S(1)}, bf16[128,128]{1,0:T(8,128)(2,1)S(1)}, u32[]{:S(2)}, u32[]{:S(2)}) %collective-permute-start.2) | collective-permute-done | bytes 32800 | tf_op jit(solution)/shard_map/ppermute | solution.py:257
  17.2 0.6 copy-done.15
  17.8 0.2 copy-done.13
  18.0 0.2 copy-done.14
  18.2 11.2 %shard_map.112 = (bf16[128,2048]{1,0:T(8,128)(2,1)}, bf16[128,2176]{1,0:T(8,128)(2,1)}, f32[16,2048]{1,0:T(8,128)}) custom-call(s32[2]{0:T(128)} %pad_add_fusion.1.meta, bf16[128,2048]{1,0:T(8,128)(2,1)} %copy-done.13, bf16[128,2048]{1,0:T(8,128)(2,1)} %copy-done.14, bf16[128,128]{1,0:T(8,128)(2,1)} %copy-done.15, f32[1,2048]{1,0:T(1,128)} %bitcast.29, ...), custom_call_target="tpu_custom_call" | custom-call | flops 2818572288 | bytes 11010048 | tf_op jit(solution)/shard_map/pallas_call | solution.py:290
  29.4 2.1 %collective-permute-start.7 = (bf16[128,2176]{1,0:T(8,128)(2,1)}, bf16[128,2176]{1,0:T(8,128)(2,1)S(1)}, u32[]{:S(2)}, u32[]{:S(2)}) collective-permute-start(bf16[128,2176]{1,0:T(8,128)(2,1)} %get-tuple-element.27), channel_id=1, source_target_pairs={{0,33},{1,32},{2,35},{3,34},{4,37},{5,36},{6,39},{7,38},{8,41},{9,... | collective-permute-start | bytes 1671176 | tf_op jit(solution)/shard_map/ppermute | solution.py:260
  31.6 11.1 %shard_map.113 = (bf16[128,2048]{1,0:T(8,128)(2,1)}, bf16[128,2176]{1,0:T(8,128)(2,1)}, f32[16,2048]{1,0:T(8,128)}) custom-call(s32[2]{0:T(128)} %pad_add_fusion.1.meta, bf16[128,2048]{1,0:T(8,128)(2,1)} %copy-done.2, bf16[128,2048]{1,0:T(8,128)(2,1)} %bitcast.21, bf16[128,128]{1,0:T(8,128)(2,1)} %copy-done.11, f32[16,2048]{1,0:T(8,128)} %get-tuple-element.23.side_ref, ...), custom_call_target="tpu_custom_call" | custom-call | flops 2818572288 | bytes 11010048 | tf_op jit(solution)/shard_map/pallas_call | solution.py:290
  42.8 0.7 collective-permute-start.9
  43.5 1.1 %collective-permute-start.8 = (f32[16,2048]{1,0:T(8,128)}, f32[16,2048]{1,0:T(8,128)S(1)}, u32[]{:S(2)}, u32[]{:S(2)}) collective-permute-start(f32[16,2048]{1,0:T(8,128)} %get-tuple-element.28.sums_own), channel_id=1, source_target_pairs={{0,64},{64,0},{1,65},{65,1},{2,66},{66,2},{3,67},{67,3},{4,68},{68... | collective-permute-start | bytes 393224 | tf_op jit(solution)/shard_map/ppermute | solution.py:263
  44.6 4.1 %collective-permute-done.10.sums_diagonal = f32[16,2048]{1,0:T(8,128)S(1)} collective-permute-done((f32[16,2048]{1,0:T(8,128)}, f32[16,2048]{1,0:T(8,128)S(1)}, u32[]{:S(2)}, u32[]{:S(2)}) %collective-permute-start.10) | collective-permute-done | bytes 131104 | tf_op jit(solution)/shard_map/ppermute | solution.py:310
  48.7 1.3 %collective-permute-done.9.sums_across = f32[16,2048]{1,0:T(8,128)S(1)} collective-permute-done((f32[16,2048]{1,0:T(8,128)}, f32[16,2048]{1,0:T(8,128)S(1)}, u32[]{:S(2)}, u32[]{:S(2)}) %collective-permute-start.9) | collective-permute-done | bytes 131104 | tf_op jit(solution)/shard_map/ppermute | solution.py:309
  50.1 1.0 copy-done.1
  51.1 1.0 copy-done.5
  52.2 0.9 copy-done.8
  53.1 1.6 %shard_map.114 = bf16[256,2176]{1,0:T(8,128)(2,1)} custom-call(bf16[128,2048]{1,0:T(8,128)(2,1)S(1)} %copy-done.5, bf16[128,2048]{1,0:T(8,128)(2,1)S(1)} %collective-permute-done.6.mix_in, bf16[128,2176]{1,0:T(8,128)(2,1)S(1)} %copy-done.1, bf16[128,2176]{1,0:T(8,128)(2,1)S(1)} %collective-permute-done.7.grad_in, f32[16,2048]{1,0:T(8,128)S(1)} %copy-done.8, ...), custom_call_target="tpu_custom_call" | custom-call | tf_op jit(solution)/shard_map/pallas_call | solution.py:311
  54.7 11.3 %all-to-all-start = ((bf16[32,8,2176]{2,1,0:T(8,128)(2,1)}), bf16[32,8,2176]{2,1,0:T(8,128)(2,1)S(1)}, u32[]{:S(2)}, u32[]{:S(2)}) async-start(bf16[32,8,2176]{2,1,0:T(8,128)(2,1)} %bitcast.12), calls=%async_computation | async-start | bytes 2228224 | tf_op jit(solution)/shard_map/all_to_all | solution.py:315
  66.1 20.0 %all-to-all-done.parts_ref = bf16[32,8,2176]{2,1,0:T(8,128)(2,1)S(1)} async-done(((bf16[32,8,2176]{2,1,0:T(8,128)(2,1)}), bf16[32,8,2176]{2,1,0:T(8,128)(2,1)S(1)}, u32[]{:S(2)}, u32[]{:S(2)}) %all-to-all-start) | async-done | bytes 1114144 | tf_op jit(solution)/shard_map/all_to_all | solution.py:315
  86.2 1.0 shard_map.115
  87.2 22.4 %all_to_all.10.all_ref = bf16[32,8,2176]{2,1,0:T(8,128)(2,1)S(1)} all-to-all(bf16[32,8,2176]{2,1,0:T(8,128)(2,1)S(1)} %shard_map.115), channel_id=1, replica_groups=mesh['section'=2,'expert'=2,'dp'=32] {'dp'}, dimensions={0} | all-to-all | bytes 2228224 | tf_op jit(solution)/shard_map/all_to_all | solution.py:342
  109.6 1.0 shard_map.116
  (34 shorter events, 0.3 us)
Async XLA Ops:
  0.6 4.2 %collective-permute-start.3 = (bf16[896,1024]{1,0:T(8,128)(2,1)}, bf16[896,1024]{1,0:T(8,128)(2,1)S(1)}, u32[]{:S(2)}, u32[]{:S(2)}) collective-permute-start(bf16[896,1024]{1,0:T(8,128)(2,1)} %bitcast.35), channel_id=1, source_target_pairs={{0,64},{64,0},{1,65},{65,1},{2,66},{66,2},{3,67},{67,3},{4,68},{68... | collective-permute-start | bytes 5505032 | tf_op jit(solution)/shard_map/ppermute | solution.py:263
  0.7 16.5 %collective-permute-start = (bf16[128,2048]{1,0:T(8,128)(2,1)}, bf16[128,2048]{1,0:T(8,128)(2,1)S(1)}, u32[]{:S(2)}, u32[]{:S(2)}) collective-permute-start(bf16[128,2048]{1,0:T(8,128)(2,1)} %bitcast.23), channel_id=1, source_target_pairs={{0,32},{1,33},{2,34},{3,35},{4,36},{5,37},{6,38},{7,39},{8,40},{9,... | collective-permute-start | bytes 1572872 | tf_op jit(solution)/shard_map/ppermute | solution.py:257
  2.4 14.8 %collective-permute-start.1 = (bf16[128,2048]{1,0:T(8,128)(2,1)}, bf16[128,2048]{1,0:T(8,128)(2,1)S(1)}, u32[]{:S(2)}, u32[]{:S(2)}) collective-permute-start(bf16[128,2048]{1,0:T(8,128)(2,1)} %bitcast.20), channel_id=1, source_target_pairs={{0,33},{1,32},{2,35},{3,34},{4,37},{5,36},{6,39},{7,38},{8,41},{9,... | collective-permute-start | bytes 1572872 | tf_op jit(solution)/shard_map/ppermute | solution.py:260
  4.0 13.2 %collective-permute-start.4 = (bf16[896,1024]{1,0:T(8,128)(2,1)}, bf16[896,1024]{1,0:T(8,128)(2,1)}, u32[]{:S(2)}, u32[]{:S(2)}) collective-permute-start(bf16[896,1024]{1,0:T(8,128)(2,1)} %bitcast.38), channel_id=1, source_target_pairs={{0,64},{64,0},{1,65},{65,1},{2,66},{66,2},{3,67},{67,3},{4,68},{68... | collective-permute-start | bytes 5505032 | tf_op jit(solution)/shard_map/ppermute | solution.py:263
  4.8 1.3 %copy-start.12 = (bf16[896,1024]{1,0:T(8,128)(2,1)}, bf16[896,1024]{1,0:T(8,128)(2,1)S(1)}, u32[]{:S(2)}) copy-start(bf16[896,1024]{1,0:T(8,128)(2,1)S(1)} %collective-permute-done.3.gate_1) | copy-start | bytes 5505028
  4.8 12.4 %collective-permute-start.5 = (bf16[896,1024]{1,0:T(8,128)(2,1)}, bf16[896,1024]{1,0:T(8,128)(2,1)}, u32[]{:S(2)}, u32[]{:S(2)}) collective-permute-start(bf16[896,1024]{1,0:T(8,128)(2,1)} %bitcast.41), channel_id=1, source_target_pairs={{0,64},{64,0},{1,65},{65,1},{2,66},{66,2},{3,67},{67,3},{4,68},{68... | collective-permute-start | bytes 5505032 | tf_op jit(solution)/shard_map/ppermute | solution.py:263
  6.1 1.0 copy-start.3
  7.1 0.8 copy-start.6
  8.0 0.7 copy-start.9
  9.9 0.8 copy-start.2
  10.7 18.7 %copy-start.11 = (bf16[128,128]{1,0:T(8,128)(2,1)}, bf16[128,128]{1,0:T(8,128)(2,1)S(1)}, u32[]{:S(2)}) copy-start(bf16[128,128]{1,0:T(8,128)(2,1)S(1)} %get-tuple-element.20.extra_ref) | copy-start | bytes 98308
  10.7 6.5 %collective-permute-start.2 = (bf16[128,128]{1,0:T(8,128)(2,1)S(1)}, bf16[128,128]{1,0:T(8,128)(2,1)S(1)}, u32[]{:S(2)}, u32[]{:S(2)}) collective-permute-start(bf16[128,128]{1,0:T(8,128)(2,1)S(1)} %get-tuple-element.20.extra_ref), channel_id=1, source_target_pairs={{0,32},{1,33},{2,34},{3,35},{4,36},{5,37},{6,38},{7,39},{8,40},{9,... | collective-permute-start | bytes 98312 | tf_op jit(solution)/shard_map/ppermute | solution.py:257
  17.2 0.6 copy-start.15
  17.2 0.8 copy-start.13
  17.2 1.0 copy-start.14
  29.4 20.7 %collective-permute-start.7 = (bf16[128,2176]{1,0:T(8,128)(2,1)}, bf16[128,2176]{1,0:T(8,128)(2,1)S(1)}, u32[]{:S(2)}, u32[]{:S(2)}) collective-permute-start(bf16[128,2176]{1,0:T(8,128)(2,1)} %get-tuple-element.27), channel_id=1, source_target_pairs={{0,33},{1,32},{2,35},{3,34},{4,37},{5,36},{6,39},{7,38},{8,41},{9,... | collective-permute-start | bytes 1671176 | tf_op jit(solution)/shard_map/ppermute | solution.py:260
  31.6 18.5 %collective-permute-start.6 = (bf16[128,2048]{1,0:T(8,128)(2,1)}, bf16[128,2048]{1,0:T(8,128)(2,1)S(1)}, u32[]{:S(2)}, u32[]{:S(2)}) collective-permute-start(bf16[128,2048]{1,0:T(8,128)(2,1)} %get-tuple-element.25), channel_id=1, source_target_pairs={{0,32},{1,33},{2,34},{3,35},{4,36},{5,37},{6,38},{7,39},{8,40},{9,... | collective-permute-start | bytes 1572872 | tf_op jit(solution)/shard_map/ppermute | solution.py:257
  42.7 6.0 %collective-permute-start.10 = (f32[16,2048]{1,0:T(8,128)}, f32[16,2048]{1,0:T(8,128)S(1)}, u32[]{:S(2)}, u32[]{:S(2)}) collective-permute-start(f32[16,2048]{1,0:T(8,128)} %get-tuple-element.28.sums_own), channel_id=1, source_target_pairs={{0,96},{32,64},{64,32},{96,0},{1,97},{33,65},{65,33},{97,1},{2,98}... | collective-permute-start | bytes 393224 | tf_op jit(solution)/shard_map/ppermute | solution.py:310
  42.8 7.3 %collective-permute-start.9 = (f32[16,2048]{1,0:T(8,128)}, f32[16,2048]{1,0:T(8,128)S(1)}, u32[]{:S(2)}, u32[]{:S(2)}) collective-permute-start(f32[16,2048]{1,0:T(8,128)} %get-tuple-element.28.sums_own), channel_id=1, source_target_pairs={{0,32},{32,0},{1,33},{33,1},{2,34},{34,2},{3,35},{35,3},{4,36},{36... | collective-permute-start | bytes 393224 | tf_op jit(solution)/shard_map/ppermute | solution.py:309
  43.5 6.6 %collective-permute-start.8 = (f32[16,2048]{1,0:T(8,128)}, f32[16,2048]{1,0:T(8,128)S(1)}, u32[]{:S(2)}, u32[]{:S(2)}) collective-permute-start(f32[16,2048]{1,0:T(8,128)} %get-tuple-element.28.sums_own), channel_id=1, source_target_pairs={{0,64},{64,0},{1,65},{65,1},{2,66},{66,2},{3,67},{67,3},{4,68},{68... | collective-permute-start | bytes 393224 | tf_op jit(solution)/shard_map/ppermute | solution.py:263
  50.1 1.1 copy-start.1
  51.1 1.0 copy-start.5
  52.2 0.9 copy-start.8
  54.7 31.5 %copy-start = (bf16[2,64,2048]{2,1,0:T(8,128)(2,1)S(1)}, bf16[2,64,2048]{2,1,0:T(8,128)(2,1)}, u32[]{:S(2)}) copy-start(bf16[2,64,2048]{2,1,0:T(8,128)(2,1)} %param.9) | copy-start | bytes 1572868
  54.7 31.5 %copy-start.4 = (bf16[2,64,2048]{2,1,0:T(8,128)(2,1)S(1)}, bf16[2,64,2048]{2,1,0:T(8,128)(2,1)}, u32[]{:S(2)}) copy-start(bf16[2,64,2048]{2,1,0:T(8,128)(2,1)} %param.8) | copy-start | bytes 1572868
  54.7 31.5 %copy-start.7 = (f32[2048,8]{0,1:T(8,128)S(1)}, f32[2048,8]{0,1:T(8,128)}, u32[]{:S(2)}) copy-start(f32[2048,8]{0,1:T(8,128)} %param.13) | copy-start | bytes 196612
  54.7 31.5 %copy-start.10 = (f32[2048]{0:T(1024)S(1)}, f32[2048]{0:T(1024)}, u32[]{:S(2)}) copy-start(f32[2048]{0:T(1024)} %param.14) | copy-start | bytes 24580
  54.7 31.5 %all-to-all-start = ((bf16[32,8,2176]{2,1,0:T(8,128)(2,1)}), bf16[32,8,2176]{2,1,0:T(8,128)(2,1)S(1)}, u32[]{:S(2)}, u32[]{:S(2)}) async-start(bf16[32,8,2176]{2,1,0:T(8,128)(2,1)} %bitcast.12), calls=%async_computation | async-start | bytes 2228224 | tf_op jit(solution)/shard_map/all_to_all | solution.py:315

commit v3 on v2

--- a/solution.py
+++ b/solution.py
@@ -14,8 +14,10 @@
 HIGHEST = lax.Precision.HIGHEST
 NT = (((1,), (1,)), ((), ()))
 VMEM_BYTES = 16 * 1024 * 1024
-EXPERT_VMEM = 60 * 1024 * 1024
+EXPERT_VMEM = 46 * 1024 * 1024
+WIDE_VMEM = 60 * 1024 * 1024
 TILE = 256
+BACK_TILE = 512
 
 
 def params(limit=VMEM_BYTES):
@@ -68,21 +70,23 @@
 def tiles_of(extent, size):
     return [(start, min(size, extent - start)) for start in range(0, extent, size)]
 
-def expert_kernel(
-    count, units, tile, fresh,
-    meta, rows_ref, cot_ref, extra_ref, side_ref, gate_0, gate_1, up_0, up_1, down_0, down_1,
-    mix_ref, grad_ref, params_ref,
-    g_0, g_1, u_0, u_1, d_0, d_1, r_0, r_1, c_0, c_1, hid, dgate, dup, sems,
+def forward_kernel(
+    count, units, tile,
+    meta, rows_own, x_other, cot_own, cot_other, extra_own, extra_other, gain_ref,
+    gate_0, gate_1, up_0, up_1, down_0, down_1,
+    mix_own, mix_a, mix_b, dgate, dup, r_0, r_1, routing_ref, ends_ref,
+    g_0, g_1, u_0, u_1, d_0, d_1, c_0, c_1, hid, sems,
 ):
     hidden_units, half = gate_0.shape
-    total = rows_ref.shape[0]
-    width = 2 * half
+    own, sub = rows_own.shape[0], mix_a.shape[0]
+    total = 2 * own
     local = hidden_units // units
     at_0 = pl.multiple_of(meta[0] * half, half)
     at_1 = pl.multiple_of((1 - meta[0]) * half, half)
     tiles = tiles_of(hidden_units, tile)
-    copies = []
-    for number, (start, size) in enumerate(tiles):
+
+    def fetch(number):
+        start, size = tiles[number]
         group = []
         for which, (source, target) in enumerate(
             ((gate_0, g_0), (gate_1, g_1), (up_0, u_0), (up_1, u_1), (down_0, d_0), (down_1, d_1))
@@ -92,18 +96,19 @@
             )
             copy.start()
             group.append(copy)
-        copies.append(group)
-
-    scaling = inverse_rms(rows_ref[...].astype(F32)) if fresh else None
+        return group
+
+    copies = [fetch(0), fetch(1)]
+    scaling = inverse_rms(x_other[...].astype(F32))
     for at, r, c in ((at_0, r_0, c_0), (at_1, r_1, c_1)):
-        rows = rows_ref[:, pl.ds(at, half)]
-        if fresh:
-            rows = (rows.astype(F32) * scaling * side_ref[:, pl.ds(at, half)]).astype(BF16)
-        r[...] = rows
-        c[...] = cot_ref[:, pl.ds(at, half)]
+        there = pl.ds(at, half)
+        r[:own, :] = rows_own[:, there]
+        r[own:, :] = (x_other[:, there].astype(F32) * scaling * gain_ref[:, there]).astype(BF16)
+        c[:own, :] = cot_own[:, there]
+        c[own:, :] = cot_other[:, there]
 
     lane = lanes(total)
-    extra = extra_ref[...].astype(F32)
+    extra = jnp.concatenate([extra_own[...], extra_other[...]], axis=0).astype(F32)
     weights, signs = [], []
     for which in range(local):
         expert = meta[1] * local + which
@@ -113,8 +118,10 @@
         signs.append(jnp.sum(jnp.where(lane == expert + 2 * count, extra, 0.0), axis=1, keepdims=True))
 
     sums = jnp.zeros((total, 1), F32)
-    for group, (start, size) in zip(copies, tiles):
-        for copy in group:
+    for number, (start, size) in enumerate(tiles):
+        if number + 2 < len(tiles):
+            copies.append(fetch(number + 2))
+        for copy in copies[number]:
             copy.wait()
         span = slice(start, start + size)
 
@@ -141,50 +148,95 @@
         dup[:, span] = (dhid * act).astype(BF16)
         hid[:, span] = (hidden * weight).astype(BF16)
 
+    for at, d in ((at_0, d_0), (at_1, d_1)):
+        there = pl.ds(at, half)
+        mix = jnp.dot(hid[...], d[...], preferred_element_type=F32).astype(BF16)
+        mix_own[:, there] = mix[:own]
+        mix_a[:, there] = mix[own:own + sub]
+        mix_b[:, there] = mix[own + sub:]
+
     high, low = split_low(sums)
-    grad_ref[:, width:] = jnp.where(lane == 0, high, jnp.where(lane == 1, low, 0.0)).astype(BF16)
+    ends_ref[...] = jnp.where(lane == 0, high, jnp.where(lane == 1, low, 0.0)).astype(BF16)
     share = jnp.where(lane < count, extra + pltpu.roll(extra, EXT - count, 1), 0.0)
     dlogits = share * (1.0 - share) * pltpu.roll(extra, EXT - 2 * count, 1) * sums
     high, low = split_low(dlogits)
     sides = jnp.concatenate([high.T[:count], low.T[:count]], axis=0).astype(BF16)
-    for at, g, u, d, r in ((at_0, g_0, u_0, d_0, r_0), (at_1, g_1, u_1, d_1, r_1)):
-        there = pl.ds(at, half)
-        mix_ref[:, there] = jnp.dot(hid[...], d[...], preferred_element_type=F32).astype(BF16)
-        grad = jnp.dot(dgate[...], g[...], preferred_element_type=F32) + jnp.dot(
-            dup[...], u[...], preferred_element_type=F32
-        )
-        grad_ref[:, there] = grad.astype(BF16)
+    for at, r in ((at_0, r_0), (at_1, r_1)):
         routing = jnp.dot(sides, r[...], preferred_element_type=F32)
-        routing = routing[:count] + routing[count:]
-        moved = jnp.sum(grad * r[...].astype(F32), axis=0, keepdims=True)
-        moved = jnp.broadcast_to(moved, routing.shape)
-        if not fresh:
-            routing = routing + side_ref[:count, there]
-            moved = moved + side_ref[count:, there]
-        params_ref[:count, there] = routing
-        params_ref[count:, there] = moved
-
-
-def pack_kernel(mix_own, mix_in, grad_own, grad_in, sums_own, sums_core, sums_across, sums_diagonal, out_ref):
+        routing_ref[:, pl.ds(at, half)] = routing[:count] + routing[count:]
+
+
+def backward_kernel(
+    tile,
+    meta, dgate, dup, r_0, r_1, routing_ref, ends_ref, gate_0, gate_1, up_0, up_1,
+    grad_own, grad_a, grad_b, params_ref,
+    g_0, g_1, u_0, u_1, sems,
+):
+    half = gate_0.shape[1]
+    own, sub = grad_own.shape[0], grad_a.shape[0]
+    count = routing_ref.shape[0]
+    width = 2 * half
+    starts = (pl.multiple_of(meta[0] * half, half), pl.multiple_of((1 - meta[0]) * half, half))
+    spots = ((0, gate_0, g_0, up_0, u_0, r_0), (1, gate_1, g_1, up_1, u_1, r_1))
+    copies = []
+    for which, gate, g, up, u, _ in spots:
+        for number, (start, size) in enumerate(tiles_of(half, tile)):
+            pair = []
+            for kind, (source, target) in enumerate(((gate, g), (up, u))):
+                copy = pltpu.make_async_copy(
+                    source.at[:, pl.ds(start, size)], target.at[:, pl.ds(start, size)], sems.at[which, number, kind]
+                )
+                copy.start()
+                pair.append(copy)
+            copies.append(pair)
+    ends = ends_ref[...]
+    grad_own[:, width:] = ends[:own]
+    grad_a[:, width:] = ends[own:own + sub]
+    grad_b[:, width:] = ends[own + sub:]
+    for which, _, g, _, u, r in spots:
+        for start, size in tiles_of(half, tile):
+            for copy in copies.pop(0):
+                copy.wait()
+            span = slice(start, start + size)
+            grad = jnp.dot(dgate[...], g[:, span], preferred_element_type=F32) + jnp.dot(
+                dup[...], u[:, span], preferred_element_type=F32
+            )
+            there = pl.ds(pl.multiple_of(starts[which] + start, EXT), size)
+            low = grad.astype(BF16)
+            grad_own[:, there] = low[:own]
+            grad_a[:, there] = low[own:own + sub]
+            grad_b[:, there] = low[own + sub:]
+            moved = jnp.sum(grad * r[:, span].astype(F32), axis=0, keepdims=True)
+            moved = jnp.broadcast_to(moved, (count, size))
+            params_ref[:, there] = jnp.concatenate([routing_ref[:, there], moved], axis=0).astype(BF16)
+
+
+def pack_kernel(
+    mix_own, mix_a, mix_b, grad_own, grad_a, grad_b, sums_own, sums_core, sums_across, sums_diagonal, out_ref
+):
     own, width = mix_own.shape
-    out_ref[:own, :width] = (mix_own[...].astype(F32) + mix_in[...].astype(F32)).astype(BF16)
-    out_ref[own:, :width] = (grad_own[:, :width].astype(F32) + grad_in[:, :width].astype(F32)).astype(BF16)
-    both = grad_own[:, width:].astype(F32) + grad_in[:, width:].astype(F32)
-    high, low = split_low(jnp.sum(both, axis=1, keepdims=True))
-    lane = lanes(own)
-    gate_sums = jnp.where(lane == 0, high, jnp.where(lane == 1, low, 0.0))
-    totals = (sums_own[...] + sums_core[...]) + (sums_across[...] + sums_diagonal[...])
+    sub = mix_a.shape[0]
+    totals = (sums_own[...].astype(F32) + sums_core[...].astype(F32)) + (
+        sums_across[...].astype(F32) + sums_diagonal[...].astype(F32)
+    )
+    lane = lanes(sub)
     upper, row = lanes(8) >= EXT // 2, lax.broadcasted_iota(jnp.int32, (8, EXT), 0)
-    for pair in range(own // 16):
+    for begin, mix, grad in ((0, mix_a, grad_a), (sub, mix_b, grad_b)):
+        span = slice(begin, begin + sub)
+        out_ref[0, span, :width] = (mix_own[span, :].astype(F32) + mix[...].astype(F32)).astype(BF16)
+        out_ref[1, span, :width] = (grad_own[span, :width].astype(F32) + grad[:, :width].astype(F32)).astype(BF16)
+        both = grad_own[span, width:].astype(F32) + grad[:, width:].astype(F32)
+        high, low = split_low(jnp.sum(both, axis=1, keepdims=True))
+        gate_sums = jnp.where(lane == 0, high, jnp.where(lane == 1, low, 0.0))
         routing, ends = [], []
-        for place in (2 * pair, 2 * pair + 1):
+        for local in range(sub // 8):
+            place = begin // 8 + local
             part = totals[:, place * EXT:(place + 1) * EXT]
             routing.append(part[:8])
             moved = jnp.where(row == 0, part[8:], jnp.where(row == 1, pltpu.roll(part[8:], EXT // 2, 1), 0.0))
-            ends.append(jnp.where(upper, moved, gate_sums[8 * place:8 * place + 8]))
-        span = slice(16 * pair, 16 * pair + 16)
-        out_ref[span, width:] = jnp.concatenate(routing, axis=0).astype(BF16)
-        out_ref[own + 16 * pair:own + 16 * pair + 16, width:] = jnp.concatenate(ends, axis=0).astype(BF16)
+            ends.append(jnp.where(upper, moved, gate_sums[8 * local:8 * local + 8]))
+        out_ref[0, span, width:] = jnp.concatenate(routing, axis=0).astype(BF16)
+        out_ref[1, span, width:] = jnp.concatenate(ends, axis=0).astype(BF16)
 
 
 def finish_kernel(meta, parts_ref, x_ref, cot_ref, coef_ref, gain_ref, router_ref, out_ref):
@@ -276,7 +328,7 @@
     rows_own, extra_own, coef = pl.pallas_call(
         prologue_kernel,
         out_shape=(struct(own, width), struct(own, EXT), struct(own, EXT, dtype=F32)),
-        compiler_params=params(),
+        compiler_params=params(WIDE_VMEM),
         cost_estimate=pl.CostEstimate(flops=20_000_000_000, bytes_accessed=2**25, transcendentals=0),
     )(flat_x, gain_row, router_rows, routes.reshape(own, 2))
     extra_other = up_x(extra_own)
@@ -284,33 +336,46 @@
     hidden_units = local * units
     near = pl.BlockSpec(memory_space=pltpu.VMEM)
     far = pl.BlockSpec(memory_space=pltpu.HBM)
-    sums_shape = struct(2 * count, width, dtype=F32)
-
-    def experts(fresh, rows, cot, extra, side):
-        return pl.pallas_call(
-            functools.partial(expert_kernel, count, units, TILE, fresh),
-            in_specs=[pl.BlockSpec(memory_space=pltpu.SMEM)] + [near] * 4 + [far] * 6,
-            out_specs=(near, near, near),
-            out_shape=(struct(own, width), struct(own, width + EXT), sums_shape),
-            scratch_shapes=[pltpu.VMEM((hidden_units, half), BF16)] * 6
-            + [pltpu.VMEM((own, half), BF16)] * 4
-            + [pltpu.VMEM((own, hidden_units), BF16)] * 3
-            + [pltpu.SemaphoreType.DMA((len(tiles_of(hidden_units, TILE)), 6))],
-            compiler_params=params(EXPERT_VMEM),
-            cost_estimate=pl.CostEstimate(
-                flops=24 * own * hidden_units * half, bytes_accessed=12 * hidden_units * half, transcendentals=0
-            ),
-        )(meta, rows, cot, extra, side, *maps)
-
-    mix_away, grad_away, sums = experts(True, x_other, cot_other, extra_other, gain_row)
-    mix_in, grad_in = up_x(mix_away), down_x(grad_away)
-    mix_own, grad_own, sums = experts(False, rows_own, flat_cot, extra_own, sums)
+
+    total = 2 * own
+    scalar = pl.BlockSpec(memory_space=pltpu.SMEM)
+    map_room = pltpu.VMEM((hidden_units, half), BF16)
+    mix_own, mix_a, mix_b, dgate, dup, r_0, r_1, routing, ends = pl.pallas_call(
+        functools.partial(forward_kernel, count, units, TILE),
+        in_specs=[scalar] + [near] * 7 + [far] * 6,
+        out_specs=(near,) * 9,
+        out_shape=(
+            struct(own, width), struct(sub, width), struct(sub, width),
+            struct(total, hidden_units), struct(total, hidden_units), struct(total, half), struct(total, half),
+            struct(count, width, dtype=F32), struct(total, EXT),
+        ),
+        scratch_shapes=[map_room] * 6
+        + [pltpu.VMEM((total, half), BF16)] * 2
+        + [pltpu.VMEM((total, hidden_units), BF16)]
+        + [pltpu.SemaphoreType.DMA((len(tiles_of(hidden_units, TILE)), 6))],
+        compiler_params=params(EXPERT_VMEM),
+        cost_estimate=pl.CostEstimate(flops=2_000_000_000_000, bytes_accessed=1024, transcendentals=0),
+    )(meta, rows_own, x_other, flat_cot, cot_other, extra_own, extra_other, gain_row, *maps)
+    mix_a, mix_b = up_x(mix_a), down_x(mix_b)
+    grad_own, grad_a, grad_b, sums = pl.pallas_call(
+        functools.partial(backward_kernel, BACK_TILE),
+        in_specs=[scalar] + [near] * 6 + [far] * 4,
+        out_specs=(near,) * 4,
+        out_shape=(
+            struct(own, width + EXT), struct(sub, width + EXT), struct(sub, width + EXT), struct(2 * count, width),
+        ),
+        scratch_shapes=[map_room] * 4 + [pltpu.SemaphoreType.DMA((2, half // BACK_TILE, 2))],
+        compiler_params=params(EXPERT_VMEM),
+        cost_estimate=pl.CostEstimate(flops=1_000_000_000_000, bytes_accessed=1024, transcendentals=0),
+    )(meta, dgate, dup, r_0, r_1, routing, ends, *maps[:4])
+    mix_a, mix_b, grad_a, grad_b, sums = lax.optimization_barrier((mix_a, mix_b, grad_a, grad_b, sums))
+    grad_a, grad_b = up_x(grad_a), down_x(grad_b)
     core = other_core(sums)
     across = lax.ppermute(sums, "expert", [(0, 1), (1, 0)])
     diagonal = lax.ppermute(sums, ("section", "expert"), [(0, 3), (1, 2), (2, 1), (3, 0)])
-    packed = pl.pallas_call(pack_kernel, out_shape=struct(2 * own, width + EXT), compiler_params=params())(
-        mix_own, mix_in, grad_own, grad_in, sums, core, across, diagonal
-    )
+    packed = pl.pallas_call(
+        pack_kernel, out_shape=struct(2, own, width + EXT), compiler_params=params()
+    )(mix_own, mix_a, mix_b, grad_own, grad_a, grad_b, sums, core, across, diagonal)
     rows_each = 2 * own // n_dp
     chunks = lax.all_to_all(packed.reshape(n_dp, rows_each, width + EXT), "dp", 0, 0, tiled=True)
 

time: 112 us -> 107 us (0.955)
  local copies, waits for them, and re-layouts: 8.75 us -> 3.95 us
  Pallas kernels: 27.2 us -> 22.5 us
  starting transfers between devices: 20.9 us -> 25 us
  waiting for transfers between devices: 29.9 us -> 32.1 us
    pallas_call x3, Pallas kernels: 23.9 us -> 17.3 us  [the longest x1 9.84 us: shards(): pl.pallas_call(functools.partial(forward_kernel, count, units, TILE), in_...]
    unnamed x33 -> x25, local copies, waits for them, and re-layouts: 8.75 us -> 3.95 us
    ppermute x3 -> x4, waiting for transfers between devices: 4.45 us -> 7.82 us  [up_x(): return lax.ppermute(array, ('expert', 'dp'), around(1))]
    ppermute x2 -> x3, starting transfers between devices: 3.8 us -> 6.92 us  [down_x(): return lax.ppermute(array, ('expert', 'dp'), around(3))]
    pallas_call x1, Pallas kernels: 1.21 us -> 3.07 us  [shards(): pl.pallas_call(prologue_kernel, out_shape=(struct(own, width), struct(own...]
    ppermute x1, waiting for transfers between devices: 4.11 us -> 2.59 us  [shards(): lax.ppermute(sums, ('section', 'expert'), [(0, 3), (1, 2), (2, 1), (3, 0)])]
    ppermute x3 -> x4, starting transfers between devices: 3.1 us -> 3.75 us  [up_x(): return lax.ppermute(array, ('expert', 'dp'), around(1))]
  transfers between devices with their start and end apart: 12 -> 14, of which waited for: 4 -> 5; matrix products, arithmetic and copies ran while one was open for 1% -> 1% of each run, Pallas kernels for 11% -> 7%
where the time goes in v3:
time: 107 us
  waiting for transfers between devices  32.1 us (30%)
  starting transfers between devices  25 us (23%)
  Pallas kernels  22.5 us (21%)
  blocking collectives  22.3 us (21%)
  local copies, waits for them, and re-layouts  3.95 us (4%)
    all_to_all x1, blocking collectives, shards(): gathered = lax.all_to_all(finished, 'dp', 0, 0, tiled=True)  22.3 us
    all_to_all x1, waiting for transfers between devices, shards(): lax.all_to_all(packed.reshape(n_dp, rows_each, width + EXT), 'dp', 0, 0,...  19.2 us
    all_to_all x1, starting transfers between devices, shards(): lax.all_to_all(packed.reshape(n_dp, rows_each, width + EXT), 'dp', 0, 0,...  11.8 us
    pallas_call x1, Pallas kernels, shards(): pl.pallas_call(functools.partial(forward_kernel, count, units, TILE), in_...  9.84 us
    ppermute x4, waiting for transfers between devices, up_x(): return lax.ppermute(array, ('expert', 'dp'), around(1))  7.82 us
    ppermute x3, starting transfers between devices, down_x(): return lax.ppermute(array, ('expert', 'dp'), around(3))  6.92 us
    pallas_call x1, Pallas kernels, shards(): pl.pallas_call(functools.partial(backward_kernel, BACK_TILE), in_specs=[s...  4.86 us
    unnamed x25, local copies, waits for them, and re-layouts  3.95 us
  transfers between devices with their start and end apart: 14, of which 5 were waited for; matrix products, arithmetic and copies ran while one was open for 1% of the time, Pallas kernels for 7%

profile of v3, /device:TPU:0, one launch (start us, length us, event | category | flops | bytes accessed | tf_op | source)
XLA Modules:
  0.0 106.7 jit_solution(16897163086289809360)
XLA Ops:
  0.6 0.1 collective-permute-start.3
  0.7 1.6 %collective-permute-start = (bf16[128,2048]{1,0:T(8,128)(2,1)}, bf16[128,2048]{1,0:T(8,128)(2,1)S(1)}, u32[]{:S(2)}, u32[]{:S(2)}) collective-permute-start(bf16[128,2048]{1,0:T(8,128)(2,1)} %bitcast.20), channel_id=1, source_target_pairs={{0,32},{1,33},{2,34},{3,35},{4,36},{5,37},{6,38},{7,39},{8,40},{9,... | collective-permute-start | bytes 1572872 | tf_op jit(solution)/shard_map/ppermute | solution.py:309
  2.4 1.7 %collective-permute-start.1 = (bf16[128,2048]{1,0:T(8,128)(2,1)}, bf16[128,2048]{1,0:T(8,128)(2,1)S(1)}, u32[]{:S(2)}, u32[]{:S(2)}) collective-permute-start(bf16[128,2048]{1,0:T(8,128)(2,1)} %bitcast.23), channel_id=1, source_target_pairs={{0,33},{1,32},{2,35},{3,34},{4,37},{5,36},{6,39},{7,38},{8,41},{9,... | collective-permute-start | bytes 1572872 | tf_op jit(solution)/shard_map/ppermute | solution.py:312
  4.0 0.0 collective-permute-start.4
  4.0 1.4 %copy.12 = s32[2,64,2]{2,1,0:T(8,128)} copy(s32[2,64,2]{1,2,0:T(2,128)} %param.15) | data formatting | bytes 2048 | tf_op args[7]
  5.5 0.5 collective-permute-start.5
  6.0 0.7 copy-done.8
  6.7 3.1 %shard_map.111 = (bf16[128,2048]{1,0:T(8,128)(2,1)}, bf16[128,128]{1,0:T(8,128)(2,1)}, f32[128,128]{1,0:T(8,128)}) custom-call(bf16[128,2048]{1,0:T(8,128)(2,1)} %bitcast.21, f32[1,2048]{1,0:T(1,128)} %bitcast.30, f32[8,2048]{1,0:T(8,128)} %bitcast.26, s32[128,2]{1,0:T(8,128)} %bitcast.37), custom_call_target="tpu_custom_call" | custom-call | flops 20000000000 | bytes 33554432 | tf_op jit(solution)/shard_map/pallas_call | solution.py:328
  9.7 0.8 collective-permute-start.2
  10.6 0.1 pad_add_fusion.1.meta
  10.6 6.5 %collective-permute-done.2.extra_other = bf16[128,128]{1,0:T(8,128)(2,1)S(1)} collective-permute-done((bf16[128,128]{1,0:T(8,128)(2,1)}, bf16[128,128]{1,0:T(8,128)(2,1)S(1)}, u32[]{:S(2)}, u32[]{:S(2)}) %collective-permute-start.2) | collective-permute-done | bytes 32800 | tf_op jit(solution)/shard_map/ppermute | solution.py:309
  17.2 0.0 copy-start.10
  17.3 0.7 copy-done.10
  18.0 1.0 copy-done.11
  19.0 9.8 %shard_map.112 = (bf16[128,2048]{1,0:T(8,128)(2,1)S(1)}, bf16[64,2048]{1,0:T(8,128)(2,1)}, bf16[64,2048]{1,0:T(8,128)(2,1)}, bf16[256,896]{1,0:T(8,128)(2,1)S(1)...) custom-call(s32[2]{0:T(128)S(1)} %pad_add_fusion.1.meta, ...), custom_call_target="tpu_custom_call" | custom-call | flops 1999999991808 | bytes 1024 | tf_op jit(solution)/shard_map/pallas_call | solution.py:343
  28.9 0.9 collective-permute-start.6
  29.8 2.4 %collective-permute-start.7 = (bf16[64,2048]{1,0:T(8,128)(2,1)}, bf16[64,2048]{1,0:T(8,128)(2,1)}, u32[]{:S(2)}, u32[]{:S(2)}) collective-permute-start(bf16[64,2048]{1,0:T(8,128)(2,1)} %get-tuple-element.37), channel_id=1, source_target_pairs={{0,33},{1,32},{2,35},{3,34},{4,37},{5,36},{6,39},{7,38},{8,41},{9,... | collective-permute-start | bytes 786440 | tf_op jit(solution)/shard_map/ppermute | solution.py:312
  32.2 4.9 %shard_map.113 = (bf16[128,2176]{1,0:T(8,128)(2,1)S(1)}, bf16[64,2176]{1,0:T(8,128)(2,1)S(1)}, bf16[64,2176]{1,0:T(8,128)(2,1)S(1)}, bf16[16,2048]{1,0:T(8,128)(2,1)S(1)}) custom-call(s32[2]{0:T(128)S(1)} %pad_add_fusion.1.meta, bf16[256,896]{1,0:T(8,128)(2,1)S(1)} %get-tuple-element.38.dgate, bf16[256,896]{1,0:T(8,128)(2,1)S(1)} %get-tuple-element.39.dup, ...), custom_call_target="tpu_custom_call" | custom-call | flops 999999995904 | bytes 1024 | tf_op jit(solution)/shard_map/pallas_call | solution.py:360
  37.1 1.3 %collective-permute-done.6.mix_a = bf16[64,2048]{1,0:T(8,128)(2,1)} collective-permute-done((bf16[64,2048]{1,0:T(8,128)(2,1)}, bf16[64,2048]{1,0:T(8,128)(2,1)}, u32[]{:S(2)}, u32[]{:S(2)}) %collective-permute-start.6) | collective-permute-done | bytes 262176 | tf_op jit(solution)/shard_map/ppermute | solution.py:309
  38.4 0.4 collective-permute-start.8
  38.7 2.9 %collective-permute-start.9 = (bf16[64,2176]{1,0:T(8,128)(2,1)S(1)}, bf16[64,2176]{1,0:T(8,128)(2,1)S(1)}, u32[]{:S(2)}, u32[]{:S(2)}) collective-permute-start(bf16[64,2176]{1,0:T(8,128)(2,1)S(1)} %get-tuple-element.51), channel_id=1, source_target_pairs={{0,33},{1,32},{2,35},{3,34},{4,37},{5,36},{6,39},{7,38},{8,41},{9,... | collective-permute-start | bytes 835592 | tf_op jit(solution)/shard_map/ppermute | solution.py:312
  41.6 1.9 %collective-permute-start.10 = (bf16[16,2048]{1,0:T(8,128)(2,1)S(1)}, bf16[16,2048]{1,0:T(8,128)(2,1)S(1)}, u32[]{:S(2)}, u32[]{:S(2)}) collective-permute-start(bf16[16,2048]{1,0:T(8,128)(2,1)S(1)} %get-tuple-element.52.sums_own), channel_id=1, source_target_pairs={{0,64},{64,0},{1,65},{65,1},{2,66},{66,2},{3,67},{67,3},{4,68},{68... | collective-permute-start | bytes 196616 | tf_op jit(solution)/shard_map/ppermute | solution.py:315
  43.5 2.6 %collective-permute-done.12.sums_diagonal = bf16[16,2048]{1,0:T(8,128)(2,1)S(1)} collective-permute-done((bf16[16,2048]{1,0:T(8,128)(2,1)S(1)}, bf16[16,2048]{1,0:T(8,128)(2,1)S(1)}, u32[]{:S(2)}, u32[]{:S(2)}) %collective-permute-start.12) | collective-permute-done | bytes 65568 | tf_op jit(solution)/shard_map/ppermute | solution.py:375
  46.1 2.4 %collective-permute-done.11.sums_across = bf16[16,2048]{1,0:T(8,128)(2,1)S(1)} collective-permute-done((bf16[16,2048]{1,0:T(8,128)(2,1)S(1)}, bf16[16,2048]{1,0:T(8,128)(2,1)S(1)}, u32[]{:S(2)}, u32[]{:S(2)}) %collective-permute-start.11) | collective-permute-done | bytes 65568 | tf_op jit(solution)/shard_map/ppermute | solution.py:374
  48.5 2.6 %shard_map.114 = bf16[2,128,2176]{2,1,0:T(8,128)(2,1)} custom-call(bf16[128,2048]{1,0:T(8,128)(2,1)S(1)} %get-tuple-element.35.mix_own, bf16[64,2048]{1,0:T(8,128)(2,1)} %collective-permute-done.6.mix_a, bf16[64,2048]{1,0:T(8,128)(2,1)} %collective-permute-done.7.mix_b, bf16[128,2176]{1,0:T(8,128)(2,1)S(1)} %get-tuple-element.49.grad_own, ...), custom_call_target="tpu_custom_call" | custom-call | tf_op jit(solution)/shard_map/pallas_call | solution.py:376
  51.1 0.0 copy-start.6
  51.1 11.8 %all-to-all-start = ((bf16[32,8,2176]{2,1,0:T(8,128)(2,1)}), bf16[32,8,2176]{2,1,0:T(8,128)(2,1)S(1)}, u32[]{:S(2)}, u32[]{:S(2)}) async-start(bf16[32,8,2176]{2,1,0:T(8,128)(2,1)} %bitcast.12), calls=%async_computation | async-start | bytes 2228224 | tf_op jit(solution)/shard_map/all_to_all | solution.py:380
  63.0 0.1 pad_add_fusion.meta
  63.0 19.2 %all-to-all-done.parts_ref = bf16[32,8,2176]{2,1,0:T(8,128)(2,1)S(1)} async-done(((bf16[32,8,2176]{2,1,0:T(8,128)(2,1)}), bf16[32,8,2176]{2,1,0:T(8,128)(2,1)S(1)}, u32[]{:S(2)}, u32[]{:S(2)}) %all-to-all-start) | async-done | bytes 1114144 | tf_op jit(solution)/shard_map/all_to_all | solution.py:380
  82.3 1.0 shard_map.115
  83.4 22.3 %all_to_all.10.all_ref = bf16[32,8,2176]{2,1,0:T(8,128)(2,1)S(1)} all-to-all(bf16[32,8,2176]{2,1,0:T(8,128)(2,1)S(1)} %shard_map.115), channel_id=1, replica_groups=mesh['section'=2,'expert'=2,'dp'=32] {'dp'}, dimensions={0} | all-to-all | bytes 2228224 | tf_op jit(solution)/shard_map/all_to_all | solution.py:407
  105.6 1.0 shard_map.116
  (30 shorter events, 0.1 us)
Async XLA Ops:
  0.6 4.8 %collective-permute-start.3 = (bf16[896,1024]{1,0:T(8,128)(2,1)}, bf16[896,1024]{1,0:T(8,128)(2,1)S(1)}, u32[]{:S(2)}, u32[]{:S(2)}) collective-permute-start(bf16[896,1024]{1,0:T(8,128)(2,1)} %bitcast.34), channel_id=1, source_target_pairs={{0,64},{64,0},{1,65},{65,1},{2,66},{66,2},{3,67},{67,3},{4,68},{68... | collective-permute-start | bytes 5505032 | tf_op jit(solution)/shard_map/ppermute | solution.py:315
  0.7 16.5 %collective-permute-start = (bf16[128,2048]{1,0:T(8,128)(2,1)}, bf16[128,2048]{1,0:T(8,128)(2,1)S(1)}, u32[]{:S(2)}, u32[]{:S(2)}) collective-permute-start(bf16[128,2048]{1,0:T(8,128)(2,1)} %bitcast.20), channel_id=1, source_target_pairs={{0,32},{1,33},{2,34},{3,35},{4,36},{5,37},{6,38},{7,39},{8,40},{9,... | collective-permute-start | bytes 1572872 | tf_op jit(solution)/shard_map/ppermute | solution.py:309
  2.4 14.8 %collective-permute-start.1 = (bf16[128,2048]{1,0:T(8,128)(2,1)}, bf16[128,2048]{1,0:T(8,128)(2,1)S(1)}, u32[]{:S(2)}, u32[]{:S(2)}) collective-permute-start(bf16[128,2048]{1,0:T(8,128)(2,1)} %bitcast.23), channel_id=1, source_target_pairs={{0,33},{1,32},{2,35},{3,34},{4,37},{5,36},{6,39},{7,38},{8,41},{9,... | collective-permute-start | bytes 1572872 | tf_op jit(solution)/shard_map/ppermute | solution.py:312
  4.0 13.2 %collective-permute-start.4 = (bf16[896,1024]{1,0:T(8,128)(2,1)}, bf16[896,1024]{1,0:T(8,128)(2,1)}, u32[]{:S(2)}, u32[]{:S(2)}) collective-permute-start(bf16[896,1024]{1,0:T(8,128)(2,1)} %bitcast.40), channel_id=1, source_target_pairs={{0,64},{64,0},{1,65},{65,1},{2,66},{66,2},{3,67},{67,3},{4,68},{68... | collective-permute-start | bytes 5505032 | tf_op jit(solution)/shard_map/ppermute | solution.py:315
  5.5 1.2 %copy-start.8 = (bf16[896,1024]{1,0:T(8,128)(2,1)}, bf16[896,1024]{1,0:T(8,128)(2,1)S(1)}, u32[]{:S(2)}) copy-start(bf16[896,1024]{1,0:T(8,128)(2,1)S(1)} %collective-permute-done.3.gate_1) | copy-start | bytes 5505028
  5.5 11.7 %collective-permute-start.5 = (bf16[896,1024]{1,0:T(8,128)(2,1)}, bf16[896,1024]{1,0:T(8,128)(2,1)}, u32[]{:S(2)}, u32[]{:S(2)}) collective-permute-start(bf16[896,1024]{1,0:T(8,128)(2,1)} %bitcast.38), channel_id=1, source_target_pairs={{0,64},{64,0},{1,65},{65,1},{2,66},{66,2},{3,67},{67,3},{4,68},{68... | collective-permute-start | bytes 5505032 | tf_op jit(solution)/shard_map/ppermute | solution.py:315
  6.7 10.5 %copy-start.1 = (bf16[2,64,2048]{2,1,0:T(8,128)(2,1)S(1)}, bf16[2,64,2048]{2,1,0:T(8,128)(2,1)}, u32[]{:S(2)}) copy-start(bf16[2,64,2048]{2,1,0:T(8,128)(2,1)} %param.9) | copy-start | bytes 1572868
  6.7 10.6 %copy-start.5 = (f32[2048]{0:T(1024)S(1)}, f32[2048]{0:T(1024)}, u32[]{:S(2)}) copy-start(f32[2048]{0:T(1024)} %param.14) | copy-start | bytes 24580
  6.7 10.6 %copy-start.7 = (bf16[4,224,1024]{2,1,0:T(8,128)(2,1)S(1)}, bf16[4,224,1024]{2,1,0:T(8,128)(2,1)}, u32[]{:S(2)}) copy-start(bf16[4,224,1024]{2,1,0:T(8,128)(2,1)} %param.10) | copy-start | bytes 5505028
  9.7 7.4 %collective-permute-start.2 = (bf16[128,128]{1,0:T(8,128)(2,1)}, bf16[128,128]{1,0:T(8,128)(2,1)S(1)}, u32[]{:S(2)}, u32[]{:S(2)}) collective-permute-start(bf16[128,128]{1,0:T(8,128)(2,1)} %get-tuple-element.32.extra_own), channel_id=1, source_target_pairs={{0,32},{1,33},{2,34},{3,35},{4,36},{5,37},{6,38},{7,39},{8,40},{9,... | collective-permute-start | bytes 98312 | tf_op jit(solution)/shard_map/ppermute | solution.py:309
  17.2 0.8 copy-start.10
  18.0 1.0 copy-start.11
  19.0 13.2 %copy-start.9 = (bf16[896,1024]{1,0:T(8,128)(2,1)S(1)}, bf16[896,1024]{1,0:T(8,128)(2,1)}, u32[]{:S(2)}) copy-start(bf16[896,1024]{1,0:T(8,128)(2,1)} %copy-done.8) | copy-start | bytes 5505028
  28.9 9.5 %collective-permute-start.6 = (bf16[64,2048]{1,0:T(8,128)(2,1)}, bf16[64,2048]{1,0:T(8,128)(2,1)}, u32[]{:S(2)}, u32[]{:S(2)}) collective-permute-start(bf16[64,2048]{1,0:T(8,128)(2,1)} %get-tuple-element.36), channel_id=1, source_target_pairs={{0,32},{1,33},{2,34},{3,35},{4,36},{5,37},{6,38},{7,39},{8,40},{9,... | collective-permute-start | bytes 786440 | tf_op jit(solution)/shard_map/ppermute | solution.py:309
  29.8 8.5 %collective-permute-start.7 = (bf16[64,2048]{1,0:T(8,128)(2,1)}, bf16[64,2048]{1,0:T(8,128)(2,1)}, u32[]{:S(2)}, u32[]{:S(2)}) collective-permute-start(bf16[64,2048]{1,0:T(8,128)(2,1)} %get-tuple-element.37), channel_id=1, source_target_pairs={{0,33},{1,32},{2,35},{3,34},{4,37},{5,36},{6,39},{7,38},{8,41},{9,... | collective-permute-start | bytes 786440 | tf_op jit(solution)/shard_map/ppermute | solution.py:312
  38.4 10.1 %collective-permute-start.8 = (bf16[64,2176]{1,0:T(8,128)(2,1)S(1)}, bf16[64,2176]{1,0:T(8,128)(2,1)S(1)}, u32[]{:S(2)}, u32[]{:S(2)}) collective-permute-start(bf16[64,2176]{1,0:T(8,128)(2,1)S(1)} %get-tuple-element.50), channel_id=1, source_target_pairs={{0,32},{1,33},{2,34},{3,35},{4,36},{5,37},{6,38},{7,39},{8,40},{9,... | collective-permute-start | bytes 835592 | tf_op jit(solution)/shard_map/ppermute | solution.py:309
  38.7 9.8 %collective-permute-start.9 = (bf16[64,2176]{1,0:T(8,128)(2,1)S(1)}, bf16[64,2176]{1,0:T(8,128)(2,1)S(1)}, u32[]{:S(2)}, u32[]{:S(2)}) collective-permute-start(bf16[64,2176]{1,0:T(8,128)(2,1)S(1)} %get-tuple-element.51), channel_id=1, source_target_pairs={{0,33},{1,32},{2,35},{3,34},{4,37},{5,36},{6,39},{7,38},{8,41},{9,... | collective-permute-start | bytes 835592 | tf_op jit(solution)/shard_map/ppermute | solution.py:312
  41.6 4.5 %collective-permute-start.12 = (bf16[16,2048]{1,0:T(8,128)(2,1)S(1)}, bf16[16,2048]{1,0:T(8,128)(2,1)S(1)}, u32[]{:S(2)}, u32[]{:S(2)}) collective-permute-start(bf16[16,2048]{1,0:T(8,128)(2,1)S(1)} %get-tuple-element.52.sums_own), channel_id=1, source_target_pairs={{0,96},{32,64},{64,32},{96,0},{1,97},{33,65},{65,33},{97,1},{2,98}... | collective-permute-start | bytes 196616 | tf_op jit(solution)/shard_map/ppermute | solution.py:375
  41.6 6.9 %collective-permute-start.11 = (bf16[16,2048]{1,0:T(8,128)(2,1)S(1)}, bf16[16,2048]{1,0:T(8,128)(2,1)S(1)}, u32[]{:S(2)}, u32[]{:S(2)}) collective-permute-start(bf16[16,2048]{1,0:T(8,128)(2,1)S(1)} %get-tuple-element.52.sums_own), channel_id=1, source_target_pairs={{0,32},{32,0},{1,33},{33,1},{2,34},{34,2},{3,35},{35,3},{4,36},{36... | collective-permute-start | bytes 196616 | tf_op jit(solution)/shard_map/ppermute | solution.py:374
  41.6 6.9 %collective-permute-start.10 = (bf16[16,2048]{1,0:T(8,128)(2,1)S(1)}, bf16[16,2048]{1,0:T(8,128)(2,1)S(1)}, u32[]{:S(2)}, u32[]{:S(2)}) collective-permute-start(bf16[16,2048]{1,0:T(8,128)(2,1)S(1)} %get-tuple-element.52.sums_own), channel_id=1, source_target_pairs={{0,64},{64,0},{1,65},{65,1},{2,66},{66,2},{3,67},{67,3},{4,68},{68... | collective-permute-start | bytes 196616 | tf_op jit(solution)/shard_map/ppermute | solution.py:315
  51.1 31.2 %copy-start = (bf16[2,64,2048]{2,1,0:T(8,128)(2,1)S(1)}, bf16[2,64,2048]{2,1,0:T(8,128)(2,1)}, u32[]{:S(2)}) copy-start(bf16[2,64,2048]{2,1,0:T(8,128)(2,1)} %param.8) | copy-start | bytes 1572868
  51.1 31.2 %copy-start.2 = (bf16[2,64,2048]{2,1,0:T(8,128)(2,1)S(1)}, bf16[2,64,2048]{2,1,0:T(8,128)(2,1)}, u32[]{:S(2)}) copy-start(bf16[2,64,2048]{2,1,0:T(8,128)(2,1)} %param.9) | copy-start | bytes 1572868
  51.1 31.2 %copy-start.3 = (f32[2048,8]{0,1:T(8,128)S(1)}, f32[2048,8]{0,1:T(8,128)}, u32[]{:S(2)}) copy-start(f32[2048,8]{0,1:T(8,128)} %param.13) | copy-start | bytes 196612
  51.1 31.2 %copy-start.4 = (f32[128,128]{1,0:T(8,128)S(1)}, f32[128,128]{1,0:T(8,128)}, u32[]{:S(2)}) copy-start(f32[128,128]{1,0:T(8,128)} %get-tuple-element.53) | copy-start | bytes 196612
  51.1 31.2 %copy-start.6 = (f32[2048]{0:T(1024)S(1)}, f32[2048]{0:T(1024)}, u32[]{:S(2)}) copy-start(f32[2048]{0:T(1024)} %param.14) | copy-start | bytes 24580
  51.1 31.2 %all-to-all-start = ((bf16[32,8,2176]{2,1,0:T(8,128)(2,1)}), bf16[32,8,2176]{2,1,0:T(8,128)(2,1)S(1)}, u32[]{:S(2)}, u32[]{:S(2)}) async-start(bf16[32,8,2176]{2,1,0:T(8,128)(2,1)} %bitcast.12), calls=%async_computation | async-start | bytes 2228224 | tf_op jit(solution)/shard_map/all_to_all | solution.py:380

commit v4 on v3

--- a/solution.py
+++ b/solution.py
@@ -14,10 +14,10 @@
 HIGHEST = lax.Precision.HIGHEST
 NT = (((1,), (1,)), ((), ()))
 VMEM_BYTES = 16 * 1024 * 1024
-EXPERT_VMEM = 46 * 1024 * 1024
-WIDE_VMEM = 60 * 1024 * 1024
+EXPERT_VMEM = 41 * 1024 * 1024
+BACK_VMEM = 16 * 1024 * 1024
+WIDE_VMEM = 16 * 1024 * 1024
 TILE = 256
-BACK_TILE = 512
 
 
 def params(limit=VMEM_BYTES):
@@ -68,14 +68,16 @@
 
 
 def tiles_of(extent, size):
-    return [(start, min(size, extent - start)) for start in range(0, extent, size)]
+    starts = [0] + list(range(size // 2, extent, size))
+    return [(start, min(end, extent) - start) for start, end in zip(starts, starts[1:] + [extent])]
+
 
 def forward_kernel(
     count, units, tile,
     meta, rows_own, x_other, cot_own, cot_other, extra_own, extra_other, gain_ref,
     gate_0, gate_1, up_0, up_1, down_0, down_1,
-    mix_own, mix_a, mix_b, dgate, dup, r_0, r_1, routing_ref, ends_ref,
-    g_0, g_1, u_0, u_1, d_0, d_1, c_0, c_1, hid, sems,
+    mix_own, mix_a, mix_b, dgate, dup, r_0, r_1, routing_ref, ends_ref, g_0, g_1, u_0, u_1,
+    d_0, d_1, c_0, c_1, hid, sems,
 ):
     hidden_units, half = gate_0.shape
     own, sub = rows_own.shape[0], mix_a.shape[0]
@@ -117,12 +119,12 @@
         )
         signs.append(jnp.sum(jnp.where(lane == expert + 2 * count, extra, 0.0), axis=1, keepdims=True))
 
-    sums = jnp.zeros((total, 1), F32)
-    for number, (start, size) in enumerate(tiles):
+    def products(number):
         if number + 2 < len(tiles):
             copies.append(fetch(number + 2))
         for copy in copies[number]:
             copy.wait()
+        start, size = tiles[number]
         span = slice(start, start + size)
 
         def both(left_0, left_1, map_0, map_1):
@@ -130,9 +132,15 @@
                 left_1[...], map_1[span, :], NT, preferred_element_type=F32
             )
 
-        pre_gate = both(r_0, r_1, g_0, g_1)
-        pre_up = both(r_0, r_1, u_0, u_1)
-        dhid = both(c_0, c_1, d_0, d_1)
+        return both(r_0, r_1, g_0, g_1), both(r_0, r_1, u_0, u_1), both(c_0, c_1, d_0, d_1)
+
+    sums = jnp.zeros((total, 1), F32)
+    ahead = products(0)
+    for number, (start, size) in enumerate(tiles):
+        pre_gate, pre_up, dhid = ahead
+        if number + 1 < len(tiles):
+            ahead = products(number + 1)
+        span = slice(start, start + size)
         column = lax.broadcasted_iota(jnp.int32, (total, size), 1) + start
         first = start // units
         weight, sign = weights[first], signs[first]
@@ -167,58 +175,35 @@
 
 
 def backward_kernel(
-    tile,
-    meta, dgate, dup, r_0, r_1, routing_ref, ends_ref, gate_0, gate_1, up_0, up_1,
-    grad_own, grad_a, grad_b, params_ref,
-    g_0, g_1, u_0, u_1, sems,
+    meta, dgate, dup, r_0, r_1, routing_ref, ends_ref, g_0, g_1, u_0, u_1, grad_own, grad_a, grad_b, params_ref
 ):
-    half = gate_0.shape[1]
+    half = g_0.shape[1]
     own, sub = grad_own.shape[0], grad_a.shape[0]
     count = routing_ref.shape[0]
-    width = 2 * half
-    starts = (pl.multiple_of(meta[0] * half, half), pl.multiple_of((1 - meta[0]) * half, half))
-    spots = ((0, gate_0, g_0, up_0, u_0, r_0), (1, gate_1, g_1, up_1, u_1, r_1))
-    copies = []
-    for which, gate, g, up, u, _ in spots:
-        for number, (start, size) in enumerate(tiles_of(half, tile)):
-            pair = []
-            for kind, (source, target) in enumerate(((gate, g), (up, u))):
-                copy = pltpu.make_async_copy(
-                    source.at[:, pl.ds(start, size)], target.at[:, pl.ds(start, size)], sems.at[which, number, kind]
-                )
-                copy.start()
-                pair.append(copy)
-            copies.append(pair)
     ends = ends_ref[...]
-    grad_own[:, width:] = ends[:own]
-    grad_a[:, width:] = ends[own:own + sub]
-    grad_b[:, width:] = ends[own + sub:]
-    for which, _, g, _, u, r in spots:
-        for start, size in tiles_of(half, tile):
-            for copy in copies.pop(0):
-                copy.wait()
-            span = slice(start, start + size)
-            grad = jnp.dot(dgate[...], g[:, span], preferred_element_type=F32) + jnp.dot(
-                dup[...], u[:, span], preferred_element_type=F32
-            )
-            there = pl.ds(pl.multiple_of(starts[which] + start, EXT), size)
-            low = grad.astype(BF16)
-            grad_own[:, there] = low[:own]
-            grad_a[:, there] = low[own:own + sub]
-            grad_b[:, there] = low[own + sub:]
-            moved = jnp.sum(grad * r[:, span].astype(F32), axis=0, keepdims=True)
-            moved = jnp.broadcast_to(moved, (count, size))
-            params_ref[:, there] = jnp.concatenate([routing_ref[:, there], moved], axis=0).astype(BF16)
+    grad_own[:, 2 * half:] = ends[:own]
+    grad_a[:, 2 * half:] = ends[own:own + sub]
+    grad_b[:, 2 * half:] = ends[own + sub:]
+    for at, g, u, r in ((meta[0], g_0, u_0, r_0), (1 - meta[0], g_1, u_1, r_1)):
+        there = pl.ds(pl.multiple_of(at * half, half), half)
+        grad = jnp.dot(dgate[...], g[...], preferred_element_type=F32) + jnp.dot(
+            dup[...], u[...], preferred_element_type=F32
+        )
+        low = grad.astype(BF16)
+        grad_own[:, there] = low[:own]
+        grad_a[:, there] = low[own:own + sub]
+        grad_b[:, there] = low[own + sub:]
+        moved = jnp.sum(grad * r[...].astype(F32), axis=0, keepdims=True)
+        moved = jnp.broadcast_to(moved, (count, half))
+        params_ref[:, there] = jnp.concatenate([routing_ref[:, there], moved], axis=0)
 
 
 def pack_kernel(
-    mix_own, mix_a, mix_b, grad_own, grad_a, grad_b, sums_own, sums_core, sums_across, sums_diagonal, out_ref
+    mix_own, mix_a, mix_b, grad_own, grad_a, grad_b, sums_own, sums_across, out_ref
 ):
     own, width = mix_own.shape
     sub = mix_a.shape[0]
-    totals = (sums_own[...].astype(F32) + sums_core[...].astype(F32)) + (
-        sums_across[...].astype(F32) + sums_diagonal[...].astype(F32)
-    )
+    totals = sums_own[...].astype(F32) + sums_across[...].astype(F32)
     lane = lanes(sub)
     upper, row = lanes(8) >= EXT // 2, lax.broadcasted_iota(jnp.int32, (8, EXT), 0)
     for begin, mix, grad in ((0, mix_a, grad_a), (sub, mix_b, grad_b)):
@@ -340,16 +325,17 @@
     total = 2 * own
     scalar = pl.BlockSpec(memory_space=pltpu.SMEM)
     map_room = pltpu.VMEM((hidden_units, half), BF16)
-    mix_own, mix_a, mix_b, dgate, dup, r_0, r_1, routing, ends = pl.pallas_call(
+    mix_own, mix_a, mix_b, dgate, dup, r_0, r_1, routing, ends, *held = pl.pallas_call(
         functools.partial(forward_kernel, count, units, TILE),
         in_specs=[scalar] + [near] * 7 + [far] * 6,
-        out_specs=(near,) * 9,
+        out_specs=(near,) * 13,
         out_shape=(
             struct(own, width), struct(sub, width), struct(sub, width),
             struct(total, hidden_units), struct(total, hidden_units), struct(total, half), struct(total, half),
             struct(count, width, dtype=F32), struct(total, EXT),
-        ),
-        scratch_shapes=[map_room] * 6
+        )
+        + (struct(hidden_units, half),) * 4,
+        scratch_shapes=[map_room] * 2
         + [pltpu.VMEM((total, half), BF16)] * 2
         + [pltpu.VMEM((total, hidden_units), BF16)]
         + [pltpu.SemaphoreType.DMA((len(tiles_of(hidden_units, TILE)), 6))],
@@ -358,24 +344,23 @@
     )(meta, rows_own, x_other, flat_cot, cot_other, extra_own, extra_other, gain_row, *maps)
     mix_a, mix_b = up_x(mix_a), down_x(mix_b)
     grad_own, grad_a, grad_b, sums = pl.pallas_call(
-        functools.partial(backward_kernel, BACK_TILE),
-        in_specs=[scalar] + [near] * 6 + [far] * 4,
+        backward_kernel,
+        in_specs=[scalar] + [near] * 10,
         out_specs=(near,) * 4,
         out_shape=(
-            struct(own, width + EXT), struct(sub, width + EXT), struct(sub, width + EXT), struct(2 * count, width),
+            struct(own, width + EXT), struct(sub, width + EXT), struct(sub, width + EXT),
+            struct(2 * count, width, dtype=F32),
         ),
-        scratch_shapes=[map_room] * 4 + [pltpu.SemaphoreType.DMA((2, half // BACK_TILE, 2))],
-        compiler_params=params(EXPERT_VMEM),
+        compiler_params=params(BACK_VMEM),
         cost_estimate=pl.CostEstimate(flops=1_000_000_000_000, bytes_accessed=1024, transcendentals=0),
-    )(meta, dgate, dup, r_0, r_1, routing, ends, *maps[:4])
-    mix_a, mix_b, grad_a, grad_b, sums = lax.optimization_barrier((mix_a, mix_b, grad_a, grad_b, sums))
+    )(meta, dgate, dup, r_0, r_1, routing, ends, *held)
+    mix_a, mix_b, grad_a, grad_b = lax.optimization_barrier((mix_a, mix_b, grad_a, grad_b))
     grad_a, grad_b = up_x(grad_a), down_x(grad_b)
-    core = other_core(sums)
+    sums = (sums + other_core(sums)).astype(BF16)
     across = lax.ppermute(sums, "expert", [(0, 1), (1, 0)])
-    diagonal = lax.ppermute(sums, ("section", "expert"), [(0, 3), (1, 2), (2, 1), (3, 0)])
     packed = pl.pallas_call(
         pack_kernel, out_shape=struct(2, own, width + EXT), compiler_params=params()
-    )(mix_own, mix_a, mix_b, grad_own, grad_a, grad_b, sums, core, across, diagonal)
+    )(mix_own, mix_a, mix_b, grad_own, grad_a, grad_b, sums, across)
     rows_each = 2 * own // n_dp
     chunks = lax.all_to_all(packed.reshape(n_dp, rows_each, width + EXT), "dp", 0, 0, tiled=True)
 

time: 107 us -> 102 us (0.953)
  Pallas kernels: 22.5 us -> 18.3 us
    ppermute x1, waiting for transfers between devices: 2.43 us -> 5.37 us  [shards(): across = lax.ppermute(sums, 'expert', [(0, 1), (1, 0)])]
    ppermute x1 -> x0, waiting for transfers between devices: 2.59 us -> none  [shards(): lax.ppermute(sums, ('section', 'expert'), [(0, 3), (1, 2), (2, 1), (3, 0)])]
    pallas_call x1, Pallas kernels: 4.86 us -> 2.88 us  [shards(): pl.pallas_call(backward_kernel, in_specs=[scalar] + [near] * 10, out_spec...]
    pallas_call x1, Pallas kernels: 3.07 us -> 1.22 us  [shards(): pl.pallas_call(prologue_kernel, out_shape=(struct(own, width), struct(own...]
    all_to_all x1, waiting for transfers between devices: 19.2 us -> 17.4 us  [shards(): lax.all_to_all(packed.reshape(n_dp, rows_each, width + EXT), 'dp', 0, 0,...]
    ppermute x4, starting transfers between devices: 2.45 us -> 0.76 us  [other_core(): return lax.ppermute(array, 'section', [(0, 1), (1, 0)])]
    unnamed x25 -> x21, local copies, waits for them, and re-layouts: 3.95 us -> 4.03 us
  transfers between devices with their start and end apart: 14 -> 13, of which waited for: 5 -> 4; matrix products, arithmetic and copies ran while one was open for 1% -> 1% of each run, Pallas kernels for 7% -> 4%
where the time goes in v4:
time: 102 us; the launch traced here: 101 us
  waiting for transfers between devices  31.7 us (31%)
  starting transfers between devices  24 us (24%)
  blocking collectives  22.2 us (22%)
  Pallas kernels  18.3 us (18%)
  local copies, waits for them, and re-layouts  4.03 us (4%)
    all_to_all x1, blocking collectives, shards(): gathered = lax.all_to_all(finished, 'dp', 0, 0, tiled=True)  22.2 us
    all_to_all x1, waiting for transfers between devices, shards(): lax.all_to_all(packed.reshape(n_dp, rows_each, width + EXT), 'dp', 0, 0,...  17.4 us
    all_to_all x1, starting transfers between devices, shards(): lax.all_to_all(packed.reshape(n_dp, rows_each, width + EXT), 'dp', 0, 0,...  11.8 us
    pallas_call x1, Pallas kernels, shards(): pl.pallas_call(functools.partial(forward_kernel, count, units, TILE), in_...  9.59 us
    ppermute x4, waiting for transfers between devices, up_x(): return lax.ppermute(array, ('expert', 'dp'), around(1))  8.88 us
    ppermute x3, starting transfers between devices, down_x(): return lax.ppermute(array, ('expert', 'dp'), around(3))  6.91 us
    ppermute x1, waiting for transfers between devices, shards(): across = lax.ppermute(sums, 'expert', [(0, 1), (1, 0)])  5.37 us
    ppermute x4, starting transfers between devices, up_x(): return lax.ppermute(array, ('expert', 'dp'), around(1))  4.45 us
  transfers between devices with their start and end apart: 13, of which 4 were waited for; matrix products, arithmetic and copies ran while one was open for 1% of the time, Pallas kernels for 4%

profile of v4, /device:TPU:0, one launch (start us, length us, event | category | flops | bytes accessed | tf_op | source)
XLA Modules:
  0.0 101.2 jit_solution(10286799284515191514)
XLA Ops:
  0.6 0.1 collective-permute-start.3
  0.7 1.6 %collective-permute-start = (bf16[128,2048]{1,0:T(8,128)(2,1)}, bf16[128,2048]{1,0:T(8,128)(2,1)S(1)}, u32[]{:S(2)}, u32[]{:S(2)}) collective-permute-start(bf16[128,2048]{1,0:T(8,128)(2,1)} %bitcast.20), channel_id=1, source_target_pairs={{0,32},{1,33},{2,34},{3,35},{4,36},{5,37},{6,38},{7,39},{8,40},{9,... | collective-permute-start | bytes 1572872 | tf_op jit(solution)/shard_map/ppermute | solution.py:294
  2.4 1.7 %collective-permute-start.1 = (bf16[128,2048]{1,0:T(8,128)(2,1)}, bf16[128,2048]{1,0:T(8,128)(2,1)S(1)}, u32[]{:S(2)}, u32[]{:S(2)}) collective-permute-start(bf16[128,2048]{1,0:T(8,128)(2,1)} %bitcast.23), channel_id=1, source_target_pairs={{0,33},{1,32},{2,35},{3,34},{4,37},{5,36},{6,39},{7,38},{8,41},{9,... | collective-permute-start | bytes 1572872 | tf_op jit(solution)/shard_map/ppermute | solution.py:297
  4.0 0.0 collective-permute-start.4
  4.0 0.8 copy.12
  4.8 0.6 collective-permute-start.5
  5.4 0.7 copy-done.9
  6.1 1.0 %copy-done = bf16[2,64,2048]{2,1,0:T(8,128)(2,1)S(1)} copy-done((bf16[2,64,2048]{2,1,0:T(8,128)(2,1)S(1)}, bf16[2,64,2048]{2,1,0:T(8,128)(2,1)}, u32[]{:S(2)}) %copy-start) | copy-done | bytes 524312
  7.1 0.8 copy-done.4
  8.0 0.7 copy-done.6
  8.7 1.2 %shard_map.111 = (bf16[128,2048]{1,0:T(8,128)(2,1)S(1)}, bf16[128,128]{1,0:T(8,128)(2,1)S(1)}, f32[128,128]{1,0:T(8,128)S(1)}) custom-call(bf16[128,2048]{1,0:T(8,128)(2,1)S(1)} %bitcast.21, f32[1,2048]{1,0:T(1,128)S(1)} %bitcast.31, f32[8,2048]{1,0:T(8,128)S(1)} %bitcast.26, s32[128,2]{1,0:T(8,128)S(1)} %bitcast.30), custom_call_target="tpu_custom_call" | custom-call | flops 20000000000 | bytes 33554432 | tf_op jit(solution)/shard_map/pallas_call | solution.py:313
  9.9 1.5 %collective-permute-start.2 = (bf16[128,128]{1,0:T(8,128)(2,1)S(1)}, bf16[128,128]{1,0:T(8,128)(2,1)S(1)}, u32[]{:S(2)}, u32[]{:S(2)}) collective-permute-start(bf16[128,128]{1,0:T(8,128)(2,1)S(1)} %get-tuple-element.35.extra_own), channel_id=1, source_target_pairs={{0,32},{1,33},{2,34},{3,35},{4,36},{5,37},{6,38},{7,39},{8,40},{9,... | collective-permute-start | bytes 98312 | tf_op jit(solution)/shard_map/ppermute | solution.py:294
  11.4 0.1 pad_add_fusion.1.meta
  11.5 5.7 %collective-permute-done.2.extra_other = bf16[128,128]{1,0:T(8,128)(2,1)S(1)} collective-permute-done((bf16[128,128]{1,0:T(8,128)(2,1)S(1)}, bf16[128,128]{1,0:T(8,128)(2,1)S(1)}, u32[]{:S(2)}, u32[]{:S(2)}) %collective-permute-start.2) | collective-permute-done | bytes 32800 | tf_op jit(solution)/shard_map/ppermute | solution.py:294
  17.2 0.0 collective-permute-done.1.cot_other
  17.2 9.6 %shard_map.112 = (bf16[128,2048]{1,0:T(8,128)(2,1)S(1)}, bf16[64,2048]{1,0:T(8,128)(2,1)}, bf16[64,2048]{1,0:T(8,128)(2,1)}, bf16[256,896]{1,0:T(8,128)(2,1)S(1)...) custom-call(s32[2]{0:T(128)S(1)} %pad_add_fusion.1.meta, ...), custom_call_target="tpu_custom_call" | custom-call | flops 1999999991808 | bytes 1024 | tf_op jit(solution)/shard_map/pallas_call | solution.py:328
  26.8 0.9 collective-permute-start.6
  27.8 2.4 %collective-permute-start.7 = (bf16[64,2048]{1,0:T(8,128)(2,1)}, bf16[64,2048]{1,0:T(8,128)(2,1)}, u32[]{:S(2)}, u32[]{:S(2)}) collective-permute-start(bf16[64,2048]{1,0:T(8,128)(2,1)} %get-tuple-element.40), channel_id=1, source_target_pairs={{0,33},{1,32},{2,35},{3,34},{4,37},{5,36},{6,39},{7,38},{8,41},{9,... | collective-permute-start | bytes 786440 | tf_op jit(solution)/shard_map/ppermute | solution.py:297
  30.1 2.9 %shard_map.113 = (bf16[128,2176]{1,0:T(8,128)(2,1)S(1)}, bf16[64,2176]{1,0:T(8,128)(2,1)S(1)}, bf16[64,2176]{1,0:T(8,128)(2,1)S(1)}, f32[16,2048]{1,0:T(8,128)S(1)}) custom-call(s32[2]{0:T(128)S(1)} %pad_add_fusion.1.meta, bf16[256,896]{1,0:T(8,128)(2,1)S(1)} %get-tuple-element.41.dgate, bf16[256,896]{1,0:T(8,128)(2,1)S(1)} %get-tuple-element.42.dup, ...), custom_call_target="tpu_custom_call" | custom-call | flops 999999995904 | bytes 1024 | tf_op jit(solution)/shard_map/pallas_call | solution.py:346
  33.0 0.1 collective-permute-start.10
  33.1 3.2 %collective-permute-done.6.mix_a = bf16[64,2048]{1,0:T(8,128)(2,1)} collective-permute-done((bf16[64,2048]{1,0:T(8,128)(2,1)}, bf16[64,2048]{1,0:T(8,128)(2,1)}, u32[]{:S(2)}, u32[]{:S(2)}) %collective-permute-start.6) | collective-permute-done | bytes 262176 | tf_op jit(solution)/shard_map/ppermute | solution.py:294
  36.3 0.4 collective-permute-start.8
  36.7 2.9 %collective-permute-start.9 = (bf16[64,2176]{1,0:T(8,128)(2,1)S(1)}, bf16[64,2176]{1,0:T(8,128)(2,1)S(1)}, u32[]{:S(2)}, u32[]{:S(2)}) collective-permute-start(bf16[64,2176]{1,0:T(8,128)(2,1)S(1)} %get-tuple-element.57), channel_id=1, source_target_pairs={{0,33},{1,32},{2,35},{3,34},{4,37},{5,36},{6,39},{7,38},{8,41},{9,... | collective-permute-start | bytes 835592 | tf_op jit(solution)/shard_map/ppermute | solution.py:297
  39.6 0.1 collective-permute-start.11
  39.6 5.4 %collective-permute-done.11.sums_across = bf16[16,2048]{1,0:T(8,128)(2,1)S(1)} collective-permute-done((bf16[16,2048]{1,0:T(8,128)(2,1)S(1)}, bf16[16,2048]{1,0:T(8,128)(2,1)S(1)}, u32[]{:S(2)}, u32[]{:S(2)}) %collective-permute-start.11) | collective-permute-done | bytes 65568 | tf_op jit(solution)/shard_map/ppermute | solution.py:360
  45.0 2.6 %shard_map.114 = bf16[2,128,2176]{2,1,0:T(8,128)(2,1)} custom-call(bf16[128,2048]{1,0:T(8,128)(2,1)S(1)} %get-tuple-element.38.mix_own, bf16[64,2048]{1,0:T(8,128)(2,1)} %collective-permute-done.6.mix_a, bf16[64,2048]{1,0:T(8,128)(2,1)} %collective-permute-done.7.mix_b, bf16[128,2176]{1,0:T(8,128)(2,1)S(1)} %get-tuple-element.55.grad_own, ...), custom_call_target="tpu_custom_call" | custom-call | tf_op jit(solution)/shard_map/pallas_call | solution.py:361
  47.6 11.8 %all-to-all-start = ((bf16[32,8,2176]{2,1,0:T(8,128)(2,1)}), bf16[32,8,2176]{2,1,0:T(8,128)(2,1)S(1)}, u32[]{:S(2)}, u32[]{:S(2)}) async-start(bf16[32,8,2176]{2,1,0:T(8,128)(2,1)} %bitcast.12), calls=%async_computation | async-start | bytes 2228224 | tf_op jit(solution)/shard_map/all_to_all | solution.py:365
  59.4 0.1 pad_add_fusion.meta
  59.5 17.4 %all-to-all-done.parts_ref = bf16[32,8,2176]{2,1,0:T(8,128)(2,1)S(1)} async-done(((bf16[32,8,2176]{2,1,0:T(8,128)(2,1)}), bf16[32,8,2176]{2,1,0:T(8,128)(2,1)S(1)}, u32[]{:S(2)}, u32[]{:S(2)}) %all-to-all-start) | async-done | bytes 1114144 | tf_op jit(solution)/shard_map/all_to_all | solution.py:365
  76.9 1.0 %shard_map.115 = bf16[32,8,2176]{2,1,0:T(8,128)(2,1)S(1)} custom-call(s32[2]{0:T(128)S(1)} %pad_add_fusion.meta, bf16[32,8,2176]{2,1,0:T(8,128)(2,1)S(1)} %all-to-all-done.parts_ref, bf16[16,8,2048]{2,1,0:T(8,128)(2,1)S(1)} %bitcast.22, bf16[16,8,2048]{2,1,0:T(8,128)(2,1)S(1)} %bitcast.25, f32[16,8,128]{2,1,0:T(8,128)S(1)} %bitcast.29, ...), custom_call_target="tpu_custom_call" | custom-call | tf_op jit(solution)/shard_map/pallas_call | solution.py:373
  78.0 22.2 %all_to_all.10.all_ref = bf16[32,8,2176]{2,1,0:T(8,128)(2,1)S(1)} all-to-all(bf16[32,8,2176]{2,1,0:T(8,128)(2,1)S(1)} %shard_map.115), channel_id=1, replica_groups=mesh['section'=2,'expert'=2,'dp'=32] {'dp'}, dimensions={0} | all-to-all | bytes 2228224 | tf_op jit(solution)/shard_map/all_to_all | solution.py:392
  100.2 1.0 %shard_map.116 = (bf16[16,8,2048]{2,1,0:T(8,128)(2,1)}, bf16[16,8,2048]{2,1,0:T(8,128)(2,1)}, f32[8,2048]{1,0:T(8,128)}, f32[1,2048]{1,0:T(1,128)}) custom-call(bf16[32,8,2176]{2,1,0:T(8,128)(2,1)S(1)} %all_to_all.10.all_ref, f32[1,2048]{1,0:T(1,128)S(1)} %bitcast.34, f32[8,2048]{1,0:T(8,128)S(1)} %bitcast.28), custom_call_target="tpu_custom_call" | custom-call | tf_op jit(solution)/shard_map/pallas_call | solution.py:394
  (25 shorter events, 0.1 us)
Async XLA Ops:
  0.6 4.2 %collective-permute-start.3 = (bf16[896,1024]{1,0:T(8,128)(2,1)}, bf16[896,1024]{1,0:T(8,128)(2,1)S(1)}, u32[]{:S(2)}, u32[]{:S(2)}) collective-permute-start(bf16[896,1024]{1,0:T(8,128)(2,1)} %bitcast.35), channel_id=1, source_target_pairs={{0,64},{64,0},{1,65},{65,1},{2,66},{66,2},{3,67},{67,3},{4,68},{68... | collective-permute-start | bytes 5505032 | tf_op jit(solution)/shard_map/ppermute | solution.py:300
  0.7 16.5 %collective-permute-start = (bf16[128,2048]{1,0:T(8,128)(2,1)}, bf16[128,2048]{1,0:T(8,128)(2,1)S(1)}, u32[]{:S(2)}, u32[]{:S(2)}) collective-permute-start(bf16[128,2048]{1,0:T(8,128)(2,1)} %bitcast.20), channel_id=1, source_target_pairs={{0,32},{1,33},{2,34},{3,35},{4,36},{5,37},{6,38},{7,39},{8,40},{9,... | collective-permute-start | bytes 1572872 | tf_op jit(solution)/shard_map/ppermute | solution.py:294
  2.4 14.8 %collective-permute-start.1 = (bf16[128,2048]{1,0:T(8,128)(2,1)}, bf16[128,2048]{1,0:T(8,128)(2,1)S(1)}, u32[]{:S(2)}, u32[]{:S(2)}) collective-permute-start(bf16[128,2048]{1,0:T(8,128)(2,1)} %bitcast.23), channel_id=1, source_target_pairs={{0,33},{1,32},{2,35},{3,34},{4,37},{5,36},{6,39},{7,38},{8,41},{9,... | collective-permute-start | bytes 1572872 | tf_op jit(solution)/shard_map/ppermute | solution.py:297
  4.0 13.2 %collective-permute-start.4 = (bf16[896,1024]{1,0:T(8,128)(2,1)}, bf16[896,1024]{1,0:T(8,128)(2,1)}, u32[]{:S(2)}, u32[]{:S(2)}) collective-permute-start(bf16[896,1024]{1,0:T(8,128)(2,1)} %bitcast.37), channel_id=1, source_target_pairs={{0,64},{64,0},{1,65},{65,1},{2,66},{66,2},{3,67},{67,3},{4,68},{68... | collective-permute-start | bytes 5505032 | tf_op jit(solution)/shard_map/ppermute | solution.py:300
  4.8 1.3 %copy-start.9 = (bf16[896,1024]{1,0:T(8,128)(2,1)}, bf16[896,1024]{1,0:T(8,128)(2,1)S(1)}, u32[]{:S(2)}) copy-start(bf16[896,1024]{1,0:T(8,128)(2,1)S(1)} %collective-permute-done.3.gate_1) | copy-start | bytes 5505028
  4.8 12.4 %collective-permute-start.5 = (bf16[896,1024]{1,0:T(8,128)(2,1)}, bf16[896,1024]{1,0:T(8,128)(2,1)}, u32[]{:S(2)}, u32[]{:S(2)}) collective-permute-start(bf16[896,1024]{1,0:T(8,128)(2,1)} %bitcast.39), channel_id=1, source_target_pairs={{0,64},{64,0},{1,65},{65,1},{2,66},{66,2},{3,67},{67,3},{4,68},{68... | collective-permute-start | bytes 5505032 | tf_op jit(solution)/shard_map/ppermute | solution.py:300
  6.1 1.0 %copy-start = (bf16[2,64,2048]{2,1,0:T(8,128)(2,1)S(1)}, bf16[2,64,2048]{2,1,0:T(8,128)(2,1)}, u32[]{:S(2)}) copy-start(bf16[2,64,2048]{2,1,0:T(8,128)(2,1)} %param.8) | copy-start | bytes 1572868
  7.1 0.8 copy-start.4
  8.0 0.7 copy-start.6
  8.7 8.6 %copy-start.2 = (bf16[2,64,2048]{2,1,0:T(8,128)(2,1)S(1)}, bf16[2,64,2048]{2,1,0:T(8,128)(2,1)}, u32[]{:S(2)}) copy-start(bf16[2,64,2048]{2,1,0:T(8,128)(2,1)} %param.9) | copy-start | bytes 1572868
  8.7 8.6 %copy-start.7 = (f32[2048]{0:T(1024)S(1)}, f32[2048]{0:T(1024)}, u32[]{:S(2)}) copy-start(f32[2048]{0:T(1024)} %param.14) | copy-start | bytes 24580
  9.9 7.3 %collective-permute-start.2 = (bf16[128,128]{1,0:T(8,128)(2,1)S(1)}, bf16[128,128]{1,0:T(8,128)(2,1)S(1)}, u32[]{:S(2)}, u32[]{:S(2)}) collective-permute-start(bf16[128,128]{1,0:T(8,128)(2,1)S(1)} %get-tuple-element.35.extra_own), channel_id=1, source_target_pairs={{0,32},{1,33},{2,34},{3,35},{4,36},{5,37},{6,38},{7,39},{8,40},{9,... | collective-permute-start | bytes 98312 | tf_op jit(solution)/shard_map/ppermute | solution.py:294
  26.8 9.5 %collective-permute-start.6 = (bf16[64,2048]{1,0:T(8,128)(2,1)}, bf16[64,2048]{1,0:T(8,128)(2,1)}, u32[]{:S(2)}, u32[]{:S(2)}) collective-permute-start(bf16[64,2048]{1,0:T(8,128)(2,1)} %get-tuple-element.39), channel_id=1, source_target_pairs={{0,32},{1,33},{2,34},{3,35},{4,36},{5,37},{6,38},{7,39},{8,40},{9,... | collective-permute-start | bytes 786440 | tf_op jit(solution)/shard_map/ppermute | solution.py:294
  27.8 8.5 %collective-permute-start.7 = (bf16[64,2048]{1,0:T(8,128)(2,1)}, bf16[64,2048]{1,0:T(8,128)(2,1)}, u32[]{:S(2)}, u32[]{:S(2)}) collective-permute-start(bf16[64,2048]{1,0:T(8,128)(2,1)} %get-tuple-element.40), channel_id=1, source_target_pairs={{0,33},{1,32},{2,35},{3,34},{4,37},{5,36},{6,39},{7,38},{8,41},{9,... | collective-permute-start | bytes 786440 | tf_op jit(solution)/shard_map/ppermute | solution.py:297
  33.0 6.5 %collective-permute-start.10 = (f32[16,2048]{1,0:T(8,128)S(1)}, f32[16,2048]{1,0:T(8,128)S(1)}, u32[]{:S(2)}, u32[]{:S(2)}) collective-permute-start(f32[16,2048]{1,0:T(8,128)S(1)} %get-tuple-element.58), channel_id=1, source_target_pairs={{0,64},{64,0},{1,65},{65,1},{2,66},{66,2},{3,67},{67,3},{4,68},{68... | collective-permute-start | bytes 393224 | tf_op jit(solution)/shard_map/ppermute | solution.py:300
  36.3 8.7 %collective-permute-start.8 = (bf16[64,2176]{1,0:T(8,128)(2,1)S(1)}, bf16[64,2176]{1,0:T(8,128)(2,1)S(1)}, u32[]{:S(2)}, u32[]{:S(2)}) collective-permute-start(bf16[64,2176]{1,0:T(8,128)(2,1)S(1)} %get-tuple-element.56), channel_id=1, source_target_pairs={{0,32},{1,33},{2,34},{3,35},{4,36},{5,37},{6,38},{7,39},{8,40},{9,... | collective-permute-start | bytes 835592 | tf_op jit(solution)/shard_map/ppermute | solution.py:294
  36.7 8.4 %collective-permute-start.9 = (bf16[64,2176]{1,0:T(8,128)(2,1)S(1)}, bf16[64,2176]{1,0:T(8,128)(2,1)S(1)}, u32[]{:S(2)}, u32[]{:S(2)}) collective-permute-start(bf16[64,2176]{1,0:T(8,128)(2,1)S(1)} %get-tuple-element.57), channel_id=1, source_target_pairs={{0,33},{1,32},{2,35},{3,34},{4,37},{5,36},{6,39},{7,38},{8,41},{9,... | collective-permute-start | bytes 835592 | tf_op jit(solution)/shard_map/ppermute | solution.py:297
  39.6 5.5 %collective-permute-start.11 = (bf16[16,2048]{1,0:T(8,128)(2,1)S(1)}, bf16[16,2048]{1,0:T(8,128)(2,1)S(1)}, u32[]{:S(2)}, u32[]{:S(2)}) collective-permute-start(bf16[16,2048]{1,0:T(8,128)(2,1)S(1)} %add_convert_fusion.sums_own), channel_id=1, source_target_pairs={{0,32},{32,0},{1,33},{33,1},{2,34},{34,2},{3,35},{35,3},{4,36},{36... | collective-permute-start | bytes 196616 | tf_op jit(solution)/shard_map/ppermute | solution.py:360
  47.6 29.3 %copy-start.1 = (bf16[2,64,2048]{2,1,0:T(8,128)(2,1)S(1)}, bf16[2,64,2048]{2,1,0:T(8,128)(2,1)}, u32[]{:S(2)}) copy-start(bf16[2,64,2048]{2,1,0:T(8,128)(2,1)} %param.8) | copy-start | bytes 1572868
  47.6 29.3 %copy-start.3 = (bf16[2,64,2048]{2,1,0:T(8,128)(2,1)S(1)}, bf16[2,64,2048]{2,1,0:T(8,128)(2,1)}, u32[]{:S(2)}) copy-start(bf16[2,64,2048]{2,1,0:T(8,128)(2,1)} %param.9) | copy-start | bytes 1572868
  47.6 29.3 %copy-start.5 = (f32[2048,8]{0,1:T(8,128)S(1)}, f32[2048,8]{0,1:T(8,128)}, u32[]{:S(2)}) copy-start(f32[2048,8]{0,1:T(8,128)} %param.13) | copy-start | bytes 196612
  47.6 29.3 %copy-start.8 = (f32[2048]{0:T(1024)S(1)}, f32[2048]{0:T(1024)}, u32[]{:S(2)}) copy-start(f32[2048]{0:T(1024)} %param.14) | copy-start | bytes 24580
  47.6 29.3 %all-to-all-start = ((bf16[32,8,2176]{2,1,0:T(8,128)(2,1)}), bf16[32,8,2176]{2,1,0:T(8,128)(2,1)S(1)}, u32[]{:S(2)}, u32[]{:S(2)}) async-start(bf16[32,8,2176]{2,1,0:T(8,128)(2,1)} %bitcast.12), calls=%async_computation | async-start | bytes 2228224 | tf_op jit(solution)/shard_map/all_to_all | solution.py:365

commit v5 on v4

--- a/solution.py
+++ b/solution.py
@@ -100,7 +100,7 @@
             group.append(copy)
         return group
 
-    copies = [fetch(0), fetch(1)]
+    copies = [fetch(number) for number in range(len(tiles))]
     scaling = inverse_rms(x_other[...].astype(F32))
     for at, r, c in ((at_0, r_0, c_0), (at_1, r_1, c_1)):
         there = pl.ds(at, half)
@@ -120,8 +120,6 @@
         signs.append(jnp.sum(jnp.where(lane == expert + 2 * count, extra, 0.0), axis=1, keepdims=True))
 
     def products(number):
-        if number + 2 < len(tiles):
-            copies.append(fetch(number + 2))
         for copy in copies[number]:
             copy.wait()
         start, size = tiles[number]
@@ -352,7 +350,7 @@
             struct(2 * count, width, dtype=F32),
         ),
         compiler_params=params(BACK_VMEM),
-        cost_estimate=pl.CostEstimate(flops=1_000_000_000_000, bytes_accessed=1024, transcendentals=0),
+        cost_estimate=pl.CostEstimate(flops=20_000_000_000, bytes_accessed=1024, transcendentals=0),
     )(meta, dgate, dup, r_0, r_1, routing, ends, *held)
     mix_a, mix_b, grad_a, grad_b = lax.optimization_barrier((mix_a, mix_b, grad_a, grad_b))
     grad_a, grad_b = up_x(grad_a), down_x(grad_b)

time: 102 us -> 99.6 us (0.976)
  Pallas kernels: 18.3 us -> 16.6 us
    unnamed x21 -> x15, local copies, waits for them, and re-layouts: 4.03 us -> 3.37 us
where the time goes in v5:
time: 99.6 us; the launch traced here: 99.1 us
  waiting for transfers between devices  32.3 us (32%)
  starting transfers between devices  23.7 us (24%)
  blocking collectives  22.2 us (22%)
  Pallas kernels  16.6 us (17%)
  local copies, waits for them, and re-layouts  3.37 us (3%)
    all_to_all x1, blocking collectives, shards(): gathered = lax.all_to_all(finished, 'dp', 0, 0, tiled=True)  22.2 us
    all_to_all x1, waiting for transfers between devices, shards(): lax.all_to_all(packed.reshape(n_dp, rows_each, width + EXT), 'dp', 0, 0,...  17.4 us
    all_to_all x1, starting transfers between devices, shards(): lax.all_to_all(packed.reshape(n_dp, rows_each, width + EXT), 'dp', 0, 0,...  11.8 us
    ppermute x4, waiting for transfers between devices, up_x(): return lax.ppermute(array, ('expert', 'dp'), around(1))  9.54 us
    pallas_call x1, Pallas kernels, shards(): pl.pallas_call(functools.partial(forward_kernel, count, units, TILE), in_...  8.84 us
    ppermute x3, starting transfers between devices, down_x(): return lax.ppermute(array, ('expert', 'dp'), around(3))  6.92 us
    ppermute x1, waiting for transfers between devices, shards(): across = lax.ppermute(sums, 'expert', [(0, 1), (1, 0)])  5.37 us
    ppermute x4, starting transfers between devices, up_x(): return lax.ppermute(array, ('expert', 'dp'), around(1))  4.15 us
  transfers between devices with their start and end apart: 13, of which 4 were waited for; matrix products, arithmetic and copies ran while one was open for 1% of the time, Pallas kernels for 4%

profile of v5, /device:TPU:0, one launch (start us, length us, event | category | flops | bytes accessed | tf_op | source)
XLA Modules:
  0.0 99.1 jit_solution(11820778990886545549)
XLA Ops:
  0.6 0.1 collective-permute-start.3
  0.7 1.6 %collective-permute-start = (bf16[128,2048]{1,0:T(8,128)(2,1)}, bf16[128,2048]{1,0:T(8,128)(2,1)S(1)}, u32[]{:S(2)}, u32[]{:S(2)}) collective-permute-start(bf16[128,2048]{1,0:T(8,128)(2,1)} %bitcast.20), channel_id=1, source_target_pairs={{0,32},{1,33},{2,34},{3,35},{4,36},{5,37},{6,38},{7,39},{8,40},{9,... | collective-permute-start | bytes 1572872 | tf_op jit(solution)/shard_map/ppermute | solution.py:292
  2.4 1.7 %collective-permute-start.1 = (bf16[128,2048]{1,0:T(8,128)(2,1)}, bf16[128,2048]{1,0:T(8,128)(2,1)S(1)}, u32[]{:S(2)}, u32[]{:S(2)}) collective-permute-start(bf16[128,2048]{1,0:T(8,128)(2,1)} %bitcast.23), channel_id=1, source_target_pairs={{0,33},{1,32},{2,35},{3,34},{4,37},{5,36},{6,39},{7,38},{8,41},{9,... | collective-permute-start | bytes 1572872 | tf_op jit(solution)/shard_map/ppermute | solution.py:295
  4.0 0.0 collective-permute-start.4
  4.0 0.8 copy.12
  4.8 0.0 collective-permute-done.3.gate_1
  4.8 0.6 collective-permute-start.5
  5.4 1.0 %copy-done = bf16[2,64,2048]{2,1,0:T(8,128)(2,1)S(1)} copy-done((bf16[2,64,2048]{2,1,0:T(8,128)(2,1)S(1)}, bf16[2,64,2048]{2,1,0:T(8,128)(2,1)}, u32[]{:S(2)}) %copy-start) | copy-done | bytes 524312
  6.5 0.8 copy-done.3
  7.3 0.7 copy-done.5
  8.0 1.2 %shard_map.111 = (bf16[128,2048]{1,0:T(8,128)(2,1)S(1)}, bf16[128,128]{1,0:T(8,128)(2,1)S(1)}, f32[128,128]{1,0:T(8,128)S(1)}) custom-call(bf16[128,2048]{1,0:T(8,128)(2,1)S(1)} %bitcast.21, f32[1,2048]{1,0:T(1,128)S(1)} %bitcast.31, f32[8,2048]{1,0:T(8,128)S(1)} %bitcast.26, s32[128,2]{1,0:T(8,128)S(1)} %bitcast.30), custom_call_target="tpu_custom_call" | custom-call | flops 20000000000 | bytes 33554432 | tf_op jit(solution)/shard_map/pallas_call | solution.py:311
  9.2 1.2 %collective-permute-start.2 = (bf16[128,128]{1,0:T(8,128)(2,1)S(1)}, bf16[128,128]{1,0:T(8,128)(2,1)S(1)}, u32[]{:S(2)}, u32[]{:S(2)}) collective-permute-start(bf16[128,128]{1,0:T(8,128)(2,1)S(1)} %get-tuple-element.35.extra_own), channel_id=1, source_target_pairs={{0,32},{1,33},{2,34},{3,35},{4,36},{5,37},{6,38},{7,39},{8,40},{9,... | collective-permute-start | bytes 98312 | tf_op jit(solution)/shard_map/ppermute | solution.py:292
  10.4 0.1 pad_add_fusion.1.meta
  10.5 6.7 %collective-permute-done.2.extra_other = bf16[128,128]{1,0:T(8,128)(2,1)S(1)} collective-permute-done((bf16[128,128]{1,0:T(8,128)(2,1)S(1)}, bf16[128,128]{1,0:T(8,128)(2,1)S(1)}, u32[]{:S(2)}, u32[]{:S(2)}) %collective-permute-start.2) | collective-permute-done | bytes 32800 | tf_op jit(solution)/shard_map/ppermute | solution.py:292
  17.2 0.0 collective-permute-done.1.cot_other
  17.2 8.8 %shard_map.112 = (bf16[128,2048]{1,0:T(8,128)(2,1)S(1)}, bf16[64,2048]{1,0:T(8,128)(2,1)S(1)}, bf16[64,2048]{1,0:T(8,128)(2,1)S(1)}, bf16[256,896]{1,0:T(8,128)(...) custom-call(s32[2]{0:T(128)S(1)} %pad_add_fusion.1.meta, ...), custom_call_target="tpu_custom_call" | custom-call | flops 1999999991808 | bytes 1024 | tf_op jit(solution)/shard_map/pallas_call | solution.py:326
  26.1 0.9 collective-permute-start.6
  27.0 2.4 %collective-permute-start.7 = (bf16[64,2048]{1,0:T(8,128)(2,1)S(1)}, bf16[64,2048]{1,0:T(8,128)(2,1)S(1)}, u32[]{:S(2)}, u32[]{:S(2)}) collective-permute-start(bf16[64,2048]{1,0:T(8,128)(2,1)S(1)} %get-tuple-element.40), channel_id=1, source_target_pairs={{0,33},{1,32},{2,35},{3,34},{4,37},{5,36},{6,39},{7,38},{8,41},{9,... | collective-permute-start | bytes 786440 | tf_op jit(solution)/shard_map/ppermute | solution.py:295
  29.4 2.9 %shard_map.113 = (bf16[128,2176]{1,0:T(8,128)(2,1)S(1)}, bf16[64,2176]{1,0:T(8,128)(2,1)S(1)}, bf16[64,2176]{1,0:T(8,128)(2,1)S(1)}, f32[16,2048]{1,0:T(8,128)S(1)}) custom-call(s32[2]{0:T(128)S(1)} %pad_add_fusion.1.meta, bf16[256,896]{1,0:T(8,128)(2,1)S(1)} %get-tuple-element.41.dgate, bf16[256,896]{1,0:T(8,128)(2,1)S(1)} %get-tuple-element.42.dup, ...), custom_call_target="tpu_custom_call" | custom-call | flops 20000000000 | bytes 1024 | tf_op jit(solution)/shard_map/pallas_call | solution.py:344
  32.3 0.1 collective-permute-start.10
  32.4 2.9 %collective-permute-done.6.mix_a = bf16[64,2048]{1,0:T(8,128)(2,1)S(1)} collective-permute-done((bf16[64,2048]{1,0:T(8,128)(2,1)S(1)}, bf16[64,2048]{1,0:T(8,128)(2,1)S(1)}, u32[]{:S(2)}, u32[]{:S(2)}) %collective-permute-start.6) | collective-permute-done | bytes 262176 | tf_op jit(solution)/shard_map/ppermute | solution.py:292
  35.2 0.4 collective-permute-start.8
  35.6 2.9 %collective-permute-start.9 = (bf16[64,2176]{1,0:T(8,128)(2,1)S(1)}, bf16[64,2176]{1,0:T(8,128)(2,1)S(1)}, u32[]{:S(2)}, u32[]{:S(2)}) collective-permute-start(bf16[64,2176]{1,0:T(8,128)(2,1)S(1)} %get-tuple-element.57), channel_id=1, source_target_pairs={{0,33},{1,32},{2,35},{3,34},{4,37},{5,36},{6,39},{7,38},{8,41},{9,... | collective-permute-start | bytes 835592 | tf_op jit(solution)/shard_map/ppermute | solution.py:295
  38.5 0.1 collective-permute-start.11
  38.6 5.4 %collective-permute-done.11.sums_across = bf16[16,2048]{1,0:T(8,128)(2,1)S(1)} collective-permute-done((bf16[16,2048]{1,0:T(8,128)(2,1)S(1)}, bf16[16,2048]{1,0:T(8,128)(2,1)S(1)}, u32[]{:S(2)}, u32[]{:S(2)}) %collective-permute-start.11) | collective-permute-done | bytes 65568 | tf_op jit(solution)/shard_map/ppermute | solution.py:358
  44.0 1.5 %shard_map.114 = bf16[2,128,2176]{2,1,0:T(8,128)(2,1)} custom-call(bf16[128,2048]{1,0:T(8,128)(2,1)S(1)} %get-tuple-element.38.mix_own, bf16[64,2048]{1,0:T(8,128)(2,1)S(1)} %collective-permute-done.6.mix_a, bf16[64,2048]{1,0:T(8,128)(2,1)S(1)} %collective-permute-done.7.mix_b, bf16[128,2176]{1,0:T(8,128)(2,1)S(1)} %get-tuple-element.55.grad_own, ...), custom_call_target="tpu_custom_call" | custom-call | tf_op jit(solution)/shard_map/pallas_call | solution.py:359
  45.5 11.8 %all-to-all-start = ((bf16[32,8,2176]{2,1,0:T(8,128)(2,1)}), bf16[32,8,2176]{2,1,0:T(8,128)(2,1)S(1)}, u32[]{:S(2)}, u32[]{:S(2)}) async-start(bf16[32,8,2176]{2,1,0:T(8,128)(2,1)} %bitcast.12), calls=%async_computation | async-start | bytes 2228224 | tf_op jit(solution)/shard_map/all_to_all | solution.py:363
  57.3 0.1 pad_add_fusion.meta
  57.4 17.4 %all-to-all-done.parts_ref = bf16[32,8,2176]{2,1,0:T(8,128)(2,1)S(1)} async-done(((bf16[32,8,2176]{2,1,0:T(8,128)(2,1)}), bf16[32,8,2176]{2,1,0:T(8,128)(2,1)S(1)}, u32[]{:S(2)}, u32[]{:S(2)}) %all-to-all-start) | async-done | bytes 1114144 | tf_op jit(solution)/shard_map/all_to_all | solution.py:363
  74.8 1.0 %shard_map.115 = bf16[32,8,2176]{2,1,0:T(8,128)(2,1)S(1)} custom-call(s32[2]{0:T(128)S(1)} %pad_add_fusion.meta, bf16[32,8,2176]{2,1,0:T(8,128)(2,1)S(1)} %all-to-all-done.parts_ref, bf16[16,8,2048]{2,1,0:T(8,128)(2,1)S(1)} %bitcast.22, bf16[16,8,2048]{2,1,0:T(8,128)(2,1)S(1)} %bitcast.25, f32[16,8,128]{2,1,0:T(8,128)S(1)} %bitcast.29, ...), custom_call_target="tpu_custom_call" | custom-call | tf_op jit(solution)/shard_map/pallas_call | solution.py:371
  75.9 22.2 %all_to_all.10.all_ref = bf16[32,8,2176]{2,1,0:T(8,128)(2,1)S(1)} all-to-all(bf16[32,8,2176]{2,1,0:T(8,128)(2,1)S(1)} %shard_map.115), channel_id=1, replica_groups=mesh['section'=2,'expert'=2,'dp'=32] {'dp'}, dimensions={0} | all-to-all | bytes 2228224 | tf_op jit(solution)/shard_map/all_to_all | solution.py:390
  98.1 1.0 %shard_map.116 = (bf16[16,8,2048]{2,1,0:T(8,128)(2,1)}, bf16[16,8,2048]{2,1,0:T(8,128)(2,1)}, f32[8,2048]{1,0:T(8,128)}, f32[1,2048]{1,0:T(1,128)}) custom-call(bf16[32,8,2176]{2,1,0:T(8,128)(2,1)S(1)} %all_to_all.10.all_ref, f32[1,2048]{1,0:T(1,128)S(1)} %bitcast.34, f32[8,2048]{1,0:T(8,128)S(1)} %bitcast.28), custom_call_target="tpu_custom_call" | custom-call | tf_op jit(solution)/shard_map/pallas_call | solution.py:392
  (19 shorter events, 0.1 us)
Async XLA Ops:
  0.6 4.2 %collective-permute-start.3 = (bf16[896,1024]{1,0:T(8,128)(2,1)}, bf16[896,1024]{1,0:T(8,128)(2,1)}, u32[]{:S(2)}, u32[]{:S(2)}) collective-permute-start(bf16[896,1024]{1,0:T(8,128)(2,1)} %bitcast.35), channel_id=1, source_target_pairs={{0,64},{64,0},{1,65},{65,1},{2,66},{66,2},{3,67},{67,3},{4,68},{68... | collective-permute-start | bytes 5505032 | tf_op jit(solution)/shard_map/ppermute | solution.py:298
  0.7 16.5 %collective-permute-start = (bf16[128,2048]{1,0:T(8,128)(2,1)}, bf16[128,2048]{1,0:T(8,128)(2,1)S(1)}, u32[]{:S(2)}, u32[]{:S(2)}) collective-permute-start(bf16[128,2048]{1,0:T(8,128)(2,1)} %bitcast.20), channel_id=1, source_target_pairs={{0,32},{1,33},{2,34},{3,35},{4,36},{5,37},{6,38},{7,39},{8,40},{9,... | collective-permute-start | bytes 1572872 | tf_op jit(solution)/shard_map/ppermute | solution.py:292
  2.4 14.8 %collective-permute-start.1 = (bf16[128,2048]{1,0:T(8,128)(2,1)}, bf16[128,2048]{1,0:T(8,128)(2,1)S(1)}, u32[]{:S(2)}, u32[]{:S(2)}) collective-permute-start(bf16[128,2048]{1,0:T(8,128)(2,1)} %bitcast.23), channel_id=1, source_target_pairs={{0,33},{1,32},{2,35},{3,34},{4,37},{5,36},{6,39},{7,38},{8,41},{9,... | collective-permute-start | bytes 1572872 | tf_op jit(solution)/shard_map/ppermute | solution.py:295
  4.0 13.2 %collective-permute-start.4 = (bf16[896,1024]{1,0:T(8,128)(2,1)}, bf16[896,1024]{1,0:T(8,128)(2,1)}, u32[]{:S(2)}, u32[]{:S(2)}) collective-permute-start(bf16[896,1024]{1,0:T(8,128)(2,1)} %bitcast.37), channel_id=1, source_target_pairs={{0,64},{64,0},{1,65},{65,1},{2,66},{66,2},{3,67},{67,3},{4,68},{68... | collective-permute-start | bytes 5505032 | tf_op jit(solution)/shard_map/ppermute | solution.py:298
  4.8 12.4 %collective-permute-start.5 = (bf16[896,1024]{1,0:T(8,128)(2,1)}, bf16[896,1024]{1,0:T(8,128)(2,1)}, u32[]{:S(2)}, u32[]{:S(2)}) collective-permute-start(bf16[896,1024]{1,0:T(8,128)(2,1)} %bitcast.39), channel_id=1, source_target_pairs={{0,64},{64,0},{1,65},{65,1},{2,66},{66,2},{3,67},{67,3},{4,68},{68... | collective-permute-start | bytes 5505032 | tf_op jit(solution)/shard_map/ppermute | solution.py:298
  5.4 1.0 %copy-start = (bf16[2,64,2048]{2,1,0:T(8,128)(2,1)S(1)}, bf16[2,64,2048]{2,1,0:T(8,128)(2,1)}, u32[]{:S(2)}) copy-start(bf16[2,64,2048]{2,1,0:T(8,128)(2,1)} %param.8) | copy-start | bytes 1572868
  6.5 0.8 copy-start.3
  7.3 0.7 copy-start.5
  8.0 9.2 %copy-start.2 = (bf16[2,64,2048]{2,1,0:T(8,128)(2,1)S(1)}, bf16[2,64,2048]{2,1,0:T(8,128)(2,1)}, u32[]{:S(2)}) copy-start(bf16[2,64,2048]{2,1,0:T(8,128)(2,1)} %param.9) | copy-start | bytes 1572868
  8.0 9.2 %copy-start.6 = (f32[2048]{0:T(1024)S(1)}, f32[2048]{0:T(1024)}, u32[]{:S(2)}) copy-start(f32[2048]{0:T(1024)} %param.14) | copy-start | bytes 24580
  9.2 8.0 %collective-permute-start.2 = (bf16[128,128]{1,0:T(8,128)(2,1)S(1)}, bf16[128,128]{1,0:T(8,128)(2,1)S(1)}, u32[]{:S(2)}, u32[]{:S(2)}) collective-permute-start(bf16[128,128]{1,0:T(8,128)(2,1)S(1)} %get-tuple-element.35.extra_own), channel_id=1, source_target_pairs={{0,32},{1,33},{2,34},{3,35},{4,36},{5,37},{6,38},{7,39},{8,40},{9,... | collective-permute-start | bytes 98312 | tf_op jit(solution)/shard_map/ppermute | solution.py:292
  26.1 9.1 %collective-permute-start.6 = (bf16[64,2048]{1,0:T(8,128)(2,1)S(1)}, bf16[64,2048]{1,0:T(8,128)(2,1)S(1)}, u32[]{:S(2)}, u32[]{:S(2)}) collective-permute-start(bf16[64,2048]{1,0:T(8,128)(2,1)S(1)} %get-tuple-element.39), channel_id=1, source_target_pairs={{0,32},{1,33},{2,34},{3,35},{4,36},{5,37},{6,38},{7,39},{8,40},{9,... | collective-permute-start | bytes 786440 | tf_op jit(solution)/shard_map/ppermute | solution.py:292
  27.0 8.2 %collective-permute-start.7 = (bf16[64,2048]{1,0:T(8,128)(2,1)S(1)}, bf16[64,2048]{1,0:T(8,128)(2,1)S(1)}, u32[]{:S(2)}, u32[]{:S(2)}) collective-permute-start(bf16[64,2048]{1,0:T(8,128)(2,1)S(1)} %get-tuple-element.40), channel_id=1, source_target_pairs={{0,33},{1,32},{2,35},{3,34},{4,37},{5,36},{6,39},{7,38},{8,41},{9,... | collective-permute-start | bytes 786440 | tf_op jit(solution)/shard_map/ppermute | solution.py:295
  32.3 6.2 %collective-permute-start.10 = (f32[16,2048]{1,0:T(8,128)S(1)}, f32[16,2048]{1,0:T(8,128)S(1)}, u32[]{:S(2)}, u32[]{:S(2)}) collective-permute-start(f32[16,2048]{1,0:T(8,128)S(1)} %get-tuple-element.58), channel_id=1, source_target_pairs={{0,64},{64,0},{1,65},{65,1},{2,66},{66,2},{3,67},{67,3},{4,68},{68... | collective-permute-start | bytes 393224 | tf_op jit(solution)/shard_map/ppermute | solution.py:298
  35.2 8.7 %collective-permute-start.8 = (bf16[64,2176]{1,0:T(8,128)(2,1)S(1)}, bf16[64,2176]{1,0:T(8,128)(2,1)S(1)}, u32[]{:S(2)}, u32[]{:S(2)}) collective-permute-start(bf16[64,2176]{1,0:T(8,128)(2,1)S(1)} %get-tuple-element.56), channel_id=1, source_target_pairs={{0,32},{1,33},{2,34},{3,35},{4,36},{5,37},{6,38},{7,39},{8,40},{9,... | collective-permute-start | bytes 835592 | tf_op jit(solution)/shard_map/ppermute | solution.py:292
  35.6 8.4 %collective-permute-start.9 = (bf16[64,2176]{1,0:T(8,128)(2,1)S(1)}, bf16[64,2176]{1,0:T(8,128)(2,1)S(1)}, u32[]{:S(2)}, u32[]{:S(2)}) collective-permute-start(bf16[64,2176]{1,0:T(8,128)(2,1)S(1)} %get-tuple-element.57), channel_id=1, source_target_pairs={{0,33},{1,32},{2,35},{3,34},{4,37},{5,36},{6,39},{7,38},{8,41},{9,... | collective-permute-start | bytes 835592 | tf_op jit(solution)/shard_map/ppermute | solution.py:295
  38.5 5.5 %collective-permute-start.11 = (bf16[16,2048]{1,0:T(8,128)(2,1)S(1)}, bf16[16,2048]{1,0:T(8,128)(2,1)S(1)}, u32[]{:S(2)}, u32[]{:S(2)}) collective-permute-start(bf16[16,2048]{1,0:T(8,128)(2,1)S(1)} %add_convert_fusion.sums_own), channel_id=1, source_target_pairs={{0,32},{32,0},{1,33},{33,1},{2,34},{34,2},{3,35},{35,3},{4,36},{36... | collective-permute-start | bytes 196616 | tf_op jit(solution)/shard_map/ppermute | solution.py:358
  45.5 29.3 %copy-start.1 = (bf16[2,64,2048]{2,1,0:T(8,128)(2,1)S(1)}, bf16[2,64,2048]{2,1,0:T(8,128)(2,1)}, u32[]{:S(2)}) copy-start(bf16[2,64,2048]{2,1,0:T(8,128)(2,1)} %param.8) | copy-start | bytes 1572868
  45.5 29.3 %copy-start.4 = (f32[2048,8]{0,1:T(8,128)S(1)}, f32[2048,8]{0,1:T(8,128)}, u32[]{:S(2)}) copy-start(f32[2048,8]{0,1:T(8,128)} %param.13) | copy-start | bytes 196612
  45.5 29.3 %all-to-all-start = ((bf16[32,8,2176]{2,1,0:T(8,128)(2,1)}), bf16[32,8,2176]{2,1,0:T(8,128)(2,1)S(1)}, u32[]{:S(2)}, u32[]{:S(2)}) async-start(bf16[32,8,2176]{2,1,0:T(8,128)(2,1)} %bitcast.12), calls=%async_computation | async-start | bytes 2228224 | tf_op jit(solution)/shard_map/all_to_all | solution.py:363
